TPU v7x, 128 devices: a whole 4x4x4 slice. The times are simulated.
128 devices in a mesh: row: 16 (over y, z_lo, core), col: 8 (over z_hi, x).
Axes of the slice: x: 4, y: 4, z: 4 (z_hi: 2, z_lo: 2; z = z_hi * 2 + z_lo), core: 2. Of those that a mesh axis runs over, the one named last changes fastest.
Arguments:
- single: float32 [1024, 768], P('row', 'col'), may hold values from -6 to 6
- pair: float32 [1024, 1024, 128], P('row', 'col'), may hold values from -6 to 6
- single_gain: float32 [768], replicated, may hold values from 0.25 to 1.75
- pair_gain: float32 [128], replicated, may hold values from 0.25 to 1.75
- w_query: float32 [768, 768], replicated, may hold values from -0.25 to 0.25
- w_key: float32 [768, 768], replicated, may hold values from -0.25 to 0.25
- w_value: float32 [768, 768], replicated, may hold values from -0.21875 to 0.21875
- w_gate: float32 [768, 768], replicated, may hold values from -0.21875 to 0.21875
- w_bias: float32 [128, 16], replicated, may hold values from -0.5 to 0.5
- w_out: float32 [768, 768], P(None, 'col'), may hold values from -0.21875 to 0.21875
- cotangent: float32 [1024, 768], P('row', 'col'), may hold values from -6 to 6
Outputs:
- attended: float32 [1024, 768], P('row', 'col')
- pair_grad: float32 [1024, 1024, 128], P('row', 'col')
- bias_grad: float32 [128, 16], replicated
All inputs are finite; a program needn't handle non-finite values.
Results may differ from a plain program's by a relative error of at most 0.0003.
Values sent between devices are 32-bit elements; how exact they have to be, the bound alone decides.
No kernel may reach another device: no remote copies, remote signals or barrier semaphores. Data moves between devices by JAX's collectives and lax.ppermute only.
A program may use at most 128 MiB of HBM per device.

v0:
```python
import jax
import jax.numpy as jnp
from jax import lax
from jax.sharding import PartitionSpec as P


def joined(array, axis, combine):
    everything = jax.tree.map(lambda part: lax.all_gather(part, axis), array)
    initial = jax.tree.map(lambda part: part[0], everything)

    def lap(k, so_far):
        return combine(so_far, jax.tree.map(lambda part: part[k], everything))

    return lax.fori_loop(1, lax.axis_size(axis), lap, initial)


def layer_norm(values_in, gain):
    centre = jnp.mean(values_in, axis=-1, keepdims=True)
    spread = jnp.mean((values_in - centre) ** 2, axis=-1, keepdims=True)
    return (values_in - centre) * lax.rsqrt(spread + 1e-05) * gain


def combine_parts(earlier, later):
    max_a, total_a, acc_a = earlier
    max_b, total_b, acc_b = later
    top_max = jnp.maximum(max_a, max_b)
    factor_a = jnp.exp(max_a - top_max)
    factor_b = jnp.exp(max_b - top_max)
    return (
        top_max,
        total_a * factor_a + total_b * factor_b,
        acc_a * factor_a[:, :, None] + acc_b * factor_b[:, :, None],
    )


def local(
    single, pair, single_gain, pair_gain, w_query, w_key, w_value, w_gate, w_bias, w_out, cotangent
):
    highest = lax.Precision.HIGHEST
    width_model = single_gain.shape[0]
    head_count = w_bias.shape[1]
    head_dim = width_model // head_count
    query_count = pair.shape[0]
    key_count = pair.shape[1]
    row_tokens = lax.all_gather(single, "col", axis=1, tiled=True)
    normed = layer_norm(row_tokens, single_gain)
    query = jnp.dot(normed, w_query, precision=highest).reshape(query_count, head_count, head_dim)
    gating = jax.nn.sigmoid(jnp.dot(normed, w_gate, precision=highest))
    col_index = lax.axis_index("col")
    kv_rows = jnp.concatenate(
        [jnp.dot(normed, w_key, precision=highest), jnp.dot(normed, w_value, precision=highest)],
        axis=1,
    )
    all_kv = lax.all_gather(kv_rows, "row", axis=0, tiled=True)
    key_source = lax.dynamic_slice_in_dim(all_kv, col_index * key_count, key_count, 0)
    keys = key_source[:, :width_model].reshape(key_count, head_count, head_dim)
    values = key_source[:, width_model:].reshape(key_count, head_count, head_dim)

    def bias_of(pair_tile, weight):
        return jnp.einsum(
            "ijc,ch->ihj", layer_norm(pair_tile, pair_gain), weight, precision=highest
        )

    bias, pull = jax.vjp(bias_of, pair, w_bias)
    scores = jnp.einsum("ihd,jhd->ihj", query, keys, precision=highest) * head_dim ** (-0.5) + bias
    local_max = jnp.max(scores, axis=-1)
    expo = jnp.exp(scores - local_max[:, :, None])
    local_total = jnp.sum(expo, axis=-1)
    local_acc = jnp.einsum("ihj,jhd->ihd", expo, values, precision=highest)
    top_max, top_total, top_acc = joined((local_max, local_total, local_acc), "col", combine_parts)
    context = top_acc / top_total[:, :, None]
    attended = jnp.dot(gating * context.reshape(query_count, width_model), w_out, precision=highest)
    back_sum = lax.psum(jnp.dot(cotangent, w_out.T, precision=highest), "col")
    d_context = (back_sum * gating).reshape(query_count, head_count, head_dim)
    row_delta = jnp.sum(d_context * context, axis=-1)
    soft_weights = jnp.exp(scores - top_max[:, :, None]) / top_total[:, :, None]
    d_probs = jnp.einsum("ihd,jhd->ihj", d_context, values, precision=highest)
    d_scores = soft_weights * (d_probs - row_delta[:, :, None])
    pair_grad, weight_part = pull(d_scores)
    bias_grad = lax.psum(weight_part, ("row", "col"))
    return (attended, pair_grad, bias_grad)


def solution(mesh):
    placed = (
        P("row", "col"),
        P("row", "col", None),
        P(),
        P(),
        P(),
        P(),
        P(),
        P(),
        P(),
        P(None, "col"),
        P("row", "col"),
    )
    return jax.shard_map(
        local,
        mesh=mesh,
        in_specs=placed,
        out_specs=(P("row", "col"), P("row", "col", None), P()),
        check_vma=False,
    )
```

profile of v0, /device:TPU:1, one launch (start us, length us, event | category | flops | bytes accessed | tf_op | source)
XLA Modules:
  0.0 344.4 jit_solution(17542768414670368472)
XLA Ops:
  8.1 30.5 %all-gather.3 = f32[8,96,64]{1,2,0:T(8,128)S(1)} all-gather(f32[1,96,64]{1,2,0:T(8,128)} %bitcast.98), channel_id=1, replica_groups=mesh['row'=16,'col'=8] {'col'}, dimensions={0}, use_global_device_ids=true | all-gather | bytes 221184 | tf_op jit(solution)/shard_map/all_gather | solution.py:45
  39.2 3.4 fusion.34
  42.6 1.6 fusion.33
  46.3 3.3 reduce_sum.91
  49.7 5.6 %copy.55 = f32[64,128,128]{1,2,0:T(8,128)} copy(f32[64,128,128]{2,1,0:T(8,128)} %param.14) | data formatting | bytes 8388608 | tf_op args[1]
  55.3 6.3 %fusion.35 = f32[64,768]{0,1:T(8,128)} fusion(f32[768,768]{1,0:T(8,128)} %param.17, f32[768,64]{0,1:T(8,128)S(1)} %reshape.83, f32[768]{0:T(1024)S(1)} %copy-done.11, f32[64]{0:T(128)S(1)} %add_rsqrt_fusion, f32[64]{0:T(128)S(1)} %broadcast_multiply_fusion.1), kind=kOutput, calls=%fused_computation.67 | convolution fusion | flops 453132288 | bytes 2756096 | tf_op jit(solution)/shard_map/reshape | solution.py:47
  61.6 3.0 multiply_reduce_fusion.1
  64.6 4.5 %fusion.4 = f32[64,128,16]{1,2,0:T(8,128)S(1)} fusion(f32[64,128,128]{1,2,0:T(8,128)} %copy.55, f32[128]{0:T(128)S(1)} %copy-done.15, f32[64,128]{1,0:T(8,128)S(1)} %fusion.29, f32[64,128]{1,0:T(8,128)S(1)} %broadcast_multiply_fusion, f32[128,16]{0,1:T(8,128)S(1)} %copy-done.13), kind=kOutput, calls=%fused_computation.15 | convolution fusion | flops 204472320 | bytes 4792832 | tf_op jit(solution)/shard_map/jvp(ijc,ch->ihj)/dot_general | solution.py:60
  69.2 27.6 %all-gather.9.cloned.1.call-done = f32[1024,1536]{1,0:T(8,128)} async-done(((f32[64,1536]{1,0:T(8,128)}), f32[1024,1536]{1,0:T(8,128)}) %all-gather.9.cloned.1.call-update) | async-done | bytes 6291472 | tf_op jit(solution)/shard_map/all_gather | solution.py:54
  96.7 2.1 fusion.37
  98.8 1.9 copy.58
  100.7 1.9 copy.53
  102.6 2.3 fusion.32
  105.8 2.8 convolution_bitcast_fusion
  108.6 2.0 copy.59
  110.7 23.2 %all-reduce.2.cloned.1.call-done = f32[64,768]{1,0:T(8,128)} async-done(((f32[64,768]{1,0:T(8,128)}), f32[64,768]{1,0:T(8,128)}) %all-reduce.2.cloned.1.call-update) | async-done | bytes 196624 | tf_op jit(solution)/shard_map/psum | solution.py:73
  133.8 3.2 fusion.38
  137.0 1.1 reshape.72
  138.1 1.5 fusion.25
  139.6 30.1 %all-gather.5 = f32[8,64,16]{1,2,0:T(8,128)} all-gather(f32[1,64,16]{1,2,0:T(8,128)S(1)} %bitcast.97), channel_id=3, replica_groups=mesh['row'=16,'col'=8] {'col'}, dimensions={0}, use_global_device_ids=true | all-gather | bytes 36864 | tf_op jit(solution)/shard_map/all_gather | solution.py:8
  169.7 30.1 %all-gather.4 = f32[8,64,16]{1,2,0:T(8,128)} all-gather(f32[1,64,16]{1,2,0:T(8,128)S(1)} %bitcast.95), channel_id=2, replica_groups=mesh['row'=16,'col'=8] {'col'}, dimensions={0}, use_global_device_ids=true | all-gather | bytes 36864 | tf_op jit(solution)/shard_map/all_gather | solution.py:8
  200.5 1.3 slice_bitcast_fusion.1
  201.8 10.0 %all-gather.11.cloned.1.call-done = f32[512,16,48]{2,1,0:T(8,128)} async-done(((f32[64,16,48]{2,1,0:T(8,128)}), f32[512,16,48]{2,1,0:T(8,128)}) %all-gather.11.cloned.1.call-update) | async-done | bytes 1572880 | tf_op jit(solution)/shard_map/all_gather | solution.py:8
  211.8 1.1 slice.27
  212.8 20.7 %while.19 = (s32[]{:T(128)}, f32[64,16]{0,1:T(8,128)}, f32[64,16]{0,1:T(8,128)S(1)}, f32[64,16,48]{2,1,0:T(8,128)S(1)}, f32[8,64,16]{1,2,0:T(8,128)}, /*index=5*...) while((s32[]{:T(128)}, f32[64,16]{0,1:T(8,128)}, ...), condition=%wide.region_7.0_spmd, body=%wide.region_6.0_spmd.sunk | while | flops 153605 | bytes 647311 | solution.py:14
  212.9 1.3 fusion.53
  214.4 1.4 fusion.54
  215.8 1.3 fusion.53
  217.3 1.4 fusion.54
  218.8 1.3 fusion.53
  220.3 1.4 fusion.54
  221.8 1.3 fusion.53
  223.3 1.4 fusion.54
  224.7 1.3 fusion.53
  226.2 1.4 fusion.54
  227.7 1.3 fusion.53
  229.2 1.4 fusion.54
  230.6 1.3 fusion.53
  232.1 1.4 fusion.54
  233.7 2.1 multiply_reduce_fusion.4
  235.8 2.4 fusion.13
  238.3 5.7 %fusion.17 = f32[128,16]{0,1:T(8,128)S(1)} fusion(f32[64,128,128]{1,2,0:T(8,128)} %copy.55, f32[128]{0:T(128)} %param.16, f32[64,128]{1,0:T(8,128)S(1)} %fusion.29, f32[64,128]{1,0:T(8,128)S(1)} %broadcast_multiply_fusion, f32[16,64,128]{2,1,0:T(8,128)S(1)} %fusion.13), kind=kOutput, calls=%fused_computation.32 | convolution fusion | flops 204472320 | bytes 4792832 | tf_op jit(solution)/shard_map/transpose(jvp(ijc,ch->ihj))/dot_general | solution.py:60
  244.0 5.9 %multiply_reduce_fusion.3 = (f32[64,128]{1,0:T(8,128)S(1)}, f32[64,128]{1,0:T(8,128)S(1)}, f32[64,128,128]{1,2,0:T(8,128)}) fusion(f32[128]{0:T(128)S(1)} %copy-done.16, f32[64,128]{1,0:T(8,128)S(1)} %fusion.29, f32[64,128,128]{1,2,0:T(8,128)S(1)} %copy-done.1, f32[64,128]{1,0:T(8,128)S(1)} %broadcast_multiply_fusion, f32[128,16]{0,1:T(8,128)S(1)} %copy-done.14, ...), kind=kOutput, calls=%fused_computation.13 | convolution fusion | flops 207601664 | bytes 9052672 | tf_op jit(solution)/shard_map/transpose(jvp(ijc,ch->ihj))/dot_general | solution.py:60
  249.9 70.9 %psum.15 = f32[128,16]{0,1:T(8,128)} all-reduce(f32[128,16]{0,1:T(8,128)S(1)} %fusion.17), channel_id=1, replica_groups=mesh['row'=16,'col'=8] {'row','col'}, use_global_device_ids=true, to_apply=%region_13.0 | all-reduce | flops 2048 | bytes 16384 | tf_op jit(solution)/shard_map/psum | solution.py:80
  321.1 3.4 multiply_reduce_fusion.2
  324.6 5.6 %add_add_fusion = f32[64,128,128]{1,2,0:T(8,128)} fusion(f32[64,128,128]{1,2,0:T(8,128)} %get-tuple-element.235, f32[64,128,128]{1,2,0:T(8,128)S(1)} %copy-done.2, f32[64,128]{1,0:T(8,128)S(1)} %add_multiply_fusion, f32[64,128]{1,0:T(8,128)S(1)} %multiply_multiply_fusion.6, f32[128]{0:T(128)S(1)} %copy-done.16, f32[64,128]{1,0:T(8,128)S(1)} %fusion.29, ...), kind=kLoop, calls=%fused_computation.8 | loop fusion | flops 6291456 | bytes 12714496 | tf_op jit(solution)/shard_map/transpose(jvp())/add_any | solution.py:18
  330.2 5.6 %copy.67 = f32[64,128,128]{2,1,0:T(8,128)} copy(f32[64,128,128]{1,2,0:T(8,128)} %add_add_fusion) | data formatting | bytes 8388608
  335.9 1.0 fusion.27
  (70 shorter events, 5.9 us)
Async XLA Ops:
  8.0 125.8 %copy-start = (f32[768,768]{1,0:T(8,128)S(1)}, f32[768,768]{1,0:T(8,128)}, u32[]{:S(2)}) copy-start(f32[768,768]{1,0:T(8,128)} %param.20) | copy-start | bytes 7077892
  8.0 34.6 %copy-start.11 = (f32[768]{0:T(1024)S(1)}, f32[768]{0:T(1024)}, u32[]{:S(2)}) copy-start(f32[768]{0:T(1024)} %param.15) | copy-start | bytes 9220
  8.0 88.7 %all-gather.9.cloned.1.call-start = ((), (), s32[]{:S(2)}) async-start(), calls=%async_computation | async-start | bytes 6684672 | tf_op jit(solution)/shard_map/all_gather | solution.py:54
  8.1 37.0 %copy-start.6 = (f32[768,96]{0,1:T(8,128)S(1)}, f32[768,96]{0,1:T(8,128)}, u32[]{:S(2)}) copy-start(f32[768,96]{0,1:T(8,128)} %param.22) | copy-start | bytes 884740
  8.1 37.0 %copy-start.12 = (f32[64,96]{1,0:T(8,128)S(1)}, f32[64,96]{1,0:T(8,128)}, u32[]{:S(2)}) copy-start(f32[64,96]{1,0:T(8,128)} %param.23) | copy-start | bytes 73732
  39.0 3.6 %copy-start.4 = (f32[768,768]{1,0:T(8,128)S(1)}, f32[768,768]{1,0:T(8,128)}, u32[]{:S(2)}) copy-start(f32[768,768]{1,0:T(8,128)} %param.19) | copy-start | bytes 7077892
  45.0 88.9 %all-reduce.2.cloned.1.call-start = ((), (), s32[]{:S(2)}) async-start(), calls=%async_computation.1 | async-start | bytes 393216 | tf_op jit(solution)/shard_map/psum | solution.py:73
  46.1 165.7 %all-gather.11.cloned.1.call-start = ((), (), s32[]{:S(2)}) async-start(), calls=%async_computation.2 | async-start | bytes 4718592 | tf_op jit(solution)/shard_map/all_gather | solution.py:8
  55.3 9.3 %copy-start.13 = (f32[128,16]{0,1:T(8,128)S(1)}, f32[128,16]{0,1:T(8,128)}, u32[]{:S(2)}) copy-start(f32[128,16]{0,1:T(8,128)} %param.21) | copy-start | bytes 24580
  55.3 9.4 %copy-start.15 = (f32[128]{0:T(128)S(1)}, f32[128]{0:T(128)}, u32[]{:S(2)}) copy-start(f32[128]{0:T(128)} %param.16) | copy-start | bytes 1540
  64.6 40.4 %copy-start.9 = (f32[64,128]{1,0:T(8,128)}, f32[64,128]{1,0:T(8,128)S(1)}, u32[]{:S(2)}) copy-start(f32[64,128]{1,0:T(8,128)S(1)} %multiply_reduce_fusion.1) | copy-start | bytes 98308
  105.0 0.8 copy-start.3
  235.7 8.2 %copy-start.14 = (f32[128,16]{0,1:T(8,128)S(1)}, f32[128,16]{0,1:T(8,128)}, u32[]{:S(2)}) copy-start(f32[128,16]{0,1:T(8,128)} %param.21) | copy-start | bytes 24580
  235.7 8.2 %copy-start.16 = (f32[128]{0:T(128)S(1)}, f32[128]{0:T(128)}, u32[]{:S(2)}) copy-start(f32[128]{0:T(128)} %param.16) | copy-start | bytes 1540
  235.8 8.2 %copy-start.1 = (f32[64,128,128]{1,2,0:T(8,128)S(1)}, f32[64,128,128]{1,2,0:T(8,128)}, u32[]{:S(2)}) copy-start(f32[64,128,128]{1,2,0:T(8,128)} %copy.55) | copy-start | bytes 12582916
  244.0 76.9 %copy-start.5 = (f32[64,16,48]{2,1,0:T(8,128)S(1)}, f32[64,16,48]{2,1,0:T(8,128)}, u32[]{:S(2)}) copy-start(f32[64,16,48]{2,1,0:T(8,128)} %get-tuple-element.228) | copy-start | bytes 589828
  244.0 77.1 %copy-start.10 = (f32[64,128]{1,0:T(8,128)S(1)}, f32[64,128]{1,0:T(8,128)}, u32[]{:S(2)}) copy-start(f32[64,128]{1,0:T(8,128)} %copy-done.9) | copy-start | bytes 98308
  321.1 3.5 %copy-start.2 = (f32[64,128,128]{1,2,0:T(8,128)S(1)}, f32[64,128,128]{1,2,0:T(8,128)}, u32[]{:S(2)}) copy-start(f32[64,128,128]{1,2,0:T(8,128)} %copy.55) | copy-start | bytes 12582916
  330.2 5.7 %copy-start.7 = (f32[768,96]{0,1:T(8,128)S(1)}, f32[768,96]{0,1:T(8,128)}, u32[]{:S(2)}) copy-start(f32[768,96]{0,1:T(8,128)} %param.22) | copy-start | bytes 884740
  330.2 5.7 %copy-start.8 = (f32[64,768]{1,0:T(8,128)S(1)}, f32[64,768]{1,0:T(8,128)}, u32[]{:S(2)}) copy-start(f32[64,768]{1,0:T(8,128)} %get-tuple-element.232) | copy-start | bytes 589828
Sparse Core Ops, SparseCore 0:
  45.1 51.6 all-gather.8
Sparse Core Ops, SparseCore 1:
  47.9 85.9 all-reduce.1
  136.3 75.4 all-gather.10
where the time goes:
time: 346 us; the launch traced here: 344 us
  blocking collectives  162 us (47%)
  waiting for transfers between devices  60.8 us (18%)
  matrix products  40.2 us (12%)
  other arithmetic  39.5 us (11%)
  local copies, waits for them, and re-layouts  26 us (8%)
  between operations  15.8 us (5%)
    psum x1, blocking collectives, local(): bias_grad = lax.psum(weight_part, ('row', 'col'))  70.9 us
    all_gather x2, blocking collectives, joined(): everything = jax.tree.map(lambda part: lax.all_gather(part, axis), array)  60.2 us
    all_gather x1, blocking collectives, local(): row_tokens = lax.all_gather(single, 'col', axis=1, tiled=True)  30.5 us
    all_gather x1, waiting for transfers between devices, local(): all_kv = lax.all_gather(kv_rows, 'row', axis=0, tiled=True)  27.6 us
    psum x1, waiting for transfers between devices, local(): back_sum = lax.psum(jnp.dot(cotangent, w_out.T, precision=highest), 'col')  23.2 us
    dot_general x3, matrix products, bias_of(): jnp.einsum('ijc,ch->ihj', layer_norm(pair_tile, pair_gain), weight, preci...  16.1 us
    unnamed x37, local copies, waits for them, and re-layouts  12.2 us
    add x7, other arithmetic, combine_parts(): acc_a * factor_a[:, :, None] + acc_b * factor_b[:, :, None]  10.1 us
  transfers between devices with their start and end apart: 3, of which 3 were waited for; matrix products, arithmetic and copies ran while one was open for 13% of the time, Pallas kernels for 0%

commit v1 on v0

v1 whole, which is shorter than its diff:
```python
import functools

import jax
import jax.numpy as jnp
from jax import lax
from jax.experimental import pallas as pl
from jax.experimental.pallas import tpu as pltpu
from jax.sharding import PartitionSpec as P

F32 = jnp.float32
BF16 = jnp.bfloat16
EPS = 1e-05
NN = (((1,), (0,)), ((), ()))
NT = (((1,), (1,)), ((), ()))
TN = (((0,), (0,)), ((), ()))
VMEM_LIMIT = 48 * 1024 * 1024


def split(x):
    high = x.astype(BF16)
    return high, (x - high.astype(F32)).astype(BF16)


def dg(a, b, dims):
    return lax.dot_general(a, b, dims, preferred_element_type=F32)


def dot3(a, b, dims):
    ah, al = split(a)
    bh, bl = split(b)
    return dg(ah, bh, dims) + dg(al, bh, dims) + dg(ah, bl, dims)


def call(kernel, out_shape, flops, args, grid=None, in_specs=None, out_specs=None, scratch=()):
    nbytes = sum(a.size * a.dtype.itemsize for a in args)
    for o in jax.tree.leaves(out_shape):
        nbytes += o.size * jnp.dtype(o.dtype).itemsize
    kw = {}
    if grid is not None:
        kw = dict(grid=grid, in_specs=in_specs, out_specs=out_specs)
    return pl.pallas_call(
        kernel,
        out_shape=out_shape,
        scratch_shapes=list(scratch),
        compiler_params=pltpu.CompilerParams(vmem_limit_bytes=VMEM_LIMIT),
        cost_estimate=pl.CostEstimate(flops=flops, bytes_accessed=nbytes, transcendentals=0),
        **kw,
    )(*args)


def sds(*shape, dtype=F32):
    return jax.ShapeDtypeStruct(shape, dtype)


def head_mask(heads, width):
    lane = lax.broadcasted_iota(jnp.int32, (heads, width), 1)
    row = lax.broadcasted_iota(jnp.int32, (heads, width), 0)
    size = width // heads
    return (lane >= row * size) & (lane < (row + 1) * size)


def eye_mask(n):
    return lax.broadcasted_iota(jnp.int32, (n, n), 0) == lax.broadcasted_iota(jnp.int32, (n, n), 1)


def first_kernel(single_ref, cot_ref, wout_ref, out_ref):
    n, _, block = out_ref.shape
    rows = single_ref.shape[0]
    single = single_ref[...]
    cot = cot_ref[...]
    for k in range(n):
        out_ref[k, :rows] = single
        out_ref[k, rows:] = dot3(cot, wout_ref[k * block : (k + 1) * block, :], NT)


def back_kernel(recv_ref, out_ref):
    n, rows, _ = out_ref.shape
    total = recv_ref[0, rows:]
    for k in range(1, n):
        total = total + recv_ref[k, rows:]
    for k in range(n):
        out_ref[k] = total


def joined_norm(blocks, gain_ref, out_ref, row):
    rows, block = blocks[0].shape
    width = block * len(blocks)
    centre = sum(jnp.sum(b, axis=-1, keepdims=True) for b in blocks) / width
    blocks = [b - centre for b in blocks]
    spread = sum(jnp.sum(b * b, axis=-1, keepdims=True) for b in blocks) / width
    scale = lax.rsqrt(spread + EPS)
    for k, b in enumerate(blocks):
        part = slice(k * block, (k + 1) * block)
        out_ref[row : row + rows, part] = b * scale * gain_ref[:, part]


def query_kernel(recv_ref, gain_ref, wq_ref, wg_ref, query_ref, gate_ref, normed):
    n = recv_ref.shape[0]
    rows = query_ref.shape[0]
    joined_norm([recv_ref[k, :rows] for k in range(n)], gain_ref, normed, 0)
    query_ref[...] = dot3(normed[...], wq_ref[...], NN) * (48 ** -0.5)
    logits = dot3(normed[...], wg_ref[...], NN)
    gate_ref[...] = 1.0 / (1.0 + jnp.exp(-logits))


def pair_kernel(pair_ref, wt_ref, high_ref, low_ref, bias_ref, rs_ref):
    steps, keys, chans = pair_ref.shape
    heads = bias_ref.shape[1]
    wh, wl = split(wt_ref[...])
    both = jnp.concatenate([wh, wl], axis=0)
    ones = jnp.ones((8, chans), BF16)
    for i in range(steps):
        x = pair_ref[i]
        d = x - jnp.sum(x, axis=-1, keepdims=True) * (1.0 / chans)
        dh, dl = split(d)
        high_ref[i] = dh
        low_ref[i] = dl
        sh, sl = split(d * d)
        spread = (dg(ones, sh, NT) + dg(ones, sl, NT)) * (1.0 / chans)
        rs = lax.rsqrt(spread + EPS)
        two = dg(both, dh, NT)
        raw = two[:heads] + two[heads:] + dg(wh, dl, NT)
        bias_ref[i] = raw * rs[0:1]
        rs_ref[i : i + 1, :] = rs[0:1]


def attend_kernel(
    recv_ref, back_ref, gain_ref, wk_ref, wv_ref, query_ref, gate_ref, bias_ref,
    pay_ref, expo_ref, dprobs_ref, max_ref,
    normed, dctx, acc,
):
    n_row, rows, block = recv_ref.shape
    n_col = back_ref.shape[0]
    queries, heads, keys = bias_ref.shape
    width = normed.shape[1]
    per = n_row // n_col
    for t in range(per):
        joined_norm(
            [recv_ref[t * n_col + k] for k in range(n_col)], gain_ref, normed, t * rows
        )
    kh, kl = split(dot3(normed[...], wk_ref[...], NN))
    vh, vl = split(dot3(normed[...], wv_ref[...], NN))
    for k in range(n_col):
        part = slice(k * block, (k + 1) * block)
        dctx[:, part] = back_ref[k] * gate_ref[:, part]
    mask = head_mask(heads, width)[None]
    eye = eye_mask(heads)[None]
    chunk = 16
    size = chunk * heads

    def step(s, carry):
        here = pl.ds(pl.multiple_of(s * chunk, chunk), chunk)

        def spread(rows_):
            wide = jnp.where(mask, rows_[:, None, :], 0.0)
            h, l = split(wide)
            return h.reshape(size, width), l.reshape(size, width)

        qh, ql = spread(query_ref[here])
        scores = dg(qh, kh, NT) + dg(ql, kh, NT) + dg(qh, kl, NT)
        scores = scores + bias_ref[here].reshape(size, keys)
        gh, gl = spread(dctx[here])
        dp = dg(gh, vh, NT) + dg(gl, vh, NT) + dg(gh, vl, NT)
        top = jnp.max(scores, axis=-1, keepdims=True)
        expo = jnp.exp(scores - top)
        total = jnp.sum(expo, axis=-1, keepdims=True)
        inv = 1.0 / total
        delta = jnp.sum(expo * dp, axis=-1, keepdims=True) * inv
        expo_ref[here] = expo.reshape(chunk, heads, keys)
        dprobs_ref[here] = dp.reshape(chunk, heads, keys)
        eh, el = split(expo * inv)
        wide = dg(eh, vh, NN) + dg(el, vh, NN) + dg(eh, vl, NN)
        acc[here] = jnp.sum(jnp.where(mask, wide.reshape(chunk, heads, width), 0.0), axis=1)

        def lanes(col):
            return jnp.sum(jnp.where(eye, col.reshape(chunk, heads, 1), 0.0), axis=1)

        lse = lanes(top + jnp.log(total))
        dlt = lanes(delta)
        max_ref[here] = lanes(top)
        for k in range(n_col):
            pay_ref[k, here, block : block + heads] = lse
            pay_ref[k, here, block + heads : block + 2 * heads] = dlt
        return carry

    lax.fori_loop(0, queries // chunk, step, 0)
    for k in range(n_col):
        pay_ref[k, :, :block] = acc[:, k * block : (k + 1) * block]


def moment_kernel(high_ref, low_ref, expo_ref, dprobs_ref, rs_ref, out_ref):
    steps, heads, keys = expo_ref.shape
    for i in range(steps):
        e = expo_ref[i] * rs_ref[i : i + 1, :]
        both = jnp.concatenate([e * dprobs_ref[i], e], axis=0)
        bh, bl = split(both)
        dh = high_ref[i]
        first = dg(jnp.concatenate([bh, bl], axis=0), dh, NN)
        out_ref[i] = first[: 2 * heads] + first[2 * heads :] + dg(bh, low_ref[i], NN)


def join_kernel(recv_ref, max_ref, moment_ref, pgain_ref, sel_ref, pay_ref, fac_ref, dlt_ref):
    n, rows, _ = recv_ref.shape
    heads = max_ref.shape[1]
    block = sel_ref.shape[1]
    lse = [recv_ref[k, :, block : block + heads] for k in range(n)]
    top = functools.reduce(jnp.maximum, lse)
    weight = [jnp.exp(v - top) for v in lse]
    total = sum(weight)
    inv = 1.0 / total
    weight = [w * inv for w in weight]
    delta = sum(w * recv_ref[k, :, block + heads :] for k, w in enumerate(weight))
    fac = jnp.exp(max_ref[...] - (top + jnp.log(total)))
    fac_ref[...] = fac
    dlt_ref[...] = delta
    sel = sel_ref[...]
    context = sum(
        lax.dot_general(w, sel, NN, precision=lax.Precision.HIGHEST, preferred_element_type=F32)
        * recv_ref[k, :, :block]
        for k, w in enumerate(weight)
    )
    eye = eye_mask(heads)[None]

    def column(v):
        return jnp.sum(jnp.where(eye, v[:, None, :], 0.0), axis=-1, keepdims=True)

    part = jnp.sum(
        column(fac) * moment_ref[:, :heads] - column(fac * delta) * moment_ref[:, heads:], axis=0
    ) * pgain_ref[...]
    for k in range(n):
        pay_ref[k, :rows, :block] = context
        pay_ref[k, rows:, :] = part


def grad_kernel(high_ref, low_ref, expo_ref, dprobs_ref, bias_ref, rs_ref, fac_ref, dlt_ref, w_ref, out_ref):
    steps, heads, keys = expo_ref.shape
    chans = out_ref.shape[2]
    eye = eye_mask(heads)
    wh, wl = split(w_ref[...])
    weights = jnp.concatenate([wh, wh, wl], axis=0)
    for i in range(steps):
        fac = jnp.sum(jnp.where(eye, fac_ref[i : i + 1, :], 0.0), axis=-1, keepdims=True)
        dlt = jnp.sum(jnp.where(eye, dlt_ref[i : i + 1, :], 0.0), axis=-1, keepdims=True)
        rs = rs_ref[i : i + 1, :]
        u = expo_ref[i] * fac * (dprobs_ref[i] - dlt) * rs
        both = jnp.concatenate([u, u * bias_ref[i] * rs], axis=0)
        bh, bl = split(both)
        wide = dg(jnp.concatenate([bh, bl, bh], axis=0), weights, TN)
        d = high_ref[i].astype(F32) + low_ref[i].astype(F32)
        out_ref[i] = wide[:, :chans] - d * wide[:, chans:]


def out_kernel(recv_ref, gate_ref, wout_ref, att_ref, pay_ref, gated):
    n, _, _ = recv_ref.shape
    rows, block = att_ref.shape
    for k in range(n):
        part = slice(k * block, (k + 1) * block)
        gated[:, part] = recv_ref[k, :rows, :block] * gate_ref[:, part]
    att_ref[...] = dot3(gated[...], wout_ref[...], NN)
    total = recv_ref[0, rows:, :]
    for k in range(1, n):
        total = total + recv_ref[k, rows:, :]
    for k in range(pay_ref.shape[0]):
        pay_ref[k] = total


def last_kernel(recv_ref, out_ref):
    total = recv_ref[0]
    for k in range(1, recv_ref.shape[0]):
        total = total + recv_ref[k]
    out_ref[...] = total.T


def swap(x, axis):
    return lax.all_to_all(x, axis, 0, 0, tiled=True)


def local(
    single, pair, single_gain, pair_gain, w_query, w_key, w_value, w_gate, w_bias, w_out, cotangent
):
    n_row, n_col = lax.axis_size("row"), lax.axis_size("col")
    queries, keys, chans = pair.shape
    heads = w_bias.shape[1]
    width = single_gain.shape[0]
    block = single.shape[1]
    per = n_row // n_col
    gain = single_gain[None]
    pgain = pair_gain[None]

    pay = call(first_kernel, sds(n_col, 2 * queries, block), 2 * queries * width * block * 3, (single, cotangent, w_out))
    perm = [
        (r * n_col + c, ((r % per) * n_col + c) * n_col + r // per)
        for r in range(n_row)
        for c in range(n_col)
    ]
    moved = lax.ppermute(single, ("row", "col"), perm)
    recv1 = swap(pay, "col")
    recv2 = swap(jnp.broadcast_to(moved[None], (n_row,) + moved.shape), "row")

    wt = (pair_gain[:, None] * w_bias).T
    ib = 8
    grid = (queries // ib,)

    def cut(*shape):
        zeros = (0,) * (len(shape))
        return pl.BlockSpec((ib,) + shape, lambda i: (i,) + zeros)

    def whole(a):
        zeros = (0,) * a.ndim
        return pl.BlockSpec(a.shape, lambda i: zeros)

    high, low, bias, rs = call(
        pair_kernel,
        (
            sds(queries, keys, chans, dtype=BF16),
            sds(queries, keys, chans, dtype=BF16),
            sds(queries, heads, keys),
            sds(queries, keys),
        ),
        queries * keys * chans * 400,
        (pair, wt),
        grid,
        [cut(keys, chans), whole(wt)],
        (cut(keys, chans), cut(keys, chans), cut(heads, keys), cut(keys)),
    )
    back_pay = call(back_kernel, sds(n_col, queries, block), queries * width, (recv1,))
    back = swap(back_pay, "col")
    query, gate = call(
        query_kernel,
        (sds(queries, width), sds(queries, width)),
        queries * width * width * 12,
        (recv1, gain, w_query, w_gate),
        scratch=[pltpu.VMEM((queries, width), F32)],
    )
    pay4, expo, dprobs, top = call(
        attend_kernel,
        (
            sds(n_col, queries, block + 2 * heads),
            sds(queries, heads, keys),
            sds(queries, heads, keys),
            sds(queries, heads),
        ),
        keys * width * width * 12,
        (recv2, back, gain, w_key, w_value, query, gate, bias),
        scratch=[
            pltpu.VMEM((keys, width), F32),
            pltpu.VMEM((queries, width), F32),
            pltpu.VMEM((queries, width), F32),
        ],
    )
    recv4 = swap(pay4, "col")
    moment = call(
        moment_kernel,
        sds(queries, 2 * heads, chans),
        queries * keys * chans * heads * 12,
        (high, low, expo, dprobs, rs),
        grid,
        [cut(keys, chans), cut(keys, chans), cut(heads, keys), cut(heads, keys), cut(keys)],
        cut(2 * heads, chans),
    )
    lane = lax.broadcasted_iota(jnp.int32, (heads, block), 1)
    row = lax.broadcasted_iota(jnp.int32, (heads, block), 0)
    size = width // heads
    sel = (row == lax.axis_index("col") * (block // size) + lane // size).astype(F32)
    pay5, fac, dlt = call(
        join_kernel,
        (sds(n_col, queries + heads, chans), sds(queries, heads), sds(queries, heads)),
        queries * heads * chans * 8,
        (recv4, top, moment, pgain, sel),
    )
    recv5 = swap(pay5, "col")
    centred = wt - jnp.mean(wt, axis=1, keepdims=True)
    zero = jnp.zeros_like(centred)
    weights = jnp.concatenate(
        [
            jnp.concatenate([centred, zero], axis=1),
            jnp.concatenate([zero, jnp.full_like(centred, 1.0 / chans)], axis=1),
        ],
        axis=0,
    )
    pair_grad = call(
        grad_kernel,
        sds(queries, keys, chans),
        queries * keys * chans * 400,
        (high, low, expo, dprobs, bias, rs, fac, dlt, weights),
        grid,
        [
            cut(keys, chans), cut(keys, chans), cut(heads, keys), cut(heads, keys), cut(heads, keys),
            cut(keys), cut(heads), cut(heads), whole(weights),
        ],
        cut(keys, chans),
    )
    attended, pay6 = call(
        out_kernel,
        (sds(queries, block), sds(n_row, heads, chans)),
        queries * width * block * 6,
        (recv5, gate, w_out),
        scratch=[pltpu.VMEM((queries, width), F32)],
    )
    recv6 = swap(pay6, "row")
    bias_grad = call(last_kernel, sds(chans, heads), chans * heads, (recv6,))
    return attended, pair_grad, bias_grad


def solution(mesh):
    placed = (
        P("row", "col"),
        P("row", "col", None),
        P(),
        P(),
        P(),
        P(),
        P(),
        P(),
        P(),
        P(None, "col"),
        P("row", "col"),
    )
    return jax.shard_map(
        local,
        mesh=mesh,
        in_specs=placed,
        out_specs=(P("row", "col"), P("row", "col", None), P()),
        check_vma=False,
    )
```

time: 346 us -> 138 us (0.40)
  blocking collectives: 162 us -> 14.5 us
  waiting for transfers between devices: 60.8 us -> 11.9 us
  starting transfers between devices: 0.31 us -> 40.8 us
  matrix products: 40.2 us -> 0 us
  other arithmetic: 39.5 us -> 3.31 us
  Pallas kernels: 0 us -> 33.6 us
  between operations: 15.8 us -> 0.82 us
  local copies, waits for them, and re-layouts: 26 us -> 30.8 us
    all_gather x3 -> x0, blocking collectives: 90.7 us -> none  [the longest x2 60.2 us: joined(): everything = jax.tree.map(lambda part: lax.all_gather(part, axis), array)]
    psum x1 -> x0, blocking collectives: 70.9 us -> none  [local(): bias_grad = lax.psum(weight_part, ('row', 'col'))]
    all_gather x2 -> x0, waiting for transfers between devices: 37.5 us -> none  [the longest x1 27.6 us: local(): all_kv = lax.all_gather(kv_rows, 'row', axis=0, tiled=True)]
    all_to_all x0 -> x5, starting transfers between devices: none -> 35.1 us  [swap(): return lax.all_to_all(x, axis, 0, 0, tiled=True)]
    dot_general x11 -> x0, matrix products: 33.9 us -> none  [the longest x3 16.1 us: bias_of(): jnp.einsum('ijc,ch->ihj', layer_norm(pair_tile, pair_gain), weight, preci...]
    pallas_call x0 -> x10, Pallas kernels: none -> 33.6 us  [call(): pl.pallas_call(kernel, out_shape=out_shape, scratch_shapes=list(scratch),...]
    psum x1 -> x0, waiting for transfers between devices: 23.2 us -> none  [local(): back_sum = lax.psum(jnp.dot(cotangent, w_out.T, precision=highest), 'col')]
    add x14 -> x0, other arithmetic: 19.4 us -> none  [the longest x7 10.1 us: combine_parts(): acc_a * factor_a[:, :, None] + acc_b * factor_b[:, :, None]]
  transfers between devices with their start and end apart: 3 -> 6, of which waited for: 3 -> 3; matrix products, arithmetic and copies ran while one was open for 13% -> 3% of each run, Pallas kernels for 0% -> 16%
where the time goes in v1:
time: 138 us; the launch traced here: 136 us
  starting transfers between devices  40.8 us (30%)
  Pallas kernels  33.6 us (24%)
  local copies, waits for them, and re-layouts  30.8 us (22%)
  blocking collectives  14.5 us (11%)
  waiting for transfers between devices  11.9 us (9%)
  other arithmetic  3.31 us (2%)
    all_to_all x5, starting transfers between devices, swap(): return lax.all_to_all(x, axis, 0, 0, tiled=True)  35.1 us
    pallas_call x10, Pallas kernels, call(): pl.pallas_call(kernel, out_shape=out_shape, scratch_shapes=list(scratch),...  33.6 us
    unnamed x74, local copies, waits for them, and re-layouts  28.8 us
    all_to_all x1, blocking collectives, swap(): return lax.all_to_all(x, axis, 0, 0, tiled=True)  14.5 us
    all_to_all x5, waiting for transfers between devices, swap(): return lax.all_to_all(x, axis, 0, 0, tiled=True)  10 us
    ppermute x1, starting transfers between devices, local(): moved = lax.ppermute(single, ('row', 'col'), perm)  5.65 us
  transfers between devices with their start and end apart: 6, of which 3 were waited for; matrix products, arithmetic and copies ran while one was open for 3% of the time, Pallas kernels for 16%

profile of v1, /device:TPU:1, one launch (start us, length us, event | category | flops | bytes accessed | tf_op | source)
XLA Modules:
  0.0 135.7 jit_solution(636200045788721043)
XLA Ops:
  0.7 1.1 copy.17.wout_ref
  1.8 0.8 copy-done.28
  2.6 0.8 copy-done.29
  3.8 1.0 copy.18
  4.8 8.2 %all-to-all-start.1 = ((f32[8,128,96]{1,2,0:T(8,128)}), f32[8,128,96]{1,2,0:T(8,128)S(1)}, u32[]{:S(2)}, u32[]{:S(2)}) async-start(f32[8,128,96]{1,2,0:T(8,128)} %copy.18), calls=%async_computation.1 | async-start | bytes 786432 | tf_op jit(solution)/shard_map/all_to_all | solution.py:275
  12.9 5.7 %collective-permute-start = (f32[64,96]{1,0:T(8,128)S(1)}, f32[64,96]{1,0:T(8,128)S(1)}, u32[]{:S(2)}, u32[]{:S(2)}) collective-permute-start(f32[64,96]{1,0:T(8,128)S(1)} %copy-done.29), channel_id=1, source_target_pairs={{0,0},{1,8},{2,16},{3,24},{4,32},{5,40},{6,48},{7,56},{8,64},{9,72... | collective-permute-start | bytes 73736 | tf_op jit(solution)/shard_map/ppermute | solution.py:296
  18.7 1.9 %collective-permute-done = f32[64,96]{1,0:T(8,128)S(1)} collective-permute-done((f32[64,96]{1,0:T(8,128)S(1)}, f32[64,96]{1,0:T(8,128)S(1)}, u32[]{:S(2)}, u32[]{:S(2)}) %collective-permute-start) | collective-permute-done | bytes 24608 | tf_op jit(solution)/shard_map/ppermute | solution.py:296
  20.6 2.6 %all-to-all-done.1 = f32[8,128,96]{1,2,0:T(8,128)S(1)} async-done(((f32[8,128,96]{1,2,0:T(8,128)}), f32[8,128,96]{1,2,0:T(8,128)S(1)}, u32[]{:S(2)}, u32[]{:S(2)}) %all-to-all-start.1) | async-done | bytes 393248 | tf_op jit(solution)/shard_map/all_to_all | solution.py:275
  23.2 0.8 broadcast_in_dim.6
  24.1 6.0 %all-to-all-start = ((f32[16,64,96]{2,1,0:T(8,128)}), f32[16,64,96]{2,1,0:T(8,128)S(1)}, u32[]{:S(2)}, u32[]{:S(2)}) async-start(f32[16,64,96]{2,1,0:T(8,128)} %broadcast_in_dim.6), calls=%async_computation | async-start | bytes 1048576 | tf_op jit(solution)/shard_map/all_to_all | solution.py:275
  30.0 0.7 broadcast_subtract_fusion
  31.5 0.7 shard_map.131
  32.3 7.4 %all-to-all-done.recv_ref = f32[16,64,96]{2,1,0:T(8,128)S(1)} async-done(((f32[16,64,96]{2,1,0:T(8,128)}), f32[16,64,96]{2,1,0:T(8,128)S(1)}, u32[]{:S(2)}, u32[]{:S(2)}) %all-to-all-start) | async-done | bytes 393248 | tf_op jit(solution)/shard_map/all_to_all | solution.py:275
  39.7 7.2 %all-to-all-start.2 = ((f32[8,64,96]{2,1,0:T(8,128)}), f32[8,64,96]{2,1,0:T(8,128)}, u32[]{:S(2)}, u32[]{:S(2)}) async-start(f32[8,64,96]{2,1,0:T(8,128)} %shard_map.131), calls=%async_computation.2 | async-start | bytes 524288 | tf_op jit(solution)/shard_map/all_to_all | solution.py:275
  46.8 8.0 %shard_map.133 = (bf16[64,128,128]{2,1,0:T(8,128)(2,1)S(1)}, bf16[64,128,128]{2,1,0:T(8,128)(2,1)S(1)}, f32[64,16,128]{2,1,0:T(8,128)S(1)}, f32[64,128]{1,0:T(8,128)S(1)}) custom-call(f32[64,128,128]{2,1,0:T(8,128)} %pair_ref.1, f32[16,128]{1,0:T(8,128)S(1)} %get-tuple-element.40.wt_ref), custom_call_target="tpu_custom_call" | custom-call | flops 419430400 | bytes 8953856 | tf_op jit(solution)/shard_map/pallas_call | solution.py:41
  54.9 1.3 copy-done
  57.4 1.7 %copy-done.2 = f32[768,768]{1,0:T(8,128)S(1)} copy-done((f32[768,768]{1,0:T(8,128)S(1)}, f32[768,768]{1,0:T(8,128)}, u32[]{:S(2)}) %copy-start.2) | copy-done | bytes 2359320
  59.1 1.7 %copy-done.3 = f32[768,768]{1,0:T(8,128)S(1)} copy-done((f32[768,768]{1,0:T(8,128)S(1)}, f32[768,768]{1,0:T(8,128)}, u32[]{:S(2)}) %copy-start.3) | copy-done | bytes 2359320
  60.7 1.8 %shard_map.132 = (f32[64,768]{1,0:T(8,128)S(1)}, f32[64,768]{1,0:T(8,128)S(1)}) custom-call(f32[8,128,96]{2,1,0:T(8,128)S(1)} %copy.19.recv_ref, f32[1,768]{1,0:T(1,128)S(1)} %broadcast_in_dim.7.gain_ref, f32[768,768]{1,0:T(8,128)S(1)} %copy-done.2, f32[768,768]{1,0:T(8,128)S(1)} %copy-done.3), custom_call_target="tpu_custom_call" | custom-call | flops 452984832 | bytes 5508096 | tf_op jit(solution)/shard_map/pallas_call | solution.py:41
  62.6 0.7 copy-done.15
  63.2 0.7 copy-done.19
  63.9 1.7 %copy-done.4 = f32[768,768]{1,0:T(8,128)S(1)} copy-done((f32[768,768]{1,0:T(8,128)S(1)}, f32[768,768]{1,0:T(8,128)}, u32[]{:S(2)}) %copy-start.4) | copy-done | bytes 2359320
  65.6 1.0 copy-done.14
  66.6 0.9 copy-done.16
  67.6 0.9 copy-done.20
  68.5 9.2 %shard_map.134 = (f32[8,64,128]{2,1,0:T(8,128)S(1)}, f32[64,16,128]{2,1,0:T(8,128)S(1)}, f32[64,16,128]{2,1,0:T(8,128)S(1)}, f32[64,16]{1,0:T(8,128)S(1)}) custom-call(f32[16,64,96]{2,1,0:T(8,128)S(1)} %copy-done.14, f32[8,64,96]{2,1,0:T(8,128)} %all-to-all-done.2.back_ref, f32[1,768]{1,0:T(1,128)S(1)} %broadcast_in_dim.7.gain_ref, ...), custom_call_target="tpu_custom_call" | custom-call | flops 905969664 | bytes 7543808 | tf_op jit(solution)/shard_map/pallas_call | solution.py:41
  77.7 0.8 copy-done.7
  78.5 0.7 copy-done.18
  79.8 6.6 %all-to-all-start.3 = ((f32[8,64,128]{2,1,0:T(8,128)}), f32[8,64,128]{2,1,0:T(8,128)}, u32[]{:S(2)}, u32[]{:S(2)}) async-start(f32[8,64,128]{2,1,0:T(8,128)} %copy-done.18), calls=%async_computation.3 | async-start | bytes 524288 | tf_op jit(solution)/shard_map/all_to_all | solution.py:275
  87.1 1.0 copy-done.8
  88.1 1.0 copy-done.11
  89.2 0.8 copy-done.22
  89.9 5.2 %shard_map.135.moment_ref = f32[64,32,128]{2,1,0:T(8,128)S(1)} custom-call(bf16[64,128,128]{2,1,0:T(8,128)(2,1)S(1)} %get-tuple-element.23.high_ref, bf16[64,128,128]{2,1,0:T(8,128)(2,1)} %copy-done, f32[64,16,128]{2,1,0:T(8,128)S(1)} %copy-done.8, f32[64,16,128]{2,1,0:T(8,128)S(1)} %copy-done.11, f32[64,128]{1,0:T(8,128)S(1)} %copy-done.22), custom_call_target="tpu_custom_call" | custom-call | flops 201326592 | bytes 6324224 | tf_op jit(solution)/shard_map/pallas_call | solution.py:41
  95.1 0.8 copy-done.31
  95.8 1.5 %shard_map.136 = (f32[8,80,128]{2,1,0:T(8,128)S(1)}, f32[64,16]{1,0:T(8,128)S(1)}, f32[64,16]{1,0:T(8,128)S(1)}) custom-call(f32[8,64,128]{2,1,0:T(8,128)} %all-to-all-done.3.recv_ref, f32[64,16]{1,0:T(8,128)S(1)} %copy-done.31, f32[64,32,128]{2,1,0:T(8,128)S(1)} %shard_map.135.moment_ref, f32[1,128]{1,0:T(1,128)S(1)} %bitcast.4, f32[16,96]{1,0:T(8,128)S(1)} %fusion.sel_ref), custom_call_target="tpu_custom_call" | custom-call | flops 1048576 | bytes 1657344 | tf_op jit(solution)/shard_map/pallas_call | solution.py:41
  98.0 14.5 %all_to_all.30.recv_ref = f32[8,80,128]{2,1,0:T(8,128)S(1)} all-to-all(f32[8,80,128]{2,1,0:T(8,128)S(1)} %get-tuple-element.28), channel_id=1, replica_groups=mesh['row'=16,'col'=8] {'col'}, dimensions={0} | all-to-all | bytes 655360 | tf_op jit(solution)/shard_map/all_to_all | solution.py:275
  112.5 0.9 copy-done.17
  113.4 1.0 shard_map.137
  114.5 7.2 %all-to-all-start.5 = ((f32[16,16,128]{2,1,0:T(8,128)}), f32[16,16,128]{2,1,0:T(8,128)S(1)}, u32[]{:S(2)}, u32[]{:S(2)}) async-start(f32[16,16,128]{2,1,0:T(8,128)} %get-tuple-element.32), calls=%async_computation.5 | async-start | bytes 262144 | tf_op jit(solution)/shard_map/all_to_all | solution.py:275
  121.7 0.7 select_maximum_fusion.w_ref
  122.4 1.6 %copy-done.1 = bf16[64,128,128]{2,1,0:T(8,128)(2,1)S(1)} copy-done((bf16[64,128,128]{2,1,0:T(8,128)(2,1)S(1)}, bf16[64,128,128]{2,1,0:T(8,128)(2,1)}, u32[]{:S(2)}) %copy-start.1) | copy-done | bytes 2097176
  124.0 1.0 copy-done.6
  125.0 1.0 copy-done.9
  126.1 1.0 copy-done.12
  127.1 0.8 copy-done.23
  127.9 0.8 copy-done.25
  128.6 0.8 copy-done.27
  129.4 5.5 %shard_map.138 = f32[64,128,128]{2,1,0:T(8,128)} custom-call(bf16[64,128,128]{2,1,0:T(8,128)(2,1)S(1)} %get-tuple-element.23.high_ref, bf16[64,128,128]{2,1,0:T(8,128)(2,1)S(1)} %copy-done.1, f32[64,16,128]{2,1,0:T(8,128)S(1)} %copy-done.9, f32[64,16,128]{2,1,0:T(8,128)S(1)} %copy-done.12, f32[64,16,128]{2,1,0:T(8,128)S(1)} %copy-done.6, ...), custom_call_target="tpu_custom_call" | custom-call | flops 419430400 | bytes 10035200 | tf_op jit(solution)/shard_map/pallas_call | solution.py:41
  (60 shorter events, 5.3 us)
Async XLA Ops:
  0.6 18.0 %copy-start.33 = (f32[128,16]{0,1:T(8,128)S(1)}, f32[128,16]{0,1:T(8,128)}, u32[]{:S(2)}) copy-start(f32[128,16]{0,1:T(8,128)} %param.19) | copy-start | bytes 24580
  0.6 18.0 %copy-start.32 = (f32[128]{0:T(128)S(1)}, f32[128]{0:T(128)}, u32[]{:S(2)}) copy-start(f32[128]{0:T(128)} %param.14) | copy-start | bytes 1540
  1.8 0.8 copy-start.28
  2.6 0.8 copy-start.29
  4.8 18.5 %all-to-all-start.1 = ((f32[8,128,96]{1,2,0:T(8,128)}), f32[8,128,96]{1,2,0:T(8,128)S(1)}, u32[]{:S(2)}, u32[]{:S(2)}) async-start(f32[8,128,96]{1,2,0:T(8,128)} %copy.18), calls=%async_computation.1 | async-start | bytes 786432 | tf_op jit(solution)/shard_map/all_to_all | solution.py:275
  12.9 7.7 %collective-permute-start = (f32[64,96]{1,0:T(8,128)S(1)}, f32[64,96]{1,0:T(8,128)S(1)}, u32[]{:S(2)}, u32[]{:S(2)}) collective-permute-start(f32[64,96]{1,0:T(8,128)S(1)} %copy-done.29), channel_id=1, source_target_pairs={{0,0},{1,8},{2,16},{3,24},{4,32},{5,40},{6,48},{7,56},{8,64},{9,72... | collective-permute-start | bytes 73736 | tf_op jit(solution)/shard_map/ppermute | solution.py:296
  24.1 15.6 %all-to-all-start = ((f32[16,64,96]{2,1,0:T(8,128)}), f32[16,64,96]{2,1,0:T(8,128)S(1)}, u32[]{:S(2)}, u32[]{:S(2)}) async-start(f32[16,64,96]{2,1,0:T(8,128)} %broadcast_in_dim.6), calls=%async_computation | async-start | bytes 1048576 | tf_op jit(solution)/shard_map/all_to_all | solution.py:275
  32.3 24.6 %copy-start.34 = (f32[768]{0:T(1024)S(1)}, f32[768]{0:T(1024)}, u32[]{:S(2)}) copy-start(f32[768]{0:T(1024)} %param.13) | copy-start | bytes 9220
  39.7 7.2 %copy-start.13 = (f32[16,64,96]{2,1,0:T(8,128)}, f32[16,64,96]{2,1,0:T(8,128)S(1)}, u32[]{:S(2)}) copy-start(f32[16,64,96]{2,1,0:T(8,128)S(1)} %all-to-all-done.recv_ref) | copy-start | bytes 1179652
  39.7 24.2 %all-to-all-start.2 = ((f32[8,64,96]{2,1,0:T(8,128)}), f32[8,64,96]{2,1,0:T(8,128)}, u32[]{:S(2)}, u32[]{:S(2)}) async-start(f32[8,64,96]{2,1,0:T(8,128)} %shard_map.131), calls=%async_computation.2 | async-start | bytes 524288 | tf_op jit(solution)/shard_map/all_to_all | solution.py:275
  54.9 1.3 copy-start
  56.2 0.6 copy-start.21
  56.8 7.1 %copy-start.5 = (f32[64,16,128]{2,1,0:T(8,128)}, f32[64,16,128]{2,1,0:T(8,128)S(1)}, u32[]{:S(2)}) copy-start(f32[64,16,128]{2,1,0:T(8,128)S(1)} %get-tuple-element.20.bias_ref) | copy-start | bytes 1572868
  57.4 1.7 %copy-start.2 = (f32[768,768]{1,0:T(8,128)S(1)}, f32[768,768]{1,0:T(8,128)}, u32[]{:S(2)}) copy-start(f32[768,768]{1,0:T(8,128)} %wq_ref.1) | copy-start | bytes 7077892
  59.1 1.7 %copy-start.3 = (f32[768,768]{1,0:T(8,128)S(1)}, f32[768,768]{1,0:T(8,128)}, u32[]{:S(2)}) copy-start(f32[768,768]{1,0:T(8,128)} %wg_ref.1) | copy-start | bytes 7077892
  62.5 0.7 copy-start.15
  63.2 0.7 copy-start.19
  63.9 1.7 %copy-start.4 = (f32[768,768]{1,0:T(8,128)S(1)}, f32[768,768]{1,0:T(8,128)}, u32[]{:S(2)}) copy-start(f32[768,768]{1,0:T(8,128)} %wk_ref.1) | copy-start | bytes 7077892
  65.6 1.0 copy-start.14
  66.6 0.9 copy-start.16
  67.6 0.9 copy-start.20
  68.5 18.0 %copy-start.35 = (pred[96]{0:T(512)(128)(4,1)S(1)}, pred[96]{0:T(512)(128)(4,1)}, u32[]{:S(2)}) copy-start(pred[96]{0:T(512)(128)(4,1)} %compare_and_fusion) | copy-start | bytes 292
  77.7 0.8 copy-start.7
  78.5 0.7 copy-start.18
  79.2 0.6 copy-start.30
  79.8 7.3 %copy-start.10 = (f32[64,16,128]{2,1,0:T(8,128)}, f32[64,16,128]{2,1,0:T(8,128)S(1)}, u32[]{:S(2)}) copy-start(f32[64,16,128]{2,1,0:T(8,128)S(1)} %get-tuple-element.26.dprobs_ref) | copy-start | bytes 1572868
  79.8 15.3 %all-to-all-start.3 = ((f32[8,64,128]{2,1,0:T(8,128)}), f32[8,64,128]{2,1,0:T(8,128)}, u32[]{:S(2)}, u32[]{:S(2)}) async-start(f32[8,64,128]{2,1,0:T(8,128)} %copy-done.18), calls=%async_computation.3 | async-start | bytes 524288 | tf_op jit(solution)/shard_map/all_to_all | solution.py:275
  87.1 1.0 copy-start.8
  88.1 1.0 copy-start.11
  89.1 0.8 copy-start.22
  95.1 0.8 copy-start.31
  97.4 0.6 copy-start.24
  98.0 16.5 %copy-start.26 = (f32[64,16]{1,0:T(8,128)}, f32[64,16]{1,0:T(8,128)S(1)}, u32[]{:S(2)}) copy-start(f32[64,16]{1,0:T(8,128)S(1)} %get-tuple-element.31.dlt_ref) | copy-start | bytes 12292
  112.5 0.9 copy-start.17
  114.5 20.5 %all-to-all-start.5 = ((f32[16,16,128]{2,1,0:T(8,128)}), f32[16,16,128]{2,1,0:T(8,128)S(1)}, u32[]{:S(2)}, u32[]{:S(2)}) async-start(f32[16,16,128]{2,1,0:T(8,128)} %get-tuple-element.32), calls=%async_computation.5 | async-start | bytes 262144 | tf_op jit(solution)/shard_map/all_to_all | solution.py:275
  122.4 1.6 %copy-start.1 = (bf16[64,128,128]{2,1,0:T(8,128)(2,1)S(1)}, bf16[64,128,128]{2,1,0:T(8,128)(2,1)}, u32[]{:S(2)}) copy-start(bf16[64,128,128]{2,1,0:T(8,128)(2,1)} %copy-done) | copy-start | bytes 6291460
  124.0 1.0 copy-start.6
  125.0 1.0 copy-start.9
  126.1 1.0 copy-start.12
  127.1 0.8 copy-start.23
  127.9 0.8 copy-start.25
  128.6 0.8 copy-start.27

commit v2 on v0

v2 whole, which is shorter than its diff:
```python
import functools

import jax
import jax.numpy as jnp
from jax import lax
from jax.experimental import pallas as pl
from jax.experimental.pallas import tpu as pltpu
from jax.sharding import PartitionSpec as P

F32 = jnp.float32
BF16 = jnp.bfloat16
EPS = 1e-05
NN = (((1,), (0,)), ((), ()))
NT = (((1,), (1,)), ((), ()))
TN = (((0,), (0,)), ((), ()))
MIB = 1024 * 1024
VMEM_BYTES = 60 * MIB
PARTS = 4
GROUP = 4
FAR = pl.BlockSpec(memory_space=pl.ANY)
NEAR = pl.BlockSpec(memory_space=pltpu.VMEM)


def split(x):
    high = x.astype(BF16)
    return high, (x - high.astype(F32)).astype(BF16)


def dg(a, b, dims):
    return lax.dot_general(a, b, dims, preferred_element_type=F32)


def dot3(a, b, dims):
    ah, al = split(a)
    bh, bl = split(b)
    return dg(ah, bh, dims) + dg(al, bh, dims) + dg(ah, bl, dims)


class Near:
    def __init__(self, src, dst, sem):
        self.copy = pltpu.make_async_copy(src, dst, sem)
        self.copy.start()
        self.dst = dst
        self.waiting = True

    def ready(self):
        if self.waiting:
            self.copy.wait()
            self.waiting = False
        return self.dst


def call(kernel, out_shape, flops, args, scratch=(), near=None, far_out=None, alias=None, vmem=VMEM_BYTES):
    nbytes = sum(a.size * a.dtype.itemsize for a in args)
    for o in jax.tree.leaves(out_shape):
        nbytes += o.size * jnp.dtype(o.dtype).itemsize
    kw = {} if alias is None else {"input_output_aliases": alias}
    scratch = list(scratch)
    body = kernel
    if near is not None:
        kw["in_specs"] = [FAR] * len(args)
        small = [k for k, yes in enumerate(near) if yes]
        scratch += [pltpu.VMEM(args[k].shape, args[k].dtype) for k in small]
        scratch.append(pltpu.SemaphoreType.DMA((len(small),)))

        def body(*refs):
            refs = list(refs)
            places = refs[-len(small) - 1 : -1]
            for n, (k, place_) in enumerate(zip(small, places)):
                refs[k] = Near(refs[k], place_, refs[-1].at[n])
            kernel(*refs[: -len(small) - 1])

    if far_out is not None:
        specs = tuple(FAR if far else NEAR for far in far_out)
        kw["out_specs"] = specs if isinstance(out_shape, tuple) else specs[0]
    return pl.pallas_call(
        body,
        out_shape=out_shape,
        scratch_shapes=scratch,
        compiler_params=pltpu.CompilerParams(vmem_limit_bytes=vmem),
        cost_estimate=pl.CostEstimate(flops=flops, bytes_accessed=nbytes, transcendentals=0),
        **kw,
    )(*args)


class Stream:
    def __init__(self, src, dst, sems, parts=PARTS, shift=0):
        self.src, self.dst, self.sems, self.parts = src, dst, sems, parts
        self.rows = min(src.shape[0], dst.shape[0]) // parts
        self.src_shift = shift if src.shape[0] > dst.shape[0] else 0
        self.dst_shift = shift if src.shape[0] < dst.shape[0] else 0

    def copy(self, k):
        first = pl.multiple_of(k * self.rows, self.rows)
        there = pl.ds(first + self.src_shift, self.rows)
        here = pl.ds(first + self.dst_shift, self.rows)
        return pltpu.make_async_copy(self.src.at[there], self.dst.at[here], self.sems.at[k])

    def start(self):
        for k in range(self.parts):
            self.copy(k).start()

    def wait(self):
        for k in range(self.parts):
            self.copy(k).wait()


def sds(*shape, dtype=F32):
    return jax.ShapeDtypeStruct(shape, dtype)


def head_mask(heads, width):
    lane = lax.broadcasted_iota(jnp.int32, (heads, width), 1)
    row = lax.broadcasted_iota(jnp.int32, (heads, width), 0)
    size = width // heads
    return (lane >= row * size) & (lane < (row + 1) * size)


def eye_mask(n):
    return lax.broadcasted_iota(jnp.int32, (n, n), 0) == lax.broadcasted_iota(jnp.int32, (n, n), 1)


def first_kernel(single_ref, cot_ref, wout_ref, out_ref):
    n, _, lanes = out_ref.shape
    rows, block = single_ref.shape
    rest = lanes - block
    half = rows // 2
    single = single_ref[...]
    ch, cl = split(cot_ref[...])
    wh, wl = split(wout_ref[...])
    two = dg(jnp.concatenate([ch, cl], axis=0), wh, NN)
    full = two[:rows] + two[rows:] + dg(ch, wl, NN)
    for k in range(n):
        part = full[:, k * block : (k + 1) * block]
        out_ref[k, :rows, :block] = single
        out_ref[k, :rows, block:] = part[:, :rest]
        out_ref[k, rows:, : block - rest] = part[:half, rest:]
        out_ref[k, rows:, block - rest :] = part[half:, rest:]


def joined_norm(blocks, out_ref, row):
    rows, block = blocks[0].shape
    width = block * len(blocks)
    centre = sum(jnp.sum(b, axis=-1, keepdims=True) for b in blocks) / width
    blocks = [b - centre for b in blocks]
    spread = sum(jnp.sum(b * b, axis=-1, keepdims=True) for b in blocks) / width
    scale = lax.rsqrt(spread + EPS)
    for k, b in enumerate(blocks):
        part = slice(k * block, (k + 1) * block)
        out_ref[row : row + rows, part] = b * scale


def gained(normed, gain_ref):
    tiles, lanes = gain_ref.shape
    parts = [
        split(normed[:, t * lanes : (t + 1) * lanes] * gain_ref[t : t + 1, :]) for t in range(tiles)
    ]
    return jnp.concatenate(
        [jnp.concatenate([p[k] for p in parts], axis=1) for k in range(2)], axis=0
    )


def project(both, weight, copies):
    rows = both.shape[0] // 2
    third = weight.shape[0] // 3
    out = None
    for k, one in enumerate(copies):
        one.wait()
        here = slice(k * third, (k + 1) * third)
        wh, wl = split(weight[here, :])
        two = dg(both[:, here], wh, NN)
        part = two[:rows] + two[rows:] + dg(both[:rows, here], wl, NN)
        out = part if out is None else out + part
    return out


def fetch(src, dst, sems):
    rows = src.shape[0] // 3
    out = []
    for k in range(3):
        here = pl.ds(k * rows, rows)
        one = pltpu.make_async_copy(src.at[here], dst.at[here], sems.at[k])
        one.start()
        out.append(one)
    return out


def query_kernel(
    pair_far, wb, pgain, recv, gain, wq_far, wg_far,
    bias_far, rs_far, back_ref, query_ref, gate_ref,
    x_ref, bias_ref, rs_ref, sems, normed, wq, wg, qsem, gsem,
):
    take, give = bias_streams(pair_far, bias_far, rs_far, x_ref, bias_ref, rs_ref, sems, 1)
    query_copies = fetch(wq_far, wq, qsem)
    gate_copies = fetch(wg_far, wg, gsem)
    n, rows, block = back_ref.shape
    recv_ref = recv.ready()
    total = recv_ref[0]
    for k in range(1, n):
        total = total + recv_ref[k]
    rest = total.shape[1] - block
    right = jnp.concatenate([total[rows:, : block - rest], total[rows:, block - rest :]], axis=0)
    total = jnp.concatenate([total[:rows, block:], right], axis=1)
    for k in range(n):
        back_ref[k] = total
    bias_rows(take, give, wb.ready(), pgain.ready(), x_ref, bias_ref, rs_ref)
    joined_norm([recv_ref[k, :rows, :block] for k in range(n)], normed, 0)
    both = gained(normed, gain.ready())
    query_ref[...] = project(both, wq, query_copies) * (48 ** -0.5)
    gate_ref[...] = 1.0 / (1.0 + jnp.exp(-project(both, wg, gate_copies)))
    for g in give:
        g.wait()


def centred(x):
    return x - jnp.sum(x, axis=-1, keepdims=True) * (1.0 / x.shape[-1])


def bias_streams(pair_far, bias_far, rs_far, x_ref, bias_ref, rs_ref, sems, part):
    parts = PARTS // 2
    take = Stream(pair_far, x_ref, sems.at[0], parts, part * x_ref.shape[0])
    take.start()
    return take, [Stream(bias_ref, bias_far, sems.at[1], 1), Stream(rs_ref, rs_far, sems.at[2], 1)]


def bias_rows(take, give, wb_ref, pgain_ref, x_ref, bias_ref, rs_ref):
    chans = x_ref.shape[2]
    heads = bias_ref.shape[1]
    wh, wl = split(wb_ref[...] * pgain_ref[...])
    top = jnp.concatenate([wh, wh], axis=1)
    left = jnp.concatenate([top, jnp.concatenate([wl, jnp.zeros_like(wl)], axis=1)], axis=0)
    ones = jnp.ones((8, 2 * chans), BF16)

    def step(k, carry):
        take.copy(k).wait()
        for j in range(take.rows):
            i = k * take.rows + j
            d = centred(x_ref[i])
            spread = dg(ones, jnp.concatenate(split(d * d), axis=1), NT) * (1.0 / chans)
            rs = lax.rsqrt(spread[0:1] + EPS)
            two = dg(left, jnp.concatenate(split(d), axis=1), NT)
            bias_ref[i] = (two[:heads] + two[heads:]) * rs
            rs_ref[pl.ds(i, 1), :] = rs
        return carry

    lax.fori_loop(0, take.parts, step, 0)
    for g in give:
        g.start()


def pair_kernel(pair_far, wb, pgain, bias_far, rs_far, x_ref, bias_ref, rs_ref, sems):
    take, give = bias_streams(pair_far, bias_far, rs_far, x_ref, bias_ref, rs_ref, sems, 0)
    bias_rows(take, give, wb.ready(), pgain.ready(), x_ref, bias_ref, rs_ref)
    for g in give:
        g.wait()


def halves(heads, width):
    return [
        (slice(g * heads // 2, (g + 1) * heads // 2), slice(g * width // 2, (g + 1) * width // 2))
        for g in range(2)
    ]


def by_head(rows, mask):
    wide = jnp.where(mask, rows[:, None, :], 0.0)
    return split(wide.reshape(-1, rows.shape[1]))


def against(rows, mask, high, low):
    keys = high.shape[0]
    rh, rl = by_head(rows, mask)
    two = dg(rh, jnp.concatenate([high, low], axis=0), NT)
    return two[:, :keys] + two[:, keys:] + dg(rl, high, NT)


def score_kernel(
    recv, gain, wk_far, wv_far, query, bias_a, bias_b,
    high_ref, low_ref, expo_ref, acc_ref, stat_ref,
    normed, wk, wv, ksem, vsem,
):
    key_copies = fetch(wk_far, wk, ksem)
    value_copies = fetch(wv_far, wv, vsem)
    recv_ref = recv.ready()
    n_row, rows, block = recv_ref.shape
    queries, heads, keys = expo_ref.shape
    width = normed.shape[1]
    n_col = width // block
    col = lax.axis_index("col")
    for t in range(n_row // n_col):
        joined_norm([recv_ref[place(k, col, t)] for k in range(n_col)], normed, t * rows)
    both = gained(normed, gain.ready())
    kh, kl = split(project(both, wk, key_copies))
    half = heads // 2
    mask = head_mask(half, width // 2)[None]
    eye = eye_mask(half)[None]

    def lanes(column):
        return jnp.sum(jnp.where(eye, column.reshape(queries, half, 1), 0.0), axis=1)

    parts = []
    query_ref = query.ready()
    bias_refs = [bias_a.ready(), bias_b.ready()]
    for some, part in halves(heads, width):
        bias = jnp.concatenate([b[:, some] for b in bias_refs], axis=0)
        scores = against(query_ref[:, part], mask, kh[:, part], kl[:, part])
        scores = scores + bias.reshape(queries * half, keys)
        top = jnp.max(scores, axis=-1, keepdims=True)
        expo = jnp.exp(scores - top)
        total = jnp.sum(expo, axis=-1, keepdims=True)
        inv = 1.0 / total
        expo_ref[:, some] = expo.reshape(queries, half, keys)
        for place_, column in enumerate((top + jnp.log(total), top, inv)):
            first = place_ * heads + some.start
            stat_ref[:, first : first + half] = lanes(column)
        parts.append(split(expo * inv))
    vh, vl = split(project(both, wv, value_copies))
    high_ref[...] = vh
    low_ref[...] = vl
    for (some, part), (eh, el) in zip(halves(heads, width), parts):
        high = vh[:, part]
        wide = dg(jnp.concatenate([eh, el], axis=1), jnp.concatenate([high, high], axis=0), NN)
        wide = wide + dg(eh, vl[:, part], NN)
        wide = jnp.where(mask, wide.reshape(queries, half, width // 2), 0.0)
        acc_ref[:, part] = jnp.sum(wide, axis=1)


def delta_kernel(
    back, gate, high, low, expo, acc, stat, pay_ref, dprobs_ref, dctx
):
    back_ref, gate_ref, acc_ref, stat_ref = [v.ready() for v in (back, gate, acc, stat)]
    high_ref, low_ref, expo_ref = [v.ready() for v in (high, low, expo)]
    n_col, _, block = back_ref.shape
    queries, heads, keys = expo_ref.shape
    width = dctx.shape[1]
    for k in range(n_col):
        part = slice(k * block, (k + 1) * block)
        dctx[:, part] = back_ref[k] * gate_ref[:, part]
        pay_ref[k, :, :block] = acc_ref[:, part]
        pay_ref[k, :, block : block + heads] = stat_ref[:, :heads]
    half = heads // 2
    mask = head_mask(half, width // 2)[None]
    eye = eye_mask(half)[None]
    for some, part in halves(heads, width):
        dp = against(dctx[:, part], mask, high_ref[:, part], low_ref[:, part])
        dp = dp.reshape(queries, half, keys)
        dprobs_ref[:, some] = dp
        delta = jnp.sum(expo_ref[:, some] * dp, axis=-1, keepdims=True)
        first = 2 * heads + some.start
        delta = jnp.sum(jnp.where(eye, delta, 0.0), axis=1) * stat_ref[:, first : first + half]
        first = block + heads + some.start
        for k in range(n_col):
            pay_ref[k, :, first : first + half] = delta


def moment_kernel(
    x_far, expo_far, dprobs_far, rs_a, rs_b, out_far, x_ref, expo_ref, dprobs_ref, out_ref, sems
):
    heads = expo_ref.shape[1]
    chans = out_ref.shape[2]
    take = [
        Stream(x_far, x_ref, sems.at[0]),
        Stream(expo_far, expo_ref, sems.at[1], 1),
        Stream(dprobs_far, dprobs_ref, sems.at[2], 1),
    ]
    give = Stream(out_ref, out_far, sems.at[3], 2)
    for t in reversed(take):
        t.start()
    for t in take[1:]:
        t.wait()
    half = expo_ref.shape[0] // 2

    def step(rs_ref, shift, k, carry):
        take[0].copy(k).wait()
        for j in range(take[0].rows):
            i = k * take[0].rows + j
            e = expo_ref[i] * rs_ref[pl.ds(i - shift, 1), :]
            bh, bl = split(jnp.concatenate([e * dprobs_ref[i], e], axis=0))
            d2 = jnp.concatenate(split(centred(x_ref[i])), axis=1)
            wide = dg(jnp.concatenate([bh, bl], axis=0), d2, NN)
            high = wide[: 2 * heads]
            out_ref[i] = high[:, :chans] + high[:, chans:] + wide[2 * heads :, :chans]
        return carry

    lax.fori_loop(0, PARTS // 2, functools.partial(step, rs_a.ready(), 0), 0)
    give.copy(0).start()
    lax.fori_loop(PARTS // 2, PARTS, functools.partial(step, rs_b.ready(), half), 0)
    give.copy(1).start()
    give.wait()


def join_kernel(recv_ref, stat_ref, moment_ref, pgain_ref, pay_ref, join_ref):
    n, rows, lanes = recv_ref.shape
    heads = moment_ref.shape[1] // 2
    block = lanes - 2 * heads
    size = n * block // heads
    lane = lax.broadcasted_iota(jnp.int32, (heads, block), 1) + lax.axis_index("col") * block
    row = lax.broadcasted_iota(jnp.int32, (heads, block), 0) * size
    sel = jnp.where((lane >= row) & (lane < row + size), 1.0, 0.0)
    lse = [recv_ref[k, :, block : block + heads] for k in range(n)]
    top = functools.reduce(jnp.maximum, lse)
    weight = [jnp.exp(v - top) for v in lse]
    total = sum(weight)
    inv = 1.0 / total
    weight = [w * inv for w in weight]
    delta = sum(w * recv_ref[k, :, block + heads :] for k, w in enumerate(weight))
    fac = jnp.exp(stat_ref[:, heads : 2 * heads] - (top + jnp.log(total)))
    join_ref[:, :heads] = fac
    join_ref[:, heads : 2 * heads] = delta
    context = sum(
        lax.dot_general(w, sel, NN, precision=lax.Precision.HIGHEST, preferred_element_type=F32)
        * recv_ref[k, :, :block]
        for k, w in enumerate(weight)
    )
    eye = eye_mask(heads)[None]

    def column(v):
        return jnp.sum(jnp.where(eye, v[:, None, :], 0.0), axis=-1, keepdims=True)

    part = jnp.sum(
        column(fac) * moment_ref[:, :heads] - column(fac * delta) * moment_ref[:, heads:], axis=0
    ) * pgain_ref[...]
    for k in range(n):
        pay_ref[k, :rows, :block] = context
        pay_ref[k, rows:, :] = part


def grad_kernel(
    part, x_far, expo_far, dprobs_far, bias_far, rs, joined, wb, pgain, *refs
):
    out_far, x_ref, expo_ref, dprobs_ref, bias_ref, fac_ref, dlt_ref, out_ref, sems = refs[-9:]
    count, keys = out_ref.shape[:2]
    shift = part * count
    parts = PARTS // 2
    take = [
        Stream(x_far, x_ref, sems.at[0], parts, shift),
        Stream(expo_far, expo_ref, sems.at[1], 1, shift),
        Stream(dprobs_far, dprobs_ref, sems.at[2], 1, shift),
        Stream(bias_far, bias_ref, sems.at[3], 1),
    ]
    give = Stream(out_ref, out_far, sems.at[4], parts, shift)
    for t in reversed(take):
        t.start()
    heads = expo_ref.shape[1]
    chans = out_ref.shape[2]
    eye = eye_mask(heads)
    wt = centred(wb.ready()[...] * pgain.ready()[...])
    join_ref = joined.ready()
    rs_ref = rs.ready()
    zero = jnp.zeros_like(wt)
    mean = jnp.full_like(wt, 1.0 / chans)
    wh, wl = split(
        jnp.concatenate(
            [jnp.concatenate([wt, zero], axis=1), jnp.concatenate([zero, mean], axis=1)], axis=0
        )
    )

    def spread(w):
        nil = jnp.zeros_like(w)
        rows = [
            jnp.concatenate([w if m == n else nil for n in range(GROUP)], axis=1)
            for m in range(GROUP)
        ]
        return jnp.concatenate(rows, axis=0)

    weights = jnp.concatenate([spread(wh), spread(wh)], axis=0)
    rest = spread(wl)
    mask = eye[None]

    def columns(first):
        value = join_ref[pl.ds(shift, count), first : first + heads]
        value = jnp.where(mask, value[:, None, :], 0.0).reshape(count * heads, heads)
        high, rest = split(value)
        low, least = split(value - high.astype(F32))
        ones = jnp.ones((3 * heads, keys), BF16)
        return dg(jnp.concatenate([high, low, least], axis=1), ones, NN).reshape(count, heads, keys)

    fac_ref[...] = columns(0)
    dlt_ref[...] = columns(heads)
    for t in take[1:]:
        t.wait()

    def cells(i):
        rs = rs_ref[pl.ds(i, 1), :]
        u = expo_ref[i] * fac_ref[i] * (dprobs_ref[i] - dlt_ref[i]) * rs
        return [u, u * bias_ref[i] * rs]

    def step(k, carry):
        take[0].copy(k).wait()
        for j in range(0, give.rows, GROUP):
            first = k * give.rows + j
            rows = [part for m in range(GROUP) for part in cells(first + m)]
            high, low = split(jnp.concatenate(rows, axis=0).T)
            wide = dg(jnp.concatenate([high, low], axis=1), weights, NN) + dg(high, rest, NN)
            for m in range(GROUP):
                one = wide[:, 2 * chans * m : 2 * chans * (m + 1)]
                i = first + m
                out_ref[i] = one[:, :chans] - centred(x_ref[i]) * one[:, chans:]
        give.copy(k).start()
        return carry

    lax.fori_loop(0, parts, step, 0)
    give.wait()


def share_kernel(recv_ref, pay_ref):
    heads = pay_ref.shape[1]
    rows = recv_ref.shape[1] - heads
    total = recv_ref[0, rows:, :]
    for k in range(1, recv_ref.shape[0]):
        total = total + recv_ref[k, rows:, :]
    for k in range(pay_ref.shape[0]):
        pay_ref[k] = total


def out_kernel(recv_ref, gate_ref, wout_ref, att_ref, gated):
    rows, block = att_ref.shape
    for k in range(recv_ref.shape[0]):
        part = slice(k * block, (k + 1) * block)
        gated[:, part] = recv_ref[k, :rows, :block] * gate_ref[:, part]
    att_ref[...] = dot3(gated[...], wout_ref[...], NT)


def last_kernel(recv_ref, out_ref):
    total = recv_ref[0]
    for k in range(1, recv_ref.shape[0]):
        total = total + recv_ref[k]
    out_ref[...] = total


def place(col, owner, core):
    high, x = col // 4, col % 4
    y, low = owner // 2, owner % 2
    spot = (y + 6 - x + owner % 4) % 4
    near = lax.select(high == owner // 4, low, 1 - low) if not isinstance(owner, int) else (
        low if high == owner // 4 else 1 - low
    )
    return (spot * 2 + near) * 2 + core


def swap(x, axis):
    return lax.all_to_all(x, axis, 0, 0, tiled=True)


def local(
    single, pair, single_gain, pair_gain, w_query, w_key, w_value, w_gate, w_bias, w_out, cotangent
):
    n_row, n_col = lax.axis_size("row"), lax.axis_size("col")
    queries, keys, chans = pair.shape
    heads = w_bias.shape[1]
    width = single_gain.shape[0]
    block = single.shape[1]
    per = n_row // n_col
    gain = single_gain.reshape(-1, chans)
    pgain = pair_gain[None]
    wb = w_bias.T
    wout = w_out.T
    dma = pltpu.SemaphoreType.DMA
    shape_e = sds(queries, heads, keys)

    def mem(shape):
        return pltpu.VMEM(shape.shape, shape.dtype)

    perm = [
        (r * n_col + c, place(c, r // per, r % per) * n_col + r // per)
        for r in range(n_row)
        for c in range(n_col)
    ]
    moved = lax.ppermute(single, ("row", "col"), perm)
    pay1 = call(
        first_kernel,
        sds(n_col, queries + queries // 2, chans),
        2 * queries * width * block * 3,
        (single, cotangent, wout),
    )
    recv1 = swap(pay1, "col")
    shape_x = sds(queries, keys, chans)
    half_e = sds(queries // 2, heads, keys)
    half_rs = sds(queries // 2, keys)
    half_x = sds(queries // 2, keys, chans)
    held = [mem(half_x), mem(half_e), mem(half_rs), dma((3, PARTS // 2))]
    bias_a, rs_a = call(
        pair_kernel,
        (half_e, half_rs),
        queries * keys * chans * 200,
        (pair, wb, pgain),
        held,
        (0, 1, 1),
        (1, 1),
    )
    moved, rs_a = lax.optimization_barrier((moved, rs_a))
    recv2 = swap(jnp.broadcast_to(moved[None], (n_row,) + moved.shape), "row")
    square = pltpu.VMEM((width, width), F32)
    bias_b, rs_b, back_pay, query, gate = call(
        query_kernel,
        (
            half_e,
            half_rs,
            sds(n_col, queries, block),
            sds(queries, width),
            sds(queries, width),
        ),
        queries * keys * chans * 200 + queries * width * width * 12,
        (pair, wb, pgain, recv1, gain, w_query, w_gate),
        held + [pltpu.VMEM((queries, width), F32), square, square, dma((3,)), dma((3,))],
        (0, 1, 1, 1, 1, 0, 0),
        (1, 1, 0, 0, 0),
    )
    back = swap(back_pay, "col")
    vhigh, vlow, expo, acc, stat = call(
        score_kernel,
        (
            sds(keys, width, dtype=BF16),
            sds(keys, width, dtype=BF16),
            shape_e,
            sds(queries, width),
            sds(queries, chans),
        ),
        keys * width * width * 12,
        (recv2, gain, w_key, w_value, query, bias_a, bias_b),
        [pltpu.VMEM((keys, width), F32), square, square, dma((3,)), dma((3,))],
        (1, 1, 0, 0, 1, 1, 1),
    )
    pay4, dprobs = call(
        delta_kernel,
        (sds(n_col, queries, chans), shape_e),
        queries * keys * width * 12,
        (back, gate, vhigh, vlow, expo, acc, stat),
        [pltpu.VMEM((queries, width), F32)],
        (1,) * 7,
    )
    recv4 = swap(pay4, "col")
    shape_m = sds(queries, 2 * heads, chans)
    moment = call(
        moment_kernel,
        shape_m,
        queries * keys * chans * heads * 12,
        (pair, expo, dprobs, rs_a, rs_b),
        [mem(shape_x), mem(shape_e), mem(shape_e), mem(shape_m), dma((4, PARTS))],
        (0, 0, 0, 1, 1),
        (1,),
    )
    pay5, joined = call(
        join_kernel,
        (sds(n_col, queries + heads, chans), sds(queries, chans)),
        queries * heads * chans * 8,
        (recv4, stat, moment, pgain),
    )
    recv5 = swap(pay5, "col")
    cost = queries * keys * chans * 200
    held = [mem(half_x)] + 5 * [mem(half_e)] + [mem(half_x), dma((5, PARTS // 2))]
    place_of = (0, 0, 0, 0, 1, 1, 1, 1)
    first = call(
        functools.partial(grad_kernel, 0),
        shape_x,
        cost,
        (pair, expo, dprobs, bias_a, rs_a, joined, wb, pgain),
        held,
        place_of,
        (1,),
    )
    recv5, first = lax.optimization_barrier((recv5, first))
    pay6 = call(
        share_kernel, sds(n_row, heads, chans), queries * width, (recv5,), vmem=4 * MIB
    )
    recv6 = swap(pay6, "row")
    pair_grad = call(
        functools.partial(grad_kernel, 1),
        shape_x,
        cost,
        (pair, expo, dprobs, bias_b, rs_b, joined, wb, pgain, first),
        held,
        place_of + (0,),
        (1,),
        {8: 0},
    )
    attended = call(
        out_kernel,
        sds(queries, block),
        queries * width * block * 6,
        (recv5, gate, wout),
        [pltpu.VMEM((queries, width), F32)],
    )
    recv6, pair_grad, attended = lax.optimization_barrier((recv6, pair_grad, attended))
    bias_grad = call(last_kernel, sds(heads, chans), chans * heads, (recv6,), vmem=4 * MIB)
    return attended, pair_grad, bias_grad.T


def solution(mesh):
    placed = (
        P("row", "col"),
        P("row", "col", None),
        P(),
        P(),
        P(),
        P(),
        P(),
        P(),
        P(),
        P(None, "col"),
        P("row", "col"),
    )
    return jax.shard_map(
        local,
        mesh=mesh,
        in_specs=placed,
        out_specs=(P("row", "col"), P("row", "col", None), P()),
        check_vma=False,
    )
```

time: 346 us -> 99 us (0.29)
  blocking collectives: 162 us -> 0 us
  waiting for transfers between devices: 60.8 us -> 15.1 us
  Pallas kernels: 0 us -> 42.1 us
  matrix products: 40.2 us -> 0 us
  other arithmetic: 39.5 us -> 0 us
  starting transfers between devices: 0.31 us -> 37.9 us
  local copies, waits for them, and re-layouts: 26 us -> 2.33 us
  between operations: 15.8 us -> 0.72 us
    all_gather x3 -> x0, blocking collectives: 90.7 us -> none  [the longest x2 60.2 us: joined(): everything = jax.tree.map(lambda part: lax.all_gather(part, axis), array)]
    psum x1 -> x0, blocking collectives: 70.9 us -> none  [local(): bias_grad = lax.psum(weight_part, ('row', 'col'))]
    pallas_call x0 -> x12, Pallas kernels: none -> 42.1 us  [call(): pl.pallas_call(body, out_shape=out_shape, scratch_shapes=scratch, compile...]
    all_gather x2 -> x0, waiting for transfers between devices: 37.5 us -> none  [the longest x1 27.6 us: local(): all_kv = lax.all_gather(kv_rows, 'row', axis=0, tiled=True)]
    all_to_all x0 -> x6, starting transfers between devices: none -> 35 us  [swap(): return lax.all_to_all(x, axis, 0, 0, tiled=True)]
    dot_general x11 -> x0, matrix products: 33.9 us -> none  [the longest x3 16.1 us: bias_of(): jnp.einsum('ijc,ch->ihj', layer_norm(pair_tile, pair_gain), weight, preci...]
    psum x1 -> x0, waiting for transfers between devices: 23.2 us -> none  [local(): back_sum = lax.psum(jnp.dot(cotangent, w_out.T, precision=highest), 'col')]
    add x14 -> x0, other arithmetic: 19.4 us -> none  [the longest x7 10.1 us: combine_parts(): acc_a * factor_a[:, :, None] + acc_b * factor_b[:, :, None]]
  transfers between devices with their start and end apart: 3 -> 7, of which waited for: 3 -> 6; matrix products, arithmetic and copies ran while one was open for 13% -> 0% of each run, Pallas kernels for 0% -> 33%
where the time goes in v2:
time: 99 us; the launch traced here: 98.1 us
  Pallas kernels  42.1 us (43%)
  starting transfers between devices  37.9 us (38%)
  waiting for transfers between devices  15.1 us (15%)
  local copies, waits for them, and re-layouts  2.33 us (2%)
    pallas_call x12, Pallas kernels, call(): pl.pallas_call(body, out_shape=out_shape, scratch_shapes=scratch, compile...  42.1 us
    all_to_all x6, starting transfers between devices, swap(): return lax.all_to_all(x, axis, 0, 0, tiled=True)  35 us
    all_to_all x6, waiting for transfers between devices, swap(): return lax.all_to_all(x, axis, 0, 0, tiled=True)  13.6 us
    ppermute x1, starting transfers between devices, local(): moved = lax.ppermute(single, ('row', 'col'), perm)  2.91 us
  transfers between devices with their start and end apart: 7, of which 6 were waited for; matrix products, arithmetic and copies ran while one was open for 0% of the time, Pallas kernels for 33%

profile of v2, /device:TPU:1, one launch (start us, length us, event | category | flops | bytes accessed | tf_op | source)
XLA Modules:
  0.0 98.1 jit_solution(10467760658455378250)
XLA Ops:
  0.6 2.1 %shard_map.130 = f32[8,96,128]{2,1,0:T(8,128)} custom-call(f32[64,96]{1,0:T(8,128)} %single_ref.1, f32[64,96]{1,0:T(8,128)} %cot_ref.1, f32[96,768]{1,0:T(8,128)} %bitcast.5), custom_call_target="tpu_custom_call" | custom-call | flops 28311552 | bytes 737280 | tf_op jit(solution)/shard_map/pallas_call | solution.py:76
  2.7 8.2 %all-to-all-start = ((f32[8,96,128]{2,1,0:T(8,128)}), f32[8,96,128]{2,1,0:T(8,128)S(1)}, u32[]{:S(2)}, u32[]{:S(2)}) async-start(f32[8,96,128]{2,1,0:T(8,128)} %shard_map.130), calls=%async_computation | async-start | bytes 786432 | tf_op jit(solution)/shard_map/all_to_all | solution.py:542
  10.9 2.9 %collective-permute-start = (f32[64,96]{1,0:T(8,128)}, f32[64,96]{1,0:T(8,128)S(1)}, u32[]{:S(2)}, u32[]{:S(2)}) collective-permute-start(f32[64,96]{1,0:T(8,128)} %single_ref.1), channel_id=1, source_target_pairs={{0,64},{1,32},{2,0},{3,96},{4,80},{5,48},{6,16},{7,112},{8,72},{9,... | collective-permute-start | bytes 73736 | tf_op jit(solution)/shard_map/ppermute | solution.py:569
  13.8 3.5 %shard_map.132 = (f32[32,16,128]{2,1,0:T(8,128)}, f32[32,128]{1,0:T(8,128)}) custom-call(f32[64,128,128]{2,1,0:T(8,128)} %refs_0_.9, f32[16,128]{1,0:T(8,128)} %bitcast.7, f32[1,128]{1,0:T(1,128)} %bitcast.13), custom_call_target="tpu_custom_call" | custom-call | flops 209715200 | bytes 4481536 | tf_op jit(solution)/shard_map/pallas_call | solution.py:76
  17.4 1.5 %collective-permute-done = f32[64,96]{1,0:T(8,128)S(1)} collective-permute-done((f32[64,96]{1,0:T(8,128)}, f32[64,96]{1,0:T(8,128)S(1)}, u32[]{:S(2)}, u32[]{:S(2)}) %collective-permute-start) | collective-permute-done | bytes 24608 | tf_op jit(solution)/shard_map/ppermute | solution.py:569
  18.9 2.7 %all-to-all-done.refs_3_ = f32[8,96,128]{2,1,0:T(8,128)S(1)} async-done(((f32[8,96,128]{2,1,0:T(8,128)}), f32[8,96,128]{2,1,0:T(8,128)S(1)}, u32[]{:S(2)}, u32[]{:S(2)}) %all-to-all-start) | async-done | bytes 393248 | tf_op jit(solution)/shard_map/all_to_all | solution.py:542
  21.5 0.0 copy-start.2
  21.5 0.9 broadcast_in_dim.10
  22.5 5.8 %all-to-all-start.2 = ((f32[16,64,96]{2,1,0:T(8,128)}), f32[16,64,96]{2,1,0:T(8,128)S(1)}, u32[]{:S(2)}, u32[]{:S(2)}) async-start(f32[16,64,96]{2,1,0:T(8,128)} %broadcast_in_dim.10), calls=%async_computation.2 | async-start | bytes 1048576 | tf_op jit(solution)/shard_map/all_to_all | solution.py:542
  28.2 0.0 copy-done.2
  28.2 6.4 %shard_map.131 = (f32[32,16,128]{2,1,0:T(8,128)}, f32[32,128]{1,0:T(8,128)}, f32[8,64,96]{2,1,0:T(8,128)}, f32[64,768]{1,0:T(8,128)}, f32[64,768]{1,0:T(8,128)}) custom-call(f32[64,128,128]{2,1,0:T(8,128)} %refs_0_.9, f32[16,128]{1,0:T(8,128)} %bitcast.8, f32[1,128]{1,0:T(1,128)} %bitcast.14, f32[8,96,128]{2,1,0:T(8,128)} %copy-done.2, f32[6,128]{1,0:T(8,128)} %bitcast.11, ...), custom_call_target="tpu_custom_call" | custom-call | flops 662700032 | bytes 10186240 | tf_op jit(solution)/shard_map/pallas_call | solution.py:76
  34.7 3.2 %all-to-all-done.2.refs_0_ = f32[16,64,96]{2,1,0:T(8,128)S(1)} async-done(((f32[16,64,96]{2,1,0:T(8,128)}), f32[16,64,96]{2,1,0:T(8,128)S(1)}, u32[]{:S(2)}, u32[]{:S(2)}) %all-to-all-start.2) | async-done | bytes 393248 | tf_op jit(solution)/shard_map/all_to_all | solution.py:542
  37.9 0.0 copy-start.1
  37.9 4.6 %all-to-all-start.1 = ((f32[8,64,96]{2,1,0:T(8,128)}), f32[8,64,96]{2,1,0:T(8,128)S(1)}, u32[]{:S(2)}, u32[]{:S(2)}) async-start(f32[8,64,96]{2,1,0:T(8,128)} %get-tuple-element.26), calls=%async_computation.1 | async-start | bytes 524288 | tf_op jit(solution)/shard_map/all_to_all | solution.py:542
  42.4 0.0 copy-done.1
  42.4 6.6 %shard_map.133 = (bf16[128,768]{1,0:T(8,128)(2,1)}, bf16[128,768]{1,0:T(8,128)(2,1)}, f32[64,16,128]{2,1,0:T(8,128)}, f32[64,768]{1,0:T(8,128)}, f32[64,128]{1,0:T(8,128)}) custom-call(f32[16,64,96]{2,1,0:T(8,128)} %copy-done.1, f32[6,128]{1,0:T(8,128)} %bitcast.12, f32[768,768]{1,0:T(8,128)} %refs_2_.1, f32[768,768]{1,0:T(8,128)} %refs_3_.1, ...), custom_call_target="tpu_custom_call" | custom-call | flops 905969664 | bytes 6982656 | tf_op jit(solution)/shard_map/pallas_call | solution.py:76
  49.1 1.2 %all-to-all-done.1.refs_0_ = f32[8,64,96]{2,1,0:T(8,128)S(1)} async-done(((f32[8,64,96]{2,1,0:T(8,128)}), f32[8,64,96]{2,1,0:T(8,128)S(1)}, u32[]{:S(2)}, u32[]{:S(2)}) %all-to-all-start.1) | async-done | bytes 196640 | tf_op jit(solution)/shard_map/all_to_all | solution.py:542
  50.3 0.0 copy-start.3
  50.3 0.7 copy-done.3
  51.0 3.4 %shard_map.134 = (f32[8,64,128]{2,1,0:T(8,128)}, f32[64,16,128]{2,1,0:T(8,128)}) custom-call(f32[8,64,96]{2,1,0:T(8,128)} %copy-done.3, f32[64,768]{1,0:T(8,128)} %get-tuple-element.27.refs_1_.gate_ref, bf16[128,768]{1,0:T(8,128)(2,1)} %get-tuple-element.33.refs_2_, bf16[128,768]{1,0:T(8,128)(2,1)} %get-tuple-element.34.refs_3_, ...), custom_call_target="tpu_custom_call" | custom-call | flops 75497472 | bytes 2326528 | tf_op jit(solution)/shard_map/pallas_call | solution.py:76
  54.3 5.5 %all-to-all-start.3 = ((f32[8,64,128]{2,1,0:T(8,128)}), f32[8,64,128]{2,1,0:T(8,128)S(1)}, u32[]{:S(2)}, u32[]{:S(2)}) async-start(f32[8,64,128]{2,1,0:T(8,128)} %get-tuple-element.38), calls=%async_computation.3 | async-start | bytes 524288 | tf_op jit(solution)/shard_map/all_to_all | solution.py:542
  59.8 4.9 %shard_map.135.moment_ref = f32[64,32,128]{2,1,0:T(8,128)} custom-call(f32[64,128,128]{2,1,0:T(8,128)} %refs_0_.9, f32[64,16,128]{2,1,0:T(8,128)} %get-tuple-element.35.refs_4_.refs_1_, f32[64,16,128]{2,1,0:T(8,128)} %get-tuple-element.39.refs_2_, f32[32,128]{1,0:T(8,128)} %get-tuple-element.40.refs_3_.refs_4_, f32[32,128]{1,0:T(8,128)} %get-tuple-element.41.refs_4_), custom_call_target="tpu_custom_call" | custom-call | flops 201326592 | bytes 6324224 | tf_op jit(solution)/shard_map/pallas_call | solution.py:76
  64.7 2.8 %all-to-all-done.3.recv_ref = f32[8,64,128]{2,1,0:T(8,128)S(1)} async-done(((f32[8,64,128]{2,1,0:T(8,128)}), f32[8,64,128]{2,1,0:T(8,128)S(1)}, u32[]{:S(2)}, u32[]{:S(2)}) %all-to-all-start.3) | async-done | bytes 262176 | tf_op jit(solution)/shard_map/all_to_all | solution.py:542
  67.6 0.0 copy-start.4
  67.6 0.7 copy-done.4
  68.3 2.8 %shard_map.136 = (f32[8,80,128]{2,1,0:T(8,128)}, f32[64,128]{1,0:T(8,128)}) custom-call(f32[8,64,128]{2,1,0:T(8,128)} %copy-done.4, f32[64,128]{1,0:T(8,128)} %get-tuple-element.37.refs_6_.stat_ref, f32[64,32,128]{2,1,0:T(8,128)} %shard_map.135.moment_ref, f32[1,128]{1,0:T(1,128)} %bitcast.15), custom_call_target="tpu_custom_call" | custom-call | flops 1048576 | bytes 1704448 | tf_op jit(solution)/shard_map/pallas_call | solution.py:76
  71.1 3.8 %all-to-all-start.4 = ((f32[8,80,128]{2,1,0:T(8,128)}), f32[8,80,128]{2,1,0:T(8,128)S(1)}, u32[]{:S(2)}, u32[]{:S(2)}) async-start(f32[8,80,128]{2,1,0:T(8,128)} %get-tuple-element.42), calls=%async_computation.4 | async-start | bytes 655360 | tf_op jit(solution)/shard_map/all_to_all | solution.py:542
  74.9 4.4 %shard_map.137.refs_8_ = f32[64,128,128]{2,1,0:T(8,128)} custom-call(f32[64,128,128]{2,1,0:T(8,128)} %refs_0_.9, f32[64,16,128]{2,1,0:T(8,128)} %get-tuple-element.35.refs_4_.refs_1_, f32[64,16,128]{2,1,0:T(8,128)} %get-tuple-element.39.refs_2_, f32[32,16,128]{2,1,0:T(8,128)} %get-tuple-element.31.refs_5_.refs_3_, ...), custom_call_target="tpu_custom_call" | custom-call | flops 209715200 | bytes 9757184 | tf_op jit(solution)/shard_map/pallas_call | solution.py:76
  79.3 3.7 %all-to-all-done.4.recv_ref = f32[8,80,128]{2,1,0:T(8,128)S(1)} async-done(((f32[8,80,128]{2,1,0:T(8,128)}), f32[8,80,128]{2,1,0:T(8,128)S(1)}, u32[]{:S(2)}, u32[]{:S(2)}) %all-to-all-start.4) | async-done | bytes 327712 | tf_op jit(solution)/shard_map/all_to_all | solution.py:542
  83.0 0.0 copy-start
  83.0 0.7 shard_map.138
  83.7 7.1 %all-to-all-start.5 = ((f32[16,16,128]{2,1,0:T(8,128)}), f32[16,16,128]{2,1,0:T(8,128)S(1)}, u32[]{:S(2)}, u32[]{:S(2)}) async-start(f32[16,16,128]{2,1,0:T(8,128)} %shard_map.138), calls=%async_computation.5 | async-start | bytes 262144 | tf_op jit(solution)/shard_map/all_to_all | solution.py:542
  90.8 0.0 copy-done
  90.8 2.2 %shard_map.140 = f32[64,96]{1,0:T(8,128)} custom-call(f32[8,80,128]{2,1,0:T(8,128)} %copy-done, f32[64,768]{1,0:T(8,128)} %get-tuple-element.27.refs_1_.gate_ref, f32[96,768]{1,0:T(8,128)} %bitcast.6), custom_call_target="tpu_custom_call" | custom-call | flops 28311552 | bytes 843776 | tf_op jit(solution)/shard_map/pallas_call | solution.py:76
  93.1 4.4 %shard_map.139 = f32[64,128,128]{2,1,0:T(8,128)} custom-call(f32[64,128,128]{2,1,0:T(8,128)} %refs_0_.9, f32[64,16,128]{2,1,0:T(8,128)} %get-tuple-element.35.refs_4_.refs_1_, f32[64,16,128]{2,1,0:T(8,128)} %get-tuple-element.39.refs_2_, f32[32,16,128]{2,1,0:T(8,128)} %get-tuple-element.32.refs_6_.refs_3_, ...), custom_call_target="tpu_custom_call", output_to_operand_aliasing={{}: (8, {})} | custom-call | flops 209715200 | bytes 13951488 | tf_op jit(solution)/shard_map/pallas_call | solution.py:76
  97.5 0.0 all-to-all-done.5.recv_ref
  97.5 0.6 shard_map.141
Async XLA Ops:
  2.7 18.8 %all-to-all-start = ((f32[8,96,128]{2,1,0:T(8,128)}), f32[8,96,128]{2,1,0:T(8,128)S(1)}, u32[]{:S(2)}, u32[]{:S(2)}) async-start(f32[8,96,128]{2,1,0:T(8,128)} %shard_map.130), calls=%async_computation | async-start | bytes 786432 | tf_op jit(solution)/shard_map/all_to_all | solution.py:542
  10.9 8.0 %collective-permute-start = (f32[64,96]{1,0:T(8,128)}, f32[64,96]{1,0:T(8,128)S(1)}, u32[]{:S(2)}, u32[]{:S(2)}) collective-permute-start(f32[64,96]{1,0:T(8,128)} %single_ref.1), channel_id=1, source_target_pairs={{0,64},{1,32},{2,0},{3,96},{4,80},{5,48},{6,16},{7,112},{8,72},{9,... | collective-permute-start | bytes 73736 | tf_op jit(solution)/shard_map/ppermute | solution.py:569
  21.5 6.7 %copy-start.2 = (f32[8,96,128]{2,1,0:T(8,128)}, f32[8,96,128]{2,1,0:T(8,128)S(1)}, u32[]{:S(2)}) copy-start(f32[8,96,128]{2,1,0:T(8,128)S(1)} %all-to-all-done.refs_3_) | copy-start | bytes 1179652
  22.5 15.4 %all-to-all-start.2 = ((f32[16,64,96]{2,1,0:T(8,128)}), f32[16,64,96]{2,1,0:T(8,128)S(1)}, u32[]{:S(2)}, u32[]{:S(2)}) async-start(f32[16,64,96]{2,1,0:T(8,128)} %broadcast_in_dim.10), calls=%async_computation.2 | async-start | bytes 1048576 | tf_op jit(solution)/shard_map/all_to_all | solution.py:542
  37.9 4.6 %copy-start.1 = (f32[16,64,96]{2,1,0:T(8,128)}, f32[16,64,96]{2,1,0:T(8,128)S(1)}, u32[]{:S(2)}) copy-start(f32[16,64,96]{2,1,0:T(8,128)S(1)} %all-to-all-done.2.refs_0_) | copy-start | bytes 1179652
  37.9 12.4 %all-to-all-start.1 = ((f32[8,64,96]{2,1,0:T(8,128)}), f32[8,64,96]{2,1,0:T(8,128)S(1)}, u32[]{:S(2)}, u32[]{:S(2)}) async-start(f32[8,64,96]{2,1,0:T(8,128)} %get-tuple-element.26), calls=%async_computation.1 | async-start | bytes 524288 | tf_op jit(solution)/shard_map/all_to_all | solution.py:542
  50.3 0.7 copy-start.3
  54.3 13.2 %all-to-all-start.3 = ((f32[8,64,128]{2,1,0:T(8,128)}), f32[8,64,128]{2,1,0:T(8,128)S(1)}, u32[]{:S(2)}, u32[]{:S(2)}) async-start(f32[8,64,128]{2,1,0:T(8,128)} %get-tuple-element.38), calls=%async_computation.3 | async-start | bytes 524288 | tf_op jit(solution)/shard_map/all_to_all | solution.py:542
  67.6 0.7 copy-start.4
  71.1 11.9 %all-to-all-start.4 = ((f32[8,80,128]{2,1,0:T(8,128)}), f32[8,80,128]{2,1,0:T(8,128)S(1)}, u32[]{:S(2)}, u32[]{:S(2)}) async-start(f32[8,80,128]{2,1,0:T(8,128)} %get-tuple-element.42), calls=%async_computation.4 | async-start | bytes 655360 | tf_op jit(solution)/shard_map/all_to_all | solution.py:542
  83.0 7.9 %copy-start = (f32[8,80,128]{2,1,0:T(8,128)}, f32[8,80,128]{2,1,0:T(8,128)S(1)}, u32[]{:S(2)}) copy-start(f32[8,80,128]{2,1,0:T(8,128)S(1)} %all-to-all-done.4.recv_ref) | copy-start | bytes 983044
  83.7 13.8 %all-to-all-start.5 = ((f32[16,16,128]{2,1,0:T(8,128)}), f32[16,16,128]{2,1,0:T(8,128)S(1)}, u32[]{:S(2)}, u32[]{:S(2)}) async-start(f32[16,16,128]{2,1,0:T(8,128)} %shard_map.138), calls=%async_computation.5 | async-start | bytes 262144 | tf_op jit(solution)/shard_map/all_to_all | solution.py:542

commit v3 on v2

--- a/solution.py
+++ b/solution.py
@@ -17,6 +17,7 @@
 VMEM_BYTES = 60 * MIB
 PARTS = 4
 GROUP = 4
+LARGE = 48
 FAR = pl.BlockSpec(memory_space=pl.ANY)
 NEAR = pl.BlockSpec(memory_space=pltpu.VMEM)
 
@@ -185,26 +186,30 @@
     return out
 
 
+def back_kernel(recv_ref, back_ref):
+    rows, block = back_ref.shape
+    total = recv_ref[0]
+    for k in range(1, recv_ref.shape[0]):
+        total = total + recv_ref[k]
+    rest = total.shape[1] - block
+    right = jnp.concatenate([total[rows:, : block - rest], total[rows:, block - rest :]], axis=0)
+    total = jnp.concatenate([total[:rows, block:], right], axis=1)
+    back_ref[...] = total
+
+
 def query_kernel(
     pair_far, wb, pgain, recv, gain, wq_far, wg_far,
-    bias_far, rs_far, back_ref, query_ref, gate_ref,
+    bias_far, rs_far, query_ref, gate_ref,
     x_ref, bias_ref, rs_ref, sems, normed, wq, wg, qsem, gsem,
 ):
     take, give = bias_streams(pair_far, bias_far, rs_far, x_ref, bias_ref, rs_ref, sems, 1)
     query_copies = fetch(wq_far, wq, qsem)
     gate_copies = fetch(wg_far, wg, gsem)
-    n, rows, block = back_ref.shape
+    bias_rows(take, give, wb.ready(), pgain.ready(), x_ref, bias_ref, rs_ref)
     recv_ref = recv.ready()
-    total = recv_ref[0]
-    for k in range(1, n):
-        total = total + recv_ref[k]
-    rest = total.shape[1] - block
-    right = jnp.concatenate([total[rows:, : block - rest], total[rows:, block - rest :]], axis=0)
-    total = jnp.concatenate([total[:rows, block:], right], axis=1)
-    for k in range(n):
-        back_ref[k] = total
-    bias_rows(take, give, wb.ready(), pgain.ready(), x_ref, bias_ref, rs_ref)
-    joined_norm([recv_ref[k, :rows, :block] for k in range(n)], normed, 0)
+    n = recv_ref.shape[0]
+    rows, width = query_ref.shape
+    joined_norm([recv_ref[k, :rows, : width // n] for k in range(n)], normed, 0)
     both = gained(normed, gain.ready())
     query_ref[...] = project(both, wq, query_copies) * (48 ** -0.5)
     gate_ref[...] = 1.0 / (1.0 + jnp.exp(-project(both, wg, gate_copies)))
@@ -218,7 +223,7 @@
 
 def bias_streams(pair_far, bias_far, rs_far, x_ref, bias_ref, rs_ref, sems, part):
     parts = PARTS // 2
-    take = Stream(pair_far, x_ref, sems.at[0], parts, part * x_ref.shape[0])
+    take = Stream(pair_far, x_ref, sems.at[0], parts, part * LARGE)
     take.start()
     return take, [Stream(bias_ref, bias_far, sems.at[1], 1), Stream(rs_ref, rs_far, sems.at[2], 1)]
 
@@ -274,21 +279,32 @@
     return two[:, :keys] + two[:, keys:] + dg(rl, high, NT)
 
 
-def score_kernel(
-    recv, gain, wk_far, wv_far, query, bias_a, bias_b,
-    high_ref, low_ref, expo_ref, acc_ref, stat_ref,
-    normed, wk, wv, ksem, vsem,
+def attend_kernel(
+    own, far_a, far_b, far_c, gain, wk_far, wv_far, query, bias_a, bias_b, back_four, back_far, gate,
+    pay_ref, expo_ref, dprobs_ref, stat_ref,
+    normed, wk, wv, dctx, acc, ksem, vsem,
 ):
     key_copies = fetch(wk_far, wk, ksem)
     value_copies = fetch(wv_far, wv, vsem)
-    recv_ref = recv.ready()
-    n_row, rows, block = recv_ref.shape
+    blocks = [piece.ready() for piece in (own, far_a, far_b, far_c)]
+    n_sub, rows, block = blocks[0].shape
     queries, heads, keys = expo_ref.shape
     width = normed.shape[1]
     n_col = width // block
+    me = lax.axis_index("row")
     col = lax.axis_index("col")
-    for t in range(n_row // n_col):
-        joined_norm([recv_ref[place(k, col, t)] for k in range(n_col)], normed, t * rows)
+
+    def token_block(k, core):
+        there = place(k, col, core)
+        hop = (me // n_sub + 4 - there // n_sub) % 4
+        spot = (me % n_sub) ^ (there % n_sub)
+        some = [piece[spot] for piece in blocks]
+        return jnp.where(
+            hop < 2, jnp.where(hop == 0, some[0], some[1]), jnp.where(hop == 2, some[2], some[3])
+        )
+
+    for t in range(keys // rows):
+        joined_norm([token_block(k, t) for k in range(n_col)], normed, t * rows)
     both = gained(normed, gain.ready())
     kh, kl = split(project(both, wk, key_copies))
     half = heads // 2
@@ -308,49 +324,34 @@
         top = jnp.max(scores, axis=-1, keepdims=True)
         expo = jnp.exp(scores - top)
         total = jnp.sum(expo, axis=-1, keepdims=True)
-        inv = 1.0 / total
         expo_ref[:, some] = expo.reshape(queries, half, keys)
-        for place_, column in enumerate((top + jnp.log(total), top, inv)):
-            first = place_ * heads + some.start
-            stat_ref[:, first : first + half] = lanes(column)
-        parts.append(split(expo * inv))
+        stat_ref[:, some] = lanes(top)
+        lse = lanes(top + jnp.log(total))
+        for k in range(n_col):
+            pay_ref[k, :, block + some.start : block + some.stop] = lse
+        parts.append(expo * (1.0 / total))
     vh, vl = split(project(both, wv, value_copies))
-    high_ref[...] = vh
-    low_ref[...] = vl
-    for (some, part), (eh, el) in zip(halves(heads, width), parts):
-        high = vh[:, part]
-        wide = dg(jnp.concatenate([eh, el], axis=1), jnp.concatenate([high, high], axis=0), NN)
-        wide = wide + dg(eh, vl[:, part], NN)
-        wide = jnp.where(mask, wide.reshape(queries, half, width // 2), 0.0)
-        acc_ref[:, part] = jnp.sum(wide, axis=1)
-
-
-def delta_kernel(
-    back, gate, high, low, expo, acc, stat, pay_ref, dprobs_ref, dctx
-):
-    back_ref, gate_ref, acc_ref, stat_ref = [v.ready() for v in (back, gate, acc, stat)]
-    high_ref, low_ref, expo_ref = [v.ready() for v in (high, low, expo)]
-    n_col, _, block = back_ref.shape
-    queries, heads, keys = expo_ref.shape
-    width = dctx.shape[1]
+    backs, gate_ref = [back_four.ready(), back_far.ready()], gate.ready()
+    n_x = backs[0].shape[0]
     for k in range(n_col):
         part = slice(k * block, (k + 1) * block)
-        dctx[:, part] = back_ref[k] * gate_ref[:, part]
-        pay_ref[k, :, :block] = acc_ref[:, part]
-        pay_ref[k, :, block : block + heads] = stat_ref[:, :heads]
-    half = heads // 2
-    mask = head_mask(half, width // 2)[None]
-    eye = eye_mask(half)[None]
-    for some, part in halves(heads, width):
-        dp = against(dctx[:, part], mask, high_ref[:, part], low_ref[:, part])
-        dp = dp.reshape(queries, half, keys)
-        dprobs_ref[:, some] = dp
-        delta = jnp.sum(expo_ref[:, some] * dp, axis=-1, keepdims=True)
-        first = 2 * heads + some.start
-        delta = jnp.sum(jnp.where(eye, delta, 0.0), axis=1) * stat_ref[:, first : first + half]
-        first = block + heads + some.start
+        spot = (col + n_x - k) % n_x
+        near = col // n_x == k // n_x
+        dctx[:, part] = jnp.where(near, backs[0][spot], backs[1][spot]) * gate_ref[:, part]
+    for (some, part), probs in zip(halves(heads, width), parts):
+        high, low = vh[:, part], vl[:, part]
+        eh, el = split(probs)
+        wide = dg(jnp.concatenate([eh, el], axis=1), jnp.concatenate([high, high], axis=0), NN)
+        wide = wide + dg(eh, low, NN)
+        wide = jnp.where(mask, wide.reshape(queries, half, width // 2), 0.0)
+        acc[:, part] = jnp.sum(wide, axis=1)
+        dp = against(dctx[:, part], mask, high, low)
+        dprobs_ref[:, some] = dp.reshape(queries, half, keys)
+        delta = lanes(jnp.sum(probs * dp, axis=-1, keepdims=True))
         for k in range(n_col):
-            pay_ref[k, :, first : first + half] = delta
+            pay_ref[k, :, block + heads + some.start : block + heads + some.stop] = delta
+    for k in range(n_col):
+        pay_ref[k, :, :block] = acc[:, k * block : (k + 1) * block]
 
 
 def moment_kernel(
@@ -363,12 +364,12 @@
         Stream(expo_far, expo_ref, sems.at[1], 1),
         Stream(dprobs_far, dprobs_ref, sems.at[2], 1),
     ]
-    give = Stream(out_ref, out_far, sems.at[3], 2)
+    give = Stream(out_ref, out_far, sems.at[3])
     for t in reversed(take):
         t.start()
     for t in take[1:]:
         t.wait()
-    half = expo_ref.shape[0] // 2
+    cut = PARTS * LARGE // expo_ref.shape[0]
 
     def step(rs_ref, shift, k, carry):
         take[0].copy(k).wait()
@@ -382,10 +383,12 @@
             out_ref[i] = high[:, :chans] + high[:, chans:] + wide[2 * heads :, :chans]
         return carry
 
-    lax.fori_loop(0, PARTS // 2, functools.partial(step, rs_a.ready(), 0), 0)
-    give.copy(0).start()
-    lax.fori_loop(PARTS // 2, PARTS, functools.partial(step, rs_b.ready(), half), 0)
-    give.copy(1).start()
+    lax.fori_loop(0, cut, functools.partial(step, rs_a.ready(), 0), 0)
+    for k in range(cut):
+        give.copy(k).start()
+    lax.fori_loop(cut, PARTS, functools.partial(step, rs_b.ready(), LARGE), 0)
+    for k in range(cut, PARTS):
+        give.copy(k).start()
     give.wait()
 
 
@@ -404,7 +407,7 @@
     inv = 1.0 / total
     weight = [w * inv for w in weight]
     delta = sum(w * recv_ref[k, :, block + heads :] for k, w in enumerate(weight))
-    fac = jnp.exp(stat_ref[:, heads : 2 * heads] - (top + jnp.log(total)))
+    fac = jnp.exp(stat_ref[:, :heads] - (top + jnp.log(total)))
     join_ref[:, :heads] = fac
     join_ref[:, heads : 2 * heads] = delta
     context = sum(
@@ -430,7 +433,7 @@
 ):
     out_far, x_ref, expo_ref, dprobs_ref, bias_ref, fac_ref, dlt_ref, out_ref, sems = refs[-9:]
     count, keys = out_ref.shape[:2]
-    shift = part * count
+    shift = part * LARGE
     parts = PARTS // 2
     take = [
         Stream(x_far, x_ref, sems.at[0], parts, shift),
@@ -575,59 +578,70 @@
     )
     recv1 = swap(pay1, "col")
     shape_x = sds(queries, keys, chans)
-    half_e = sds(queries // 2, heads, keys)
-    half_rs = sds(queries // 2, keys)
-    half_x = sds(queries // 2, keys, chans)
-    held = [mem(half_x), mem(half_e), mem(half_rs), dma((3, PARTS // 2))]
+    counts = (LARGE, queries - LARGE)
+    parts_e = [sds(n, heads, keys) for n in counts]
+    parts_rs = [sds(n, keys) for n in counts]
+    parts_x = [sds(n, keys, chans) for n in counts]
+    held = [
+        [mem(x), mem(e), mem(rs), dma((3, PARTS // 2))]
+        for x, e, rs in zip(parts_x, parts_e, parts_rs)
+    ]
     bias_a, rs_a = call(
         pair_kernel,
-        (half_e, half_rs),
+        (parts_e[0], parts_rs[0]),
         queries * keys * chans * 200,
         (pair, wb, pgain),
-        held,
+        held[0],
         (0, 1, 1),
         (1, 1),
     )
     moved, rs_a = lax.optimization_barrier((moved, rs_a))
-    recv2 = swap(jnp.broadcast_to(moved[None], (n_row,) + moved.shape), "row")
+
+    def along(x, target):
+        return lax.ppermute(x, "row", [(r, target(r)) for r in range(n_row)])
+
+    pair_of = jnp.stack([moved, along(moved, lambda r: r ^ 1)])
+    back_pay = call(back_kernel, sds(queries, block), queries * width, (recv1,), vmem=4 * MIB)
+    four = jnp.concatenate([pair_of, along(pair_of, lambda r: r ^ 2)])
+    n_x = 4
+
+    def around(x, k):
+        return lax.ppermute(x, "col", [(c, c - c % n_x + (c + k) % n_x) for c in range(n_col)])
+
+    back_four = jnp.stack([back_pay] + [around(back_pay, k) for k in range(1, n_x)])
+    back_far = lax.ppermute(back_four, "col", [(c, (c + n_x) % n_col) for c in range(n_col)])
+    ring = [along(four, lambda r: (r + 4 * k) % n_row) for k in range(1, 4)]
+    recv1, four = lax.optimization_barrier((recv1, four))
     square = pltpu.VMEM((width, width), F32)
-    bias_b, rs_b, back_pay, query, gate = call(
+    bias_b, rs_b, query, gate = call(
         query_kernel,
         (
-            half_e,
-            half_rs,
-            sds(n_col, queries, block),
+            parts_e[1],
+            parts_rs[1],
             sds(queries, width),
             sds(queries, width),
         ),
         queries * keys * chans * 200 + queries * width * width * 12,
         (pair, wb, pgain, recv1, gain, w_query, w_gate),
-        held + [pltpu.VMEM((queries, width), F32), square, square, dma((3,)), dma((3,))],
+        held[1] + [pltpu.VMEM((queries, width), F32), square, square, dma((3,)), dma((3,))],
         (0, 1, 1, 1, 1, 0, 0),
-        (1, 1, 0, 0, 0),
-    )
-    back = swap(back_pay, "col")
-    vhigh, vlow, expo, acc, stat = call(
-        score_kernel,
-        (
-            sds(keys, width, dtype=BF16),
-            sds(keys, width, dtype=BF16),
-            shape_e,
-            sds(queries, width),
-            sds(queries, chans),
-        ),
+        (1, 1, 0, 0),
+    )
+    pay4, expo, dprobs, stat = call(
+        attend_kernel,
+        (sds(n_col, queries, chans), shape_e, shape_e, sds(queries, chans)),
         keys * width * width * 12,
-        (recv2, gain, w_key, w_value, query, bias_a, bias_b),
-        [pltpu.VMEM((keys, width), F32), square, square, dma((3,)), dma((3,))],
-        (1, 1, 0, 0, 1, 1, 1),
-    )
-    pay4, dprobs = call(
-        delta_kernel,
-        (sds(n_col, queries, chans), shape_e),
-        queries * keys * width * 12,
-        (back, gate, vhigh, vlow, expo, acc, stat),
-        [pltpu.VMEM((queries, width), F32)],
-        (1,) * 7,
+        (four, *ring, gain, w_key, w_value, query, bias_a, bias_b, back_four, back_far, gate),
+        [
+            pltpu.VMEM((keys, width), F32),
+            square,
+            square,
+            pltpu.VMEM((queries, width), F32),
+            pltpu.VMEM((queries, width), F32),
+            dma((3,)),
+            dma((3,)),
+        ],
+        (1, 1, 1, 1, 1, 0, 0, 1, 1, 1, 1, 1, 1),
     )
     recv4 = swap(pay4, "col")
     shape_m = sds(queries, 2 * heads, chans)
@@ -648,14 +662,16 @@
     )
     recv5 = swap(pay5, "col")
     cost = queries * keys * chans * 200
-    held = [mem(half_x)] + 5 * [mem(half_e)] + [mem(half_x), dma((5, PARTS // 2))]
+    held = [
+        [mem(x)] + 5 * [mem(e)] + [mem(x), dma((5, PARTS // 2))] for x, e in zip(parts_x, parts_e)
+    ]
     place_of = (0, 0, 0, 0, 1, 1, 1, 1)
     first = call(
         functools.partial(grad_kernel, 0),
         shape_x,
         cost,
         (pair, expo, dprobs, bias_a, rs_a, joined, wb, pgain),
-        held,
+        held[0],
         place_of,
         (1,),
     )
@@ -669,7 +685,7 @@
         shape_x,
         cost,
         (pair, expo, dprobs, bias_b, rs_b, joined, wb, pgain, first),
-        held,
+        held[1],
         place_of + (0,),
         (1,),
         {8: 0},

time: 99 us -> 91.9 us (0.928)
  waiting for transfers between devices: 15.1 us -> 7.82 us
  starting transfers between devices: 37.9 us -> 41 us
  Pallas kernels: 42.1 us -> 40.3 us
    ppermute x0 -> x9, starting transfers between devices: none -> 13.4 us  [the longest x5 7.65 us: along(): return lax.ppermute(x, 'row', [(r, target(r)) for r in range(n_row)])]
    all_to_all x6 -> x4, starting transfers between devices: 35 us -> 24.7 us  [swap(): return lax.all_to_all(x, axis, 0, 0, tiled=True)]
    all_to_all x6 -> x4, waiting for transfers between devices: 13.6 us -> 5.84 us  [swap(): return lax.all_to_all(x, axis, 0, 0, tiled=True)]
    pallas_call x12, Pallas kernels: 42.1 us -> 40.3 us  [call(): pl.pallas_call(body, out_shape=out_shape, scratch_shapes=scratch, compile...]
    ppermute x0 -> x9, waiting for transfers between devices: none -> 1.25 us  [the longest x5 0.87 us: along(): return lax.ppermute(x, 'row', [(r, target(r)) for r in range(n_row)])]
  transfers between devices with their start and end apart: 7 -> 14, of which waited for: 6 -> 6; matrix products, arithmetic and copies ran while one was open for 0% -> 0% of each run, Pallas kernels for 33% -> 29%
where the time goes in v3:
time: 91.9 us; the launch traced here: 91.4 us
  starting transfers between devices  41 us (45%)
  Pallas kernels  40.3 us (44%)
  waiting for transfers between devices  7.82 us (9%)
  local copies, waits for them, and re-layouts  1.42 us (2%)
    pallas_call x12, Pallas kernels, call(): pl.pallas_call(body, out_shape=out_shape, scratch_shapes=scratch, compile...  40.3 us
    all_to_all x4, starting transfers between devices, swap(): return lax.all_to_all(x, axis, 0, 0, tiled=True)  24.7 us
    ppermute x5, starting transfers between devices, along(): return lax.ppermute(x, 'row', [(r, target(r)) for r in range(n_row)])  7.65 us
    all_to_all x4, waiting for transfers between devices, swap(): return lax.all_to_all(x, axis, 0, 0, tiled=True)  5.84 us
    ppermute x1, starting transfers between devices, local(): lax.ppermute(back_four, 'col', [(c, (c + n_x) % n_col) for c in range(n_c...  3.3 us
    ppermute x1, starting transfers between devices, local(): moved = lax.ppermute(single, ('row', 'col'), perm)  2.91 us
    ppermute x3, starting transfers between devices, around(): lax.ppermute(x, 'col', [(c, c - c % n_x + (c + k) % n_x) for c in range(n...  2.47 us
  transfers between devices with their start and end apart: 14, of which 6 were waited for; matrix products, arithmetic and copies ran while one was open for 0% of the time, Pallas kernels for 29%

profile of v3, /device:TPU:1, one launch (start us, length us, event | category | flops | bytes accessed | tf_op | source)
XLA Modules:
  0.0 91.4 jit_solution(15271900714951226421)
XLA Ops:
  0.6 2.1 %shard_map.130 = f32[8,96,128]{2,1,0:T(8,128)} custom-call(f32[64,96]{1,0:T(8,128)} %single_ref.1, f32[64,96]{1,0:T(8,128)} %cot_ref.1, f32[96,768]{1,0:T(8,128)} %bitcast.12), custom_call_target="tpu_custom_call" | custom-call | flops 28311552 | bytes 737280 | tf_op jit(solution)/shard_map/pallas_call | solution.py:77
  2.7 8.2 %all-to-all-start = ((f32[8,96,128]{2,1,0:T(8,128)}), f32[8,96,128]{2,1,0:T(8,128)S(1)}, u32[]{:S(2)}, u32[]{:S(2)}) async-start(f32[8,96,128]{2,1,0:T(8,128)} %shard_map.130), calls=%async_computation | async-start | bytes 786432 | tf_op jit(solution)/shard_map/all_to_all | solution.py:545
  10.9 2.9 %collective-permute-start = (f32[64,96]{1,0:T(8,128)}, f32[64,96]{1,0:T(8,128)S(1)}, u32[]{:S(2)}, u32[]{:S(2)}) collective-permute-start(f32[64,96]{1,0:T(8,128)} %single_ref.1), channel_id=1, source_target_pairs={{0,64},{1,32},{2,0},{3,96},{4,80},{5,48},{6,16},{7,112},{8,72},{9,... | collective-permute-start | bytes 73736 | tf_op jit(solution)/shard_map/ppermute | solution.py:572
  13.8 4.3 %shard_map.131 = (f32[48,16,128]{2,1,0:T(8,128)}, f32[48,128]{1,0:T(8,128)}) custom-call(f32[64,128,128]{2,1,0:T(8,128)} %refs_0_.9, f32[16,128]{1,0:T(8,128)} %bitcast.18, f32[1,128]{1,0:T(1,128)} %bitcast.27), custom_call_target="tpu_custom_call" | custom-call | flops 209715200 | bytes 4620800 | tf_op jit(solution)/shard_map/pallas_call | solution.py:77
  18.1 0.7 collective-permute-done
  18.9 1.9 %collective-permute-start.1 = (f32[64,96]{1,0:T(8,128)S(1)}, f32[64,96]{1,0:T(8,128)S(1)}, u32[]{:S(2)}, u32[]{:S(2)}) collective-permute-start(f32[64,96]{1,0:T(8,128)S(1)} %collective-permute-done), channel_id=1, source_target_pairs={{0,8},{8,0},{16,24},{24,16},{32,40},{40,32},{48,56},{56,48},{64,72... | collective-permute-start | bytes 73736 | tf_op jit(solution)/shard_map/ppermute | solution.py:601
  20.8 0.9 collective-permute-done.1
  21.6 2.4 %collective-permute-start.2 = (f32[2,64,96]{2,1,0:T(8,128)S(1)}, f32[2,64,96]{2,1,0:T(8,128)S(1)}, u32[]{:S(2)}, u32[]{:S(2)}) collective-permute-start(f32[2,64,96]{2,1,0:T(8,128)S(1)} %pad_maximum_fusion.2), channel_id=1, source_target_pairs={{0,16},{8,24},{16,0},{24,8},{32,48},{40,56},{48,32},{56,40},{64,80... | collective-permute-start | bytes 147464 | tf_op jit(solution)/shard_map/ppermute | solution.py:601
  24.1 0.0 all-to-all-done.refs_3_.recv_ref
  24.1 0.1 shard_map.133
  24.2 1.5 %collective-permute-start.8 = (f32[64,96]{1,0:T(8,128)S(1)}, f32[64,96]{1,0:T(8,128)S(1)}, u32[]{:S(2)}, u32[]{:S(2)}) collective-permute-start(f32[64,96]{1,0:T(8,128)S(1)} %shard_map.133), channel_id=1, source_target_pairs={{0,3},{1,0},{2,1},{3,2},{4,7},{5,4},{6,5},{7,6},{8,11},{9,8},{10,9... | collective-permute-start | bytes 73736 | tf_op jit(solution)/shard_map/ppermute | solution.py:609
  25.7 0.7 collective-permute-start.7
  26.4 0.3 collective-permute-start.6
  26.7 0.0 collective-permute-done.2
  26.7 2.5 %collective-permute-start.5 = (f32[4,64,96]{2,1,0:T(8,128)S(1)}, f32[4,64,96]{2,1,0:T(8,128)S(1)}, u32[]{:S(2)}, u32[]{:S(2)}) collective-permute-start(f32[4,64,96]{2,1,0:T(8,128)S(1)} %pad_maximum_fusion.refs_0_), channel_id=1, source_target_pairs={{0,96},{8,104},{16,112},{24,120},{32,0},{40,8},{48,16},{56,24},{64... | collective-permute-start | bytes 294920 | tf_op jit(solution)/shard_map/ppermute | solution.py:601
  29.2 0.4 collective-permute-start.4
  29.6 0.0 collective-permute-done.8
  29.6 0.4 collective-permute-start.3
  30.0 0.0 collective-permute-done.7
  30.0 0.4 collective-permute-done.6
  30.4 3.3 %collective-permute-start.9 = (f32[4,64,96]{2,1,0:T(8,128)S(1)}, f32[4,64,96]{2,1,0:T(8,128)S(1)}, u32[]{:S(2)}, u32[]{:S(2)}) collective-permute-start(f32[4,64,96]{2,1,0:T(8,128)S(1)} %pad_maximum_fusion.1.refs_10_), channel_id=1, source_target_pairs={{0,4},{1,5},{2,6},{3,7},{4,0},{5,1},{6,2},{7,3},{8,12},{9,13},{10,... | collective-permute-start | bytes 294920 | tf_op jit(solution)/shard_map/ppermute | solution.py:612
  33.7 5.8 %shard_map.132 = (f32[16,16,128]{2,1,0:T(8,128)}, f32[16,128]{1,0:T(8,128)}, f32[64,768]{1,0:T(8,128)}, f32[64,768]{1,0:T(8,128)}) custom-call(f32[64,128,128]{2,1,0:T(8,128)} %refs_0_.9, f32[16,128]{1,0:T(8,128)} %bitcast.19, f32[1,128]{1,0:T(1,128)} %bitcast.28, f32[8,96,128]{2,1,0:T(8,128)} %copy-done, f32[6,128]{1,0:T(8,128)} %bitcast.25, ...), custom_call_target="tpu_custom_call" | custom-call | flops 662700032 | bytes 9850368 | tf_op jit(solution)/shard_map/pallas_call | solution.py:77
  39.5 0.0 collective-permute-done.5.refs_3_
  39.5 0.0 collective-permute-done.4.refs_2_
  39.6 0.0 copy-start.6
  39.6 0.0 collective-permute-done.3.refs_1_
  39.6 0.0 copy-start.7
  39.6 0.0 collective-permute-done.9.refs_11_
  39.6 0.0 copy-start.8
  39.6 0.6 copy-done.5
  40.2 0.1 copy-done.6
  40.2 0.0 copy-done.7
  40.3 0.0 copy-done.8
  40.3 7.9 %shard_map.134 = (f32[8,64,128]{2,1,0:T(8,128)}, f32[64,16,128]{2,1,0:T(8,128)}, f32[64,16,128]{2,1,0:T(8,128)}, f32[64,128]{1,0:T(8,128)}) custom-call(f32[4,64,96]{2,1,0:T(8,128)} %copy-done.3, f32[4,64,96]{2,1,0:T(8,128)} %copy-done.7, f32[4,64,96]{2,1,0:T(8,128)} %copy-done.6, f32[4,64,96]{2,1,0:T(8,128)} %copy-done.5, f32[6,128]{1,0:T(8,128)} %bitcast.26, ...), custom_call_target="tpu_custom_call" | custom-call | flops 905969664 | bytes 7572480 | tf_op jit(solution)/shard_map/pallas_call | solution.py:77
  48.2 4.0 %all-to-all-start.1 = ((f32[8,64,128]{2,1,0:T(8,128)}), f32[8,64,128]{2,1,0:T(8,128)S(1)}, u32[]{:S(2)}, u32[]{:S(2)}) async-start(f32[8,64,128]{2,1,0:T(8,128)} %get-tuple-element.32), calls=%async_computation.1 | async-start | bytes 524288 | tf_op jit(solution)/shard_map/all_to_all | solution.py:545
  52.2 4.9 %shard_map.135.moment_ref = f32[64,32,128]{2,1,0:T(8,128)} custom-call(f32[64,128,128]{2,1,0:T(8,128)} %refs_0_.9, f32[64,16,128]{2,1,0:T(8,128)} %get-tuple-element.34.refs_1_, f32[64,16,128]{2,1,0:T(8,128)} %get-tuple-element.35.refs_2_, f32[48,128]{1,0:T(8,128)} %get-tuple-element.36.refs_3_.refs_4_, f32[16,128]{1,0:T(8,128)} %get-tuple-element.37.refs_4_), custom_call_target="tpu_custom_call" | custom-call | flops 201326592 | bytes 6324224 | tf_op jit(solution)/shard_map/pallas_call | solution.py:77
  57.1 2.7 %all-to-all-done.1.recv_ref = f32[8,64,128]{2,1,0:T(8,128)S(1)} async-done(((f32[8,64,128]{2,1,0:T(8,128)}), f32[8,64,128]{2,1,0:T(8,128)S(1)}, u32[]{:S(2)}, u32[]{:S(2)}) %all-to-all-start.1) | async-done | bytes 262176 | tf_op jit(solution)/shard_map/all_to_all | solution.py:545
  59.8 0.7 copy-done.2
  60.5 2.8 %shard_map.136 = (f32[8,80,128]{2,1,0:T(8,128)}, f32[64,128]{1,0:T(8,128)}) custom-call(f32[8,64,128]{2,1,0:T(8,128)} %copy-done.2, f32[64,128]{1,0:T(8,128)} %get-tuple-element.33.stat_ref, f32[64,32,128]{2,1,0:T(8,128)} %shard_map.135.moment_ref, f32[1,128]{1,0:T(1,128)} %bitcast.29), custom_call_target="tpu_custom_call" | custom-call | flops 1048576 | bytes 1704448 | tf_op jit(solution)/shard_map/pallas_call | solution.py:77
  63.3 3.9 %all-to-all-start.2 = ((f32[8,80,128]{2,1,0:T(8,128)}), f32[8,80,128]{2,1,0:T(8,128)S(1)}, u32[]{:S(2)}, u32[]{:S(2)}) async-start(f32[8,80,128]{2,1,0:T(8,128)} %get-tuple-element.38), calls=%async_computation.2 | async-start | bytes 655360 | tf_op jit(solution)/shard_map/all_to_all | solution.py:545
  67.2 5.5 %shard_map.137.refs_8_ = f32[64,128,128]{2,1,0:T(8,128)} custom-call(f32[64,128,128]{2,1,0:T(8,128)} %refs_0_.9, f32[64,16,128]{2,1,0:T(8,128)} %get-tuple-element.34.refs_1_, f32[64,16,128]{2,1,0:T(8,128)} %get-tuple-element.35.refs_2_, f32[48,16,128]{2,1,0:T(8,128)} %get-tuple-element.29.refs_8_.refs_3_, f32[48,128]{1,0:T(8,128)} %get-tuple-element.36.refs_3_.refs_4_, ...), custom_call_target="tpu_custom_call" | custom-call | flops 209715200 | bytes 9896448 | tf_op jit(solution)/shard_map/pallas_call | solution.py:77
  72.7 2.6 %all-to-all-done.2.recv_ref = f32[8,80,128]{2,1,0:T(8,128)S(1)} async-done(((f32[8,80,128]{2,1,0:T(8,128)}), f32[8,80,128]{2,1,0:T(8,128)S(1)}, u32[]{:S(2)}, u32[]{:S(2)}) %all-to-all-start.2) | async-done | bytes 327712 | tf_op jit(solution)/shard_map/all_to_all | solution.py:545
  75.2 0.7 shard_map.138
  76.0 8.6 %all-to-all-start.3 = ((f32[16,16,128]{2,1,0:T(8,128)}), f32[16,16,128]{2,1,0:T(8,128)S(1)}, u32[]{:S(2)}, u32[]{:S(2)}) async-start(f32[16,16,128]{2,1,0:T(8,128)} %shard_map.138), calls=%async_computation.3 | async-start | bytes 262144 | tf_op jit(solution)/shard_map/all_to_all | solution.py:545
  84.6 2.2 %shard_map.140 = f32[64,96]{1,0:T(8,128)} custom-call(f32[8,80,128]{2,1,0:T(8,128)} %copy-done.1, f32[64,768]{1,0:T(8,128)} %get-tuple-element.31.refs_12_.gate_ref, f32[96,768]{1,0:T(8,128)} %bitcast.13), custom_call_target="tpu_custom_call" | custom-call | flops 28311552 | bytes 843776 | tf_op jit(solution)/shard_map/pallas_call | solution.py:77
  86.8 3.4 %shard_map.139 = f32[64,128,128]{2,1,0:T(8,128)} custom-call(f32[64,128,128]{2,1,0:T(8,128)} %refs_0_.9, f32[64,16,128]{2,1,0:T(8,128)} %get-tuple-element.34.refs_1_, f32[64,16,128]{2,1,0:T(8,128)} %get-tuple-element.35.refs_2_, f32[16,16,128]{2,1,0:T(8,128)} %get-tuple-element.30.refs_9_.refs_3_, ...), custom_call_target="tpu_custom_call", output_to_operand_aliasing={{}: (8, {})} | custom-call | flops 209715200 | bytes 13812224 | tf_op jit(solution)/shard_map/pallas_call | solution.py:77
  90.2 0.5 all-to-all-done.3.recv_ref
  90.8 0.6 shard_map.141
  (13 shorter events, 0.1 us)
Async XLA Ops:
  2.7 21.3 %all-to-all-start = ((f32[8,96,128]{2,1,0:T(8,128)}), f32[8,96,128]{2,1,0:T(8,128)S(1)}, u32[]{:S(2)}, u32[]{:S(2)}) async-start(f32[8,96,128]{2,1,0:T(8,128)} %shard_map.130), calls=%async_computation | async-start | bytes 786432 | tf_op jit(solution)/shard_map/all_to_all | solution.py:545
  10.9 8.0 %collective-permute-start = (f32[64,96]{1,0:T(8,128)}, f32[64,96]{1,0:T(8,128)S(1)}, u32[]{:S(2)}, u32[]{:S(2)}) collective-permute-start(f32[64,96]{1,0:T(8,128)} %single_ref.1), channel_id=1, source_target_pairs={{0,64},{1,32},{2,0},{3,96},{4,80},{5,48},{6,16},{7,112},{8,72},{9,... | collective-permute-start | bytes 73736 | tf_op jit(solution)/shard_map/ppermute | solution.py:572
  18.9 2.8 %collective-permute-start.1 = (f32[64,96]{1,0:T(8,128)S(1)}, f32[64,96]{1,0:T(8,128)S(1)}, u32[]{:S(2)}, u32[]{:S(2)}) collective-permute-start(f32[64,96]{1,0:T(8,128)S(1)} %collective-permute-done), channel_id=1, source_target_pairs={{0,8},{8,0},{16,24},{24,16},{32,40},{40,32},{48,56},{56,48},{64,72... | collective-permute-start | bytes 73736 | tf_op jit(solution)/shard_map/ppermute | solution.py:601
  21.6 5.1 %collective-permute-start.2 = (f32[2,64,96]{2,1,0:T(8,128)S(1)}, f32[2,64,96]{2,1,0:T(8,128)S(1)}, u32[]{:S(2)}, u32[]{:S(2)}) collective-permute-start(f32[2,64,96]{2,1,0:T(8,128)S(1)} %pad_maximum_fusion.2), channel_id=1, source_target_pairs={{0,16},{8,24},{16,0},{24,8},{32,48},{40,56},{48,32},{56,40},{64,80... | collective-permute-start | bytes 147464 | tf_op jit(solution)/shard_map/ppermute | solution.py:601
  24.1 9.7 %copy-start = (f32[8,96,128]{2,1,0:T(8,128)}, f32[8,96,128]{2,1,0:T(8,128)S(1)}, u32[]{:S(2)}) copy-start(f32[8,96,128]{2,1,0:T(8,128)S(1)} %all-to-all-done.refs_3_.recv_ref) | copy-start | bytes 1179652
  24.2 5.4 %collective-permute-start.8 = (f32[64,96]{1,0:T(8,128)S(1)}, f32[64,96]{1,0:T(8,128)S(1)}, u32[]{:S(2)}, u32[]{:S(2)}) collective-permute-start(f32[64,96]{1,0:T(8,128)S(1)} %shard_map.133), channel_id=1, source_target_pairs={{0,3},{1,0},{2,1},{3,2},{4,7},{5,4},{6,5},{7,6},{8,11},{9,8},{10,9... | collective-permute-start | bytes 73736 | tf_op jit(solution)/shard_map/ppermute | solution.py:609
  25.7 4.3 %collective-permute-start.7 = (f32[64,96]{1,0:T(8,128)S(1)}, f32[64,96]{1,0:T(8,128)S(1)}, u32[]{:S(2)}, u32[]{:S(2)}) collective-permute-start(f32[64,96]{1,0:T(8,128)S(1)} %shard_map.133), channel_id=1, source_target_pairs={{0,2},{1,3},{2,0},{3,1},{4,6},{5,7},{6,4},{7,5},{8,10},{9,11},{10,... | collective-permute-start | bytes 73736 | tf_op jit(solution)/shard_map/ppermute | solution.py:609
  26.4 4.0 %collective-permute-start.6 = (f32[64,96]{1,0:T(8,128)S(1)}, f32[64,96]{1,0:T(8,128)S(1)}, u32[]{:S(2)}, u32[]{:S(2)}) collective-permute-start(f32[64,96]{1,0:T(8,128)S(1)} %shard_map.133), channel_id=1, source_target_pairs={{0,1},{1,2},{2,3},{3,0},{4,5},{5,6},{6,7},{7,4},{8,9},{9,10},{10,1... | collective-permute-start | bytes 73736 | tf_op jit(solution)/shard_map/ppermute | solution.py:609
  26.7 12.8 %copy-start.3 = (f32[4,64,96]{2,1,0:T(8,128)}, f32[4,64,96]{2,1,0:T(8,128)S(1)}, u32[]{:S(2)}) copy-start(f32[4,64,96]{2,1,0:T(8,128)S(1)} %pad_maximum_fusion.refs_0_) | copy-start | bytes 294916
  26.7 12.8 %collective-permute-start.5 = (f32[4,64,96]{2,1,0:T(8,128)S(1)}, f32[4,64,96]{2,1,0:T(8,128)S(1)}, u32[]{:S(2)}, u32[]{:S(2)}) collective-permute-start(f32[4,64,96]{2,1,0:T(8,128)S(1)} %pad_maximum_fusion.refs_0_), channel_id=1, source_target_pairs={{0,96},{8,104},{16,112},{24,120},{32,0},{40,8},{48,16},{56,24},{64... | collective-permute-start | bytes 294920 | tf_op jit(solution)/shard_map/ppermute | solution.py:601
  29.2 10.3 %collective-permute-start.4 = (f32[4,64,96]{2,1,0:T(8,128)S(1)}, f32[4,64,96]{2,1,0:T(8,128)S(1)}, u32[]{:S(2)}, u32[]{:S(2)}) collective-permute-start(f32[4,64,96]{2,1,0:T(8,128)S(1)} %pad_maximum_fusion.refs_0_), channel_id=1, source_target_pairs={{0,64},{8,72},{16,80},{24,88},{32,96},{40,104},{48,112},{56,120},{... | collective-permute-start | bytes 294920 | tf_op jit(solution)/shard_map/ppermute | solution.py:601
  29.6 10.0 %collective-permute-start.3 = (f32[4,64,96]{2,1,0:T(8,128)S(1)}, f32[4,64,96]{2,1,0:T(8,128)S(1)}, u32[]{:S(2)}, u32[]{:S(2)}) collective-permute-start(f32[4,64,96]{2,1,0:T(8,128)S(1)} %pad_maximum_fusion.refs_0_), channel_id=1, source_target_pairs={{0,32},{8,40},{16,48},{24,56},{32,64},{40,72},{48,80},{56,88},{64,... | collective-permute-start | bytes 294920 | tf_op jit(solution)/shard_map/ppermute | solution.py:601
  30.4 9.1 %copy-start.4 = (f32[4,64,96]{2,1,0:T(8,128)}, f32[4,64,96]{2,1,0:T(8,128)S(1)}, u32[]{:S(2)}) copy-start(f32[4,64,96]{2,1,0:T(8,128)S(1)} %pad_maximum_fusion.1.refs_10_) | copy-start | bytes 294916
  30.4 9.2 %collective-permute-start.9 = (f32[4,64,96]{2,1,0:T(8,128)S(1)}, f32[4,64,96]{2,1,0:T(8,128)S(1)}, u32[]{:S(2)}, u32[]{:S(2)}) collective-permute-start(f32[4,64,96]{2,1,0:T(8,128)S(1)} %pad_maximum_fusion.1.refs_10_), channel_id=1, source_target_pairs={{0,4},{1,5},{2,6},{3,7},{4,0},{5,1},{6,2},{7,3},{8,12},{9,13},{10,... | collective-permute-start | bytes 294920 | tf_op jit(solution)/shard_map/ppermute | solution.py:612
  39.5 0.7 copy-start.5
  39.6 0.7 copy-start.6
  39.6 0.7 copy-start.7
  39.6 0.7 copy-start.8
  48.2 11.6 %all-to-all-start.1 = ((f32[8,64,128]{2,1,0:T(8,128)}), f32[8,64,128]{2,1,0:T(8,128)S(1)}, u32[]{:S(2)}, u32[]{:S(2)}) async-start(f32[8,64,128]{2,1,0:T(8,128)} %get-tuple-element.32), calls=%async_computation.1 | async-start | bytes 524288 | tf_op jit(solution)/shard_map/all_to_all | solution.py:545
  59.8 0.7 copy-start.2
  63.3 12.0 %all-to-all-start.2 = ((f32[8,80,128]{2,1,0:T(8,128)}), f32[8,80,128]{2,1,0:T(8,128)S(1)}, u32[]{:S(2)}, u32[]{:S(2)}) async-start(f32[8,80,128]{2,1,0:T(8,128)} %get-tuple-element.38), calls=%async_computation.2 | async-start | bytes 655360 | tf_op jit(solution)/shard_map/all_to_all | solution.py:545
  75.2 9.4 %copy-start.1 = (f32[8,80,128]{2,1,0:T(8,128)}, f32[8,80,128]{2,1,0:T(8,128)S(1)}, u32[]{:S(2)}) copy-start(f32[8,80,128]{2,1,0:T(8,128)S(1)} %all-to-all-done.2.recv_ref) | copy-start | bytes 983044
  76.0 14.8 %all-to-all-start.3 = ((f32[16,16,128]{2,1,0:T(8,128)}), f32[16,16,128]{2,1,0:T(8,128)S(1)}, u32[]{:S(2)}, u32[]{:S(2)}) async-start(f32[16,16,128]{2,1,0:T(8,128)} %shard_map.138), calls=%async_computation.3 | async-start | bytes 262144 | tf_op jit(solution)/shard_map/all_to_all | solution.py:545

commit v4 on v3

--- a/solution.py
+++ b/solution.py
@@ -17,6 +17,7 @@
 VMEM_BYTES = 60 * MIB
 PARTS = 4
 GROUP = 4
+LANES = 128
 LARGE = 48
 FAR = pl.BlockSpec(memory_space=pl.ANY)
 NEAR = pl.BlockSpec(memory_space=pltpu.VMEM)
@@ -40,9 +41,12 @@
 class Near:
     def __init__(self, src, dst, sem):
         self.copy = pltpu.make_async_copy(src, dst, sem)
-        self.copy.start()
         self.dst = dst
         self.waiting = True
+
+    def start(self):
+        self.copy.start()
+        return self
 
     def ready(self):
         if self.waiting:
@@ -69,6 +73,8 @@
             places = refs[-len(small) - 1 : -1]
             for n, (k, place_) in enumerate(zip(small, places)):
                 refs[k] = Near(refs[k], place_, refs[-1].at[n])
+                if near[k] == 1:
+                    refs[k].start()
             kernel(*refs[: -len(small) - 1])
 
     if far_out is not None:
@@ -285,7 +291,11 @@
     normed, wk, wv, dctx, acc, ksem, vsem,
 ):
     key_copies = fetch(wk_far, wk, ksem)
+    for later in (query, bias_a, bias_b):
+        later.start()
     value_copies = fetch(wv_far, wv, vsem)
+    for later in (back_four, back_far, gate):
+        later.start()
     blocks = [piece.ready() for piece in (own, far_a, far_b, far_c)]
     n_sub, rows, block = blocks[0].shape
     queries, heads, keys = expo_ref.shape
@@ -392,6 +402,25 @@
     give.wait()
 
 
+def packed(x):
+    rows, block = x.shape
+    half, rest = rows // 2, LANES - block
+    low = x[half:]
+    right = jnp.concatenate([low[: half // 2, rest:], low[half // 2 :, rest:]], axis=1)
+    return jnp.concatenate([jnp.concatenate([x[:half], low[:, :rest]], axis=1), right], axis=0)
+
+
+def unpacked(x, rows, block):
+    half, wide = rows // 2, 2 * block - LANES
+    top, low = x[:half], x[half:]
+    left = top[:, block:]
+    lower = [
+        jnp.concatenate([left[: half // 2], low[:, :wide]], axis=1),
+        jnp.concatenate([left[half // 2 :], low[:, wide:]], axis=1),
+    ]
+    return jnp.concatenate([top[:, :block]] + lower, axis=0)
+
+
 def join_kernel(recv_ref, stat_ref, moment_ref, pgain_ref, pay_ref, join_ref):
     n, rows, lanes = recv_ref.shape
     heads = moment_ref.shape[1] // 2
@@ -423,15 +452,19 @@
     part = jnp.sum(
         column(fac) * moment_ref[:, :heads] - column(fac * delta) * moment_ref[:, heads:], axis=0
     ) * pgain_ref[...]
+    whole = jnp.concatenate([packed(context), part], axis=0)
     for k in range(n):
-        pay_ref[k, :rows, :block] = context
-        pay_ref[k, rows:, :] = part
+        pay_ref[k] = whole
 
 
 def grad_kernel(
     part, x_far, expo_far, dprobs_far, bias_far, rs, joined, wb, pgain, *refs
 ):
-    out_far, x_ref, expo_ref, dprobs_ref, bias_ref, fac_ref, dlt_ref, out_ref, sems = refs[-9:]
+    if part == 0:
+        out_far, x_ref, expo_ref, dprobs_ref, bias_ref, fac_ref, dlt_ref, out_ref, sems = refs
+    else:
+        _, recv, gate, wout, out_far, att_ref = refs[:6]
+        x_ref, expo_ref, dprobs_ref, bias_ref, fac_ref, dlt_ref, out_ref, sems, gated = refs[6:]
     count, keys = out_ref.shape[:2]
     shift = part * LARGE
     parts = PARTS // 2
@@ -503,6 +536,8 @@
         return carry
 
     lax.fori_loop(0, parts, step, 0)
+    if part == 1:
+        attended_rows(recv.ready(), gate.ready(), wout.ready(), att_ref, gated)
     give.wait()
 
 
@@ -516,11 +551,12 @@
         pay_ref[k] = total
 
 
-def out_kernel(recv_ref, gate_ref, wout_ref, att_ref, gated):
+def attended_rows(recv_ref, gate_ref, wout_ref, att_ref, gated):
     rows, block = att_ref.shape
     for k in range(recv_ref.shape[0]):
         part = slice(k * block, (k + 1) * block)
-        gated[:, part] = recv_ref[k, :rows, :block] * gate_ref[:, part]
+        held = recv_ref[k, : rows * block // LANES]
+        gated[:, part] = unpacked(held, rows, block) * gate_ref[:, part]
     att_ref[...] = dot3(gated[...], wout_ref[...], NT)
 
 
@@ -641,7 +677,7 @@
             dma((3,)),
             dma((3,)),
         ],
-        (1, 1, 1, 1, 1, 0, 0, 1, 1, 1, 1, 1, 1),
+        (1, 1, 1, 1, 1, 0, 0, 2, 2, 2, 2, 2, 2),
     )
     recv4 = swap(pay4, "col")
     shape_m = sds(queries, 2 * heads, chans)
@@ -656,7 +692,7 @@
     )
     pay5, joined = call(
         join_kernel,
-        (sds(n_col, queries + heads, chans), sds(queries, chans)),
+        (sds(n_col, queries * block // LANES + heads, chans), sds(queries, chans)),
         queries * heads * chans * 8,
         (recv4, stat, moment, pgain),
     )
@@ -680,22 +716,15 @@
         share_kernel, sds(n_row, heads, chans), queries * width, (recv5,), vmem=4 * MIB
     )
     recv6 = swap(pay6, "row")
-    pair_grad = call(
+    pair_grad, attended = call(
         functools.partial(grad_kernel, 1),
-        shape_x,
+        (shape_x, sds(queries, block)),
         cost,
-        (pair, expo, dprobs, bias_b, rs_b, joined, wb, pgain, first),
-        held[1],
-        place_of + (0,),
-        (1,),
+        (pair, expo, dprobs, bias_b, rs_b, joined, wb, pgain, first, recv5, gate, wout),
+        held[1] + [pltpu.VMEM((queries, width), F32)],
+        place_of + (0, 1, 1, 1),
+        (1, 0),
         {8: 0},
-    )
-    attended = call(
-        out_kernel,
-        sds(queries, block),
-        queries * width * block * 6,
-        (recv5, gate, wout),
-        [pltpu.VMEM((queries, width), F32)],
     )
     recv6, pair_grad, attended = lax.optimization_barrier((recv6, pair_grad, attended))
     bias_grad = call(last_kernel, sds(heads, chans), chans * heads, (recv6,), vmem=4 * MIB)

time: 91.9 us -> 91.4 us (level)
  Pallas kernels: 40.3 us -> 38.4 us
  waiting for transfers between devices: 7.82 us -> 9.2 us
    pallas_call x12 -> x11, Pallas kernels: 40.3 us -> 38.4 us  [call(): pl.pallas_call(body, out_shape=out_shape, scratch_shapes=scratch, compile...]
    all_to_all x4, waiting for transfers between devices: 5.84 us -> 7.24 us  [swap(): return lax.all_to_all(x, axis, 0, 0, tiled=True)]
  transfers between devices with their start and end apart: 14 -> 14, of which waited for: 6 -> 6; matrix products, arithmetic and copies ran while one was open for 0% -> 0% of each run, Pallas kernels for 29% -> 27%
where the time goes in v4:
time: 91.4 us; the launch traced here: 90.9 us
  starting transfers between devices  41 us (45%)
  Pallas kernels  38.4 us (42%)
  waiting for transfers between devices  9.2 us (10%)
  local copies, waits for them, and re-layouts  1.43 us (2%)
    pallas_call x11, Pallas kernels, call(): pl.pallas_call(body, out_shape=out_shape, scratch_shapes=scratch, compile...  38.4 us
    all_to_all x4, starting transfers between devices, swap(): return lax.all_to_all(x, axis, 0, 0, tiled=True)  24.7 us
    ppermute x5, starting transfers between devices, along(): return lax.ppermute(x, 'row', [(r, target(r)) for r in range(n_row)])  7.65 us
    all_to_all x4, waiting for transfers between devices, swap(): return lax.all_to_all(x, axis, 0, 0, tiled=True)  7.24 us
    ppermute x1, starting transfers between devices, local(): lax.ppermute(back_four, 'col', [(c, (c + n_x) % n_col) for c in range(n_c...  3.3 us
    ppermute x1, starting transfers between devices, local(): moved = lax.ppermute(single, ('row', 'col'), perm)  2.91 us
    ppermute x3, starting transfers between devices, around(): lax.ppermute(x, 'col', [(c, c - c % n_x + (c + k) % n_x) for c in range(n...  2.47 us
  transfers between devices with their start and end apart: 14, of which 6 were waited for; matrix products, arithmetic and copies ran while one was open for 0% of the time, Pallas kernels for 27%

profile of v4, /device:TPU:1, one launch (start us, length us, event | category | flops | bytes accessed | tf_op | source)
XLA Modules:
  0.0 90.9 jit_solution(3137596095222510641)
XLA Ops:
  0.6 2.1 %shard_map.130 = f32[8,96,128]{2,1,0:T(8,128)} custom-call(f32[64,96]{1,0:T(8,128)} %single_ref.1, f32[64,96]{1,0:T(8,128)} %cot_ref.1, f32[96,768]{1,0:T(8,128)} %bitcast.12), custom_call_target="tpu_custom_call" | custom-call | flops 28311552 | bytes 737280 | tf_op jit(solution)/shard_map/pallas_call | solution.py:83
  2.7 8.2 %all-to-all-start = ((f32[8,96,128]{2,1,0:T(8,128)}), f32[8,96,128]{2,1,0:T(8,128)S(1)}, u32[]{:S(2)}, u32[]{:S(2)}) async-start(f32[8,96,128]{2,1,0:T(8,128)} %shard_map.130), calls=%async_computation | async-start | bytes 786432 | tf_op jit(solution)/shard_map/all_to_all | solution.py:581
  10.9 2.9 %collective-permute-start = (f32[64,96]{1,0:T(8,128)}, f32[64,96]{1,0:T(8,128)S(1)}, u32[]{:S(2)}, u32[]{:S(2)}) collective-permute-start(f32[64,96]{1,0:T(8,128)} %single_ref.1), channel_id=1, source_target_pairs={{0,64},{1,32},{2,0},{3,96},{4,80},{5,48},{6,16},{7,112},{8,72},{9,... | collective-permute-start | bytes 73736 | tf_op jit(solution)/shard_map/ppermute | solution.py:608
  13.8 4.3 %shard_map.131 = (f32[48,16,128]{2,1,0:T(8,128)}, f32[48,128]{1,0:T(8,128)}) custom-call(f32[64,128,128]{2,1,0:T(8,128)} %refs_0_.9, f32[16,128]{1,0:T(8,128)} %bitcast.18, f32[1,128]{1,0:T(1,128)} %bitcast.27), custom_call_target="tpu_custom_call" | custom-call | flops 209715200 | bytes 4620800 | tf_op jit(solution)/shard_map/pallas_call | solution.py:83
  18.1 0.7 collective-permute-done
  18.9 1.9 %collective-permute-start.1 = (f32[64,96]{1,0:T(8,128)S(1)}, f32[64,96]{1,0:T(8,128)S(1)}, u32[]{:S(2)}, u32[]{:S(2)}) collective-permute-start(f32[64,96]{1,0:T(8,128)S(1)} %collective-permute-done), channel_id=1, source_target_pairs={{0,8},{8,0},{16,24},{24,16},{32,40},{40,32},{48,56},{56,48},{64,72... | collective-permute-start | bytes 73736 | tf_op jit(solution)/shard_map/ppermute | solution.py:637
  20.8 0.9 collective-permute-done.1
  21.6 2.4 %collective-permute-start.2 = (f32[2,64,96]{2,1,0:T(8,128)S(1)}, f32[2,64,96]{2,1,0:T(8,128)S(1)}, u32[]{:S(2)}, u32[]{:S(2)}) collective-permute-start(f32[2,64,96]{2,1,0:T(8,128)S(1)} %pad_maximum_fusion.2), channel_id=1, source_target_pairs={{0,16},{8,24},{16,0},{24,8},{32,48},{40,56},{48,32},{56,40},{64,80... | collective-permute-start | bytes 147464 | tf_op jit(solution)/shard_map/ppermute | solution.py:637
  24.1 0.0 all-to-all-done.refs_3_.recv_ref
  24.1 0.1 shard_map.133
  24.2 1.5 %collective-permute-start.8 = (f32[64,96]{1,0:T(8,128)S(1)}, f32[64,96]{1,0:T(8,128)S(1)}, u32[]{:S(2)}, u32[]{:S(2)}) collective-permute-start(f32[64,96]{1,0:T(8,128)S(1)} %shard_map.133), channel_id=1, source_target_pairs={{0,3},{1,0},{2,1},{3,2},{4,7},{5,4},{6,5},{7,6},{8,11},{9,8},{10,9... | collective-permute-start | bytes 73736 | tf_op jit(solution)/shard_map/ppermute | solution.py:645
  25.7 0.7 collective-permute-start.7
  26.4 0.3 collective-permute-start.6
  26.7 0.0 collective-permute-done.2
  26.7 0.0 copy-start.3
  26.7 2.5 %collective-permute-start.5 = (f32[4,64,96]{2,1,0:T(8,128)S(1)}, f32[4,64,96]{2,1,0:T(8,128)S(1)}, u32[]{:S(2)}, u32[]{:S(2)}) collective-permute-start(f32[4,64,96]{2,1,0:T(8,128)S(1)} %pad_maximum_fusion.refs_0_), channel_id=1, source_target_pairs={{0,96},{8,104},{16,112},{24,120},{32,0},{40,8},{48,16},{56,24},{64... | collective-permute-start | bytes 294920 | tf_op jit(solution)/shard_map/ppermute | solution.py:637
  29.3 0.3 collective-permute-start.4
  29.6 0.0 collective-permute-done.8
  29.6 0.4 collective-permute-start.3
  30.0 0.0 collective-permute-done.7
  30.0 0.4 collective-permute-done.6
  30.4 0.0 copy-start.4
  30.4 3.3 %collective-permute-start.9 = (f32[4,64,96]{2,1,0:T(8,128)S(1)}, f32[4,64,96]{2,1,0:T(8,128)S(1)}, u32[]{:S(2)}, u32[]{:S(2)}) collective-permute-start(f32[4,64,96]{2,1,0:T(8,128)S(1)} %pad_maximum_fusion.1.refs_10_), channel_id=1, source_target_pairs={{0,4},{1,5},{2,6},{3,7},{4,0},{5,1},{6,2},{7,3},{8,12},{9,13},{10,... | collective-permute-start | bytes 294920 | tf_op jit(solution)/shard_map/ppermute | solution.py:648
  33.7 5.7 %shard_map.132 = (f32[16,16,128]{2,1,0:T(8,128)}, f32[16,128]{1,0:T(8,128)}, f32[64,768]{1,0:T(8,128)}, f32[64,768]{1,0:T(8,128)}) custom-call(f32[64,128,128]{2,1,0:T(8,128)} %refs_0_.9, f32[16,128]{1,0:T(8,128)} %bitcast.19, f32[1,128]{1,0:T(1,128)} %bitcast.28, f32[8,96,128]{2,1,0:T(8,128)} %copy-done, f32[6,128]{1,0:T(8,128)} %bitcast.25, ...), custom_call_target="tpu_custom_call" | custom-call | flops 662700032 | bytes 9850368 | tf_op jit(solution)/shard_map/pallas_call | solution.py:83
  39.5 0.0 collective-permute-done.5.refs_3_
  39.5 0.0 copy-start.5
  39.5 0.0 collective-permute-done.4.refs_2_
  39.5 0.0 collective-permute-done.3.refs_1_
  39.5 0.0 copy-start.7
  39.5 0.0 collective-permute-done.9.refs_11_
  39.6 0.6 copy-done.5
  40.1 0.1 copy-done.6
  40.2 0.0 copy-done.7
  40.2 0.0 copy-done.8
  40.3 7.8 %shard_map.134 = (f32[8,64,128]{2,1,0:T(8,128)}, f32[64,16,128]{2,1,0:T(8,128)}, f32[64,16,128]{2,1,0:T(8,128)}, f32[64,128]{1,0:T(8,128)}) custom-call(f32[4,64,96]{2,1,0:T(8,128)} %copy-done.3, f32[4,64,96]{2,1,0:T(8,128)} %copy-done.7, f32[4,64,96]{2,1,0:T(8,128)} %copy-done.6, f32[4,64,96]{2,1,0:T(8,128)} %copy-done.5, f32[6,128]{1,0:T(8,128)} %bitcast.26, ...), custom_call_target="tpu_custom_call" | custom-call | flops 905969664 | bytes 7572480 | tf_op jit(solution)/shard_map/pallas_call | solution.py:83
  48.1 4.0 %all-to-all-start.1 = ((f32[8,64,128]{2,1,0:T(8,128)}), f32[8,64,128]{2,1,0:T(8,128)S(1)}, u32[]{:S(2)}, u32[]{:S(2)}) async-start(f32[8,64,128]{2,1,0:T(8,128)} %get-tuple-element.34), calls=%async_computation.1 | async-start | bytes 524288 | tf_op jit(solution)/shard_map/all_to_all | solution.py:581
  52.1 4.8 %shard_map.135.moment_ref = f32[64,32,128]{2,1,0:T(8,128)} custom-call(f32[64,128,128]{2,1,0:T(8,128)} %refs_0_.9, f32[64,16,128]{2,1,0:T(8,128)} %get-tuple-element.36.refs_1_, f32[64,16,128]{2,1,0:T(8,128)} %get-tuple-element.37.refs_2_, f32[48,128]{1,0:T(8,128)} %get-tuple-element.38.refs_3_.refs_4_, f32[16,128]{1,0:T(8,128)} %get-tuple-element.39.refs_4_), custom_call_target="tpu_custom_call" | custom-call | flops 201326592 | bytes 6324224 | tf_op jit(solution)/shard_map/pallas_call | solution.py:83
  56.9 2.8 %all-to-all-done.1.recv_ref = f32[8,64,128]{2,1,0:T(8,128)S(1)} async-done(((f32[8,64,128]{2,1,0:T(8,128)}), f32[8,64,128]{2,1,0:T(8,128)S(1)}, u32[]{:S(2)}, u32[]{:S(2)}) %all-to-all-start.1) | async-done | bytes 262176 | tf_op jit(solution)/shard_map/all_to_all | solution.py:581
  59.8 0.7 copy-done.2
  60.5 2.7 %shard_map.136 = (f32[8,64,128]{2,1,0:T(8,128)}, f32[64,128]{1,0:T(8,128)}) custom-call(f32[8,64,128]{2,1,0:T(8,128)} %copy-done.2, f32[64,128]{1,0:T(8,128)} %get-tuple-element.35.stat_ref, f32[64,32,128]{2,1,0:T(8,128)} %shard_map.135.moment_ref, f32[1,128]{1,0:T(1,128)} %bitcast.29), custom_call_target="tpu_custom_call" | custom-call | flops 1048576 | bytes 1638912 | tf_op jit(solution)/shard_map/pallas_call | solution.py:83
  63.2 3.8 %all-to-all-start.2 = ((f32[8,64,128]{2,1,0:T(8,128)}), f32[8,64,128]{2,1,0:T(8,128)S(1)}, u32[]{:S(2)}, u32[]{:S(2)}) async-start(f32[8,64,128]{2,1,0:T(8,128)} %get-tuple-element.40), calls=%async_computation.2 | async-start | bytes 524288 | tf_op jit(solution)/shard_map/all_to_all | solution.py:581
  67.0 5.5 %shard_map.137.refs_8_ = f32[64,128,128]{2,1,0:T(8,128)} custom-call(f32[64,128,128]{2,1,0:T(8,128)} %refs_0_.9, f32[64,16,128]{2,1,0:T(8,128)} %get-tuple-element.36.refs_1_, f32[64,16,128]{2,1,0:T(8,128)} %get-tuple-element.37.refs_2_, f32[48,16,128]{2,1,0:T(8,128)} %get-tuple-element.31.refs_8_.refs_3_, f32[48,128]{1,0:T(8,128)} %get-tuple-element.38.refs_3_.refs_4_, ...), custom_call_target="tpu_custom_call" | custom-call | flops 209715200 | bytes 9896448 | tf_op jit(solution)/shard_map/pallas_call | solution.py:83
  72.5 2.2 %all-to-all-done.2.recv_ref.refs_9_ = f32[8,64,128]{2,1,0:T(8,128)S(1)} async-done(((f32[8,64,128]{2,1,0:T(8,128)}), f32[8,64,128]{2,1,0:T(8,128)S(1)}, u32[]{:S(2)}, u32[]{:S(2)}) %all-to-all-start.2) | async-done | bytes 262176 | tf_op jit(solution)/shard_map/all_to_all | solution.py:581
  74.7 0.7 shard_map.138
  75.4 8.6 %all-to-all-start.3 = ((f32[16,16,128]{2,1,0:T(8,128)}), f32[16,16,128]{2,1,0:T(8,128)S(1)}, u32[]{:S(2)}, u32[]{:S(2)}) async-start(f32[16,16,128]{2,1,0:T(8,128)} %shard_map.138), calls=%async_computation.3 | async-start | bytes 262144 | tf_op jit(solution)/shard_map/all_to_all | solution.py:581
  84.1 4.0 %shard_map.139 = (f32[64,128,128]{2,1,0:T(8,128)}, f32[64,96]{1,0:T(8,128)}) custom-call(f32[64,128,128]{2,1,0:T(8,128)} %refs_0_.9, f32[64,16,128]{2,1,0:T(8,128)} %get-tuple-element.36.refs_1_, f32[64,16,128]{2,1,0:T(8,128)} %get-tuple-element.37.refs_2_, f32[16,16,128]{2,1,0:T(8,128)} %get-tuple-element.32.refs_9_.refs_3_, ...), custom_call_target="tpu_custom_call", output_to_operand_aliasing={{0}: (8, {})} | custom-call | flops 209715200 | bytes 14590464 | tf_op jit(solution)/shard_map/pallas_call | solution.py:83
  88.1 2.2 %all-to-all-done.3.recv_ref = f32[16,16,128]{2,1,0:T(8,128)S(1)} async-done(((f32[16,16,128]{2,1,0:T(8,128)}), f32[16,16,128]{2,1,0:T(8,128)S(1)}, u32[]{:S(2)}, u32[]{:S(2)}) %all-to-all-start.3) | async-done | bytes 131104 | tf_op jit(solution)/shard_map/all_to_all | solution.py:581
  90.3 0.6 shard_map.140
  (12 shorter events, 0.0 us)
Async XLA Ops:
  2.7 21.3 %all-to-all-start = ((f32[8,96,128]{2,1,0:T(8,128)}), f32[8,96,128]{2,1,0:T(8,128)S(1)}, u32[]{:S(2)}, u32[]{:S(2)}) async-start(f32[8,96,128]{2,1,0:T(8,128)} %shard_map.130), calls=%async_computation | async-start | bytes 786432 | tf_op jit(solution)/shard_map/all_to_all | solution.py:581
  10.9 8.0 %collective-permute-start = (f32[64,96]{1,0:T(8,128)}, f32[64,96]{1,0:T(8,128)S(1)}, u32[]{:S(2)}, u32[]{:S(2)}) collective-permute-start(f32[64,96]{1,0:T(8,128)} %single_ref.1), channel_id=1, source_target_pairs={{0,64},{1,32},{2,0},{3,96},{4,80},{5,48},{6,16},{7,112},{8,72},{9,... | collective-permute-start | bytes 73736 | tf_op jit(solution)/shard_map/ppermute | solution.py:608
  18.9 2.8 %collective-permute-start.1 = (f32[64,96]{1,0:T(8,128)S(1)}, f32[64,96]{1,0:T(8,128)S(1)}, u32[]{:S(2)}, u32[]{:S(2)}) collective-permute-start(f32[64,96]{1,0:T(8,128)S(1)} %collective-permute-done), channel_id=1, source_target_pairs={{0,8},{8,0},{16,24},{24,16},{32,40},{40,32},{48,56},{56,48},{64,72... | collective-permute-start | bytes 73736 | tf_op jit(solution)/shard_map/ppermute | solution.py:637
  21.6 5.1 %collective-permute-start.2 = (f32[2,64,96]{2,1,0:T(8,128)S(1)}, f32[2,64,96]{2,1,0:T(8,128)S(1)}, u32[]{:S(2)}, u32[]{:S(2)}) collective-permute-start(f32[2,64,96]{2,1,0:T(8,128)S(1)} %pad_maximum_fusion.2), channel_id=1, source_target_pairs={{0,16},{8,24},{16,0},{24,8},{32,48},{40,56},{48,32},{56,40},{64,80... | collective-permute-start | bytes 147464 | tf_op jit(solution)/shard_map/ppermute | solution.py:637
  24.1 9.7 %copy-start = (f32[8,96,128]{2,1,0:T(8,128)}, f32[8,96,128]{2,1,0:T(8,128)S(1)}, u32[]{:S(2)}) copy-start(f32[8,96,128]{2,1,0:T(8,128)S(1)} %all-to-all-done.refs_3_.recv_ref) | copy-start | bytes 1179652
  24.2 5.4 %collective-permute-start.8 = (f32[64,96]{1,0:T(8,128)S(1)}, f32[64,96]{1,0:T(8,128)S(1)}, u32[]{:S(2)}, u32[]{:S(2)}) collective-permute-start(f32[64,96]{1,0:T(8,128)S(1)} %shard_map.133), channel_id=1, source_target_pairs={{0,3},{1,0},{2,1},{3,2},{4,7},{5,4},{6,5},{7,6},{8,11},{9,8},{10,9... | collective-permute-start | bytes 73736 | tf_op jit(solution)/shard_map/ppermute | solution.py:645
  25.7 4.3 %collective-permute-start.7 = (f32[64,96]{1,0:T(8,128)S(1)}, f32[64,96]{1,0:T(8,128)S(1)}, u32[]{:S(2)}, u32[]{:S(2)}) collective-permute-start(f32[64,96]{1,0:T(8,128)S(1)} %shard_map.133), channel_id=1, source_target_pairs={{0,2},{1,3},{2,0},{3,1},{4,6},{5,7},{6,4},{7,5},{8,10},{9,11},{10,... | collective-permute-start | bytes 73736 | tf_op jit(solution)/shard_map/ppermute | solution.py:645
  26.4 4.0 %collective-permute-start.6 = (f32[64,96]{1,0:T(8,128)S(1)}, f32[64,96]{1,0:T(8,128)S(1)}, u32[]{:S(2)}, u32[]{:S(2)}) collective-permute-start(f32[64,96]{1,0:T(8,128)S(1)} %shard_map.133), channel_id=1, source_target_pairs={{0,1},{1,2},{2,3},{3,0},{4,5},{5,6},{6,7},{7,4},{8,9},{9,10},{10,1... | collective-permute-start | bytes 73736 | tf_op jit(solution)/shard_map/ppermute | solution.py:645
  26.7 12.7 %copy-start.3 = (f32[4,64,96]{2,1,0:T(8,128)}, f32[4,64,96]{2,1,0:T(8,128)S(1)}, u32[]{:S(2)}) copy-start(f32[4,64,96]{2,1,0:T(8,128)S(1)} %pad_maximum_fusion.refs_0_) | copy-start | bytes 294916
  26.7 12.8 %collective-permute-start.5 = (f32[4,64,96]{2,1,0:T(8,128)S(1)}, f32[4,64,96]{2,1,0:T(8,128)S(1)}, u32[]{:S(2)}, u32[]{:S(2)}) collective-permute-start(f32[4,64,96]{2,1,0:T(8,128)S(1)} %pad_maximum_fusion.refs_0_), channel_id=1, source_target_pairs={{0,96},{8,104},{16,112},{24,120},{32,0},{40,8},{48,16},{56,24},{64... | collective-permute-start | bytes 294920 | tf_op jit(solution)/shard_map/ppermute | solution.py:637
  29.3 10.2 %collective-permute-start.4 = (f32[4,64,96]{2,1,0:T(8,128)S(1)}, f32[4,64,96]{2,1,0:T(8,128)S(1)}, u32[]{:S(2)}, u32[]{:S(2)}) collective-permute-start(f32[4,64,96]{2,1,0:T(8,128)S(1)} %pad_maximum_fusion.refs_0_), channel_id=1, source_target_pairs={{0,64},{8,72},{16,80},{24,88},{32,96},{40,104},{48,112},{56,120},{... | collective-permute-start | bytes 294920 | tf_op jit(solution)/shard_map/ppermute | solution.py:637
  29.6 9.9 %collective-permute-start.3 = (f32[4,64,96]{2,1,0:T(8,128)S(1)}, f32[4,64,96]{2,1,0:T(8,128)S(1)}, u32[]{:S(2)}, u32[]{:S(2)}) collective-permute-start(f32[4,64,96]{2,1,0:T(8,128)S(1)} %pad_maximum_fusion.refs_0_), channel_id=1, source_target_pairs={{0,32},{8,40},{16,48},{24,56},{32,64},{40,72},{48,80},{56,88},{64,... | collective-permute-start | bytes 294920 | tf_op jit(solution)/shard_map/ppermute | solution.py:637
  30.4 9.0 %copy-start.4 = (f32[4,64,96]{2,1,0:T(8,128)}, f32[4,64,96]{2,1,0:T(8,128)S(1)}, u32[]{:S(2)}) copy-start(f32[4,64,96]{2,1,0:T(8,128)S(1)} %pad_maximum_fusion.1.refs_10_) | copy-start | bytes 294916
  30.4 9.1 %collective-permute-start.9 = (f32[4,64,96]{2,1,0:T(8,128)S(1)}, f32[4,64,96]{2,1,0:T(8,128)S(1)}, u32[]{:S(2)}, u32[]{:S(2)}) collective-permute-start(f32[4,64,96]{2,1,0:T(8,128)S(1)} %pad_maximum_fusion.1.refs_10_), channel_id=1, source_target_pairs={{0,4},{1,5},{2,6},{3,7},{4,0},{5,1},{6,2},{7,3},{8,12},{9,13},{10,... | collective-permute-start | bytes 294920 | tf_op jit(solution)/shard_map/ppermute | solution.py:648
  39.5 0.6 copy-start.5
  39.5 0.7 copy-start.6
  39.5 0.7 copy-start.7
  39.5 0.7 copy-start.8
  48.1 11.7 %all-to-all-start.1 = ((f32[8,64,128]{2,1,0:T(8,128)}), f32[8,64,128]{2,1,0:T(8,128)S(1)}, u32[]{:S(2)}, u32[]{:S(2)}) async-start(f32[8,64,128]{2,1,0:T(8,128)} %get-tuple-element.34), calls=%async_computation.1 | async-start | bytes 524288 | tf_op jit(solution)/shard_map/all_to_all | solution.py:581
  59.8 0.7 copy-start.2
  63.2 11.5 %all-to-all-start.2 = ((f32[8,64,128]{2,1,0:T(8,128)}), f32[8,64,128]{2,1,0:T(8,128)S(1)}, u32[]{:S(2)}, u32[]{:S(2)}) async-start(f32[8,64,128]{2,1,0:T(8,128)} %get-tuple-element.40), calls=%async_computation.2 | async-start | bytes 524288 | tf_op jit(solution)/shard_map/all_to_all | solution.py:581
  74.7 9.4 %copy-start.1 = (f32[8,64,128]{2,1,0:T(8,128)}, f32[8,64,128]{2,1,0:T(8,128)S(1)}, u32[]{:S(2)}) copy-start(f32[8,64,128]{2,1,0:T(8,128)S(1)} %all-to-all-done.2.recv_ref.refs_9_) | copy-start | bytes 786436
  75.4 14.8 %all-to-all-start.3 = ((f32[16,16,128]{2,1,0:T(8,128)}), f32[16,16,128]{2,1,0:T(8,128)S(1)}, u32[]{:S(2)}, u32[]{:S(2)}) async-start(f32[16,16,128]{2,1,0:T(8,128)} %shard_map.138), calls=%async_computation.3 | async-start | bytes 262144 | tf_op jit(solution)/shard_map/all_to_all | solution.py:581

commit v5 on v4

--- a/solution.py
+++ b/solution.py
@@ -127,7 +127,27 @@
     return lax.broadcasted_iota(jnp.int32, (n, n), 0) == lax.broadcasted_iota(jnp.int32, (n, n), 1)
 
 
-def first_kernel(single_ref, cot_ref, wout_ref, out_ref):
+def packed(x):
+    rows, block = x.shape
+    half, rest = rows // 2, LANES - block
+    low = x[half:]
+    right = jnp.concatenate([low[: half // 2, rest:], low[half // 2 :, rest:]], axis=1)
+    return jnp.concatenate([jnp.concatenate([x[:half], low[:, :rest]], axis=1), right], axis=0)
+
+
+def unpacked(x, rows, block):
+    half, wide = rows // 2, 2 * block - LANES
+    top, low = x[:half], x[half:]
+    left = top[:, block:]
+    lower = [
+        jnp.concatenate([left[: half // 2], low[:, :wide]], axis=1),
+        jnp.concatenate([left[half // 2 :], low[:, wide:]], axis=1),
+    ]
+    return jnp.concatenate([top[:, :block]] + lower, axis=0)
+
+
+def first_kernel(single_ref, cot_ref, wout_ref, out_ref, packed_ref):
+    packed_ref[...] = packed(single_ref[...])
     n, _, lanes = out_ref.shape
     rows, block = single_ref.shape
     rest = lanes - block
@@ -297,7 +317,8 @@
     for later in (back_four, back_far, gate):
         later.start()
     blocks = [piece.ready() for piece in (own, far_a, far_b, far_c)]
-    n_sub, rows, block = blocks[0].shape
+    n_sub = blocks[0].shape[0]
+    rows, block = back_four.dst.shape[1:]
     queries, heads, keys = expo_ref.shape
     width = normed.shape[1]
     n_col = width // block
@@ -309,9 +330,10 @@
         hop = (me // n_sub + 4 - there // n_sub) % 4
         spot = (me % n_sub) ^ (there % n_sub)
         some = [piece[spot] for piece in blocks]
-        return jnp.where(
+        one = jnp.where(
             hop < 2, jnp.where(hop == 0, some[0], some[1]), jnp.where(hop == 2, some[2], some[3])
         )
+        return unpacked(one, rows, block)
 
     for t in range(keys // rows):
         joined_norm([token_block(k, t) for k in range(n_col)], normed, t * rows)
@@ -402,25 +424,6 @@
     give.wait()
 
 
-def packed(x):
-    rows, block = x.shape
-    half, rest = rows // 2, LANES - block
-    low = x[half:]
-    right = jnp.concatenate([low[: half // 2, rest:], low[half // 2 :, rest:]], axis=1)
-    return jnp.concatenate([jnp.concatenate([x[:half], low[:, :rest]], axis=1), right], axis=0)
-
-
-def unpacked(x, rows, block):
-    half, wide = rows // 2, 2 * block - LANES
-    top, low = x[:half], x[half:]
-    left = top[:, block:]
-    lower = [
-        jnp.concatenate([left[: half // 2], low[:, :wide]], axis=1),
-        jnp.concatenate([left[half // 2 :], low[:, wide:]], axis=1),
-    ]
-    return jnp.concatenate([top[:, :block]] + lower, axis=0)
-
-
 def join_kernel(recv_ref, stat_ref, moment_ref, pgain_ref, pay_ref, join_ref):
     n, rows, lanes = recv_ref.shape
     heads = moment_ref.shape[1] // 2
@@ -605,13 +608,13 @@
         for r in range(n_row)
         for c in range(n_col)
     ]
-    moved = lax.ppermute(single, ("row", "col"), perm)
-    pay1 = call(
+    pay1, packed_single = call(
         first_kernel,
-        sds(n_col, queries + queries // 2, chans),
+        (sds(n_col, queries + queries // 2, chans), sds(queries * block // LANES, LANES)),
         2 * queries * width * block * 3,
         (single, cotangent, wout),
     )
+    moved = lax.ppermute(packed_single, ("row", "col"), perm)
     recv1 = swap(pay1, "col")
     shape_x = sds(queries, keys, chans)
     counts = (LARGE, queries - LARGE)

time: 91.4 us -> 91.1 us (level)
  no operation moved by 1% of the time
where the time goes in v5:
time: 91.1 us; the launch traced here: 90.5 us
  starting transfers between devices  41.1 us (45%)
  Pallas kernels  38.5 us (42%)
  waiting for transfers between devices  8.75 us (10%)
  local copies, waits for them, and re-layouts  1.42 us (2%)
    pallas_call x11, Pallas kernels, call(): pl.pallas_call(body, out_shape=out_shape, scratch_shapes=scratch, compile...  38.5 us
    all_to_all x4, starting transfers between devices, swap(): return lax.all_to_all(x, axis, 0, 0, tiled=True)  25.4 us
    ppermute x5, starting transfers between devices, along(): return lax.ppermute(x, 'row', [(r, target(r)) for r in range(n_row)])  7.9 us
    all_to_all x4, waiting for transfers between devices, swap(): return lax.all_to_all(x, axis, 0, 0, tiled=True)  7.23 us
    ppermute x1, starting transfers between devices, local(): moved = lax.ppermute(packed_single, ('row', 'col'), perm)  2.91 us
    ppermute x1, starting transfers between devices, local(): lax.ppermute(back_four, 'col', [(c, (c + n_x) % n_col) for c in range(n_c...  2.46 us
    ppermute x3, starting transfers between devices, around(): lax.ppermute(x, 'col', [(c, c - c % n_x + (c + k) % n_x) for c in range(n...  2.36 us
  transfers between devices with their start and end apart: 14, of which 6 were waited for; matrix products, arithmetic and copies ran while one was open for 0% of the time, Pallas kernels for 27%

profile of v5, /device:TPU:1, one launch (start us, length us, event | category | flops | bytes accessed | tf_op | source)
XLA Modules:
  0.0 90.5 jit_solution(14911849137849083167)
XLA Ops:
  0.6 2.1 %shard_map.130 = (f32[8,96,128]{2,1,0:T(8,128)}, f32[48,128]{1,0:T(8,128)}) custom-call(f32[64,96]{1,0:T(8,128)} %single_ref.1, f32[64,96]{1,0:T(8,128)} %cot_ref.1, f32[96,768]{1,0:T(8,128)} %bitcast.12), custom_call_target="tpu_custom_call" | custom-call | flops 28311552 | bytes 761856 | tf_op jit(solution)/shard_map/pallas_call | solution.py:83
  2.7 8.2 %all-to-all-start = ((f32[8,96,128]{2,1,0:T(8,128)}), f32[8,96,128]{2,1,0:T(8,128)S(1)}, u32[]{:S(2)}, u32[]{:S(2)}) async-start(f32[8,96,128]{2,1,0:T(8,128)} %get-tuple-element.28), calls=%async_computation | async-start | bytes 786432 | tf_op jit(solution)/shard_map/all_to_all | solution.py:584
  10.9 2.9 %collective-permute-start = (f32[48,128]{1,0:T(8,128)}, f32[48,128]{1,0:T(8,128)S(1)}, u32[]{:S(2)}, u32[]{:S(2)}) collective-permute-start(f32[48,128]{1,0:T(8,128)} %get-tuple-element.29), channel_id=1, source_target_pairs={{0,64},{1,32},{2,0},{3,96},{4,80},{5,48},{6,16},{7,112},{8,72},{9,... | collective-permute-start | bytes 73736 | tf_op jit(solution)/shard_map/ppermute | solution.py:617
  13.8 4.3 %shard_map.131 = (f32[48,16,128]{2,1,0:T(8,128)}, f32[48,128]{1,0:T(8,128)}) custom-call(f32[64,128,128]{2,1,0:T(8,128)} %refs_0_.9, f32[16,128]{1,0:T(8,128)} %bitcast.14, f32[1,128]{1,0:T(1,128)} %bitcast.27), custom_call_target="tpu_custom_call" | custom-call | flops 209715200 | bytes 4620800 | tf_op jit(solution)/shard_map/pallas_call | solution.py:83
  18.2 0.2 collective-permute-done
  18.4 2.2 %collective-permute-start.1 = (f32[48,128]{1,0:T(8,128)S(1)}, f32[48,128]{1,0:T(8,128)S(1)}, u32[]{:S(2)}, u32[]{:S(2)}) collective-permute-start(f32[48,128]{1,0:T(8,128)S(1)} %collective-permute-done), channel_id=1, source_target_pairs={{0,8},{8,0},{16,24},{24,16},{32,40},{40,32},{48,56},{56,48},{64,72... | collective-permute-start | bytes 73736 | tf_op jit(solution)/shard_map/ppermute | solution.py:640
  20.6 0.8 collective-permute-done.1
  21.5 2.3 %collective-permute-start.2 = (f32[2,48,128]{2,1,0:T(8,128)S(1)}, f32[2,48,128]{2,1,0:T(8,128)S(1)}, u32[]{:S(2)}, u32[]{:S(2)}) collective-permute-start(f32[2,48,128]{2,1,0:T(8,128)S(1)} %pad_maximum_fusion.2), channel_id=1, source_target_pairs={{0,16},{8,24},{16,0},{24,8},{32,48},{40,56},{48,32},{56,40},{64,80... | collective-permute-start | bytes 147464 | tf_op jit(solution)/shard_map/ppermute | solution.py:640
  23.8 0.0 all-to-all-done.refs_3_.recv_ref
  23.8 0.1 shard_map.133
  23.9 1.5 %collective-permute-start.8 = (f32[64,96]{1,0:T(8,128)S(1)}, f32[64,96]{1,0:T(8,128)S(1)}, u32[]{:S(2)}, u32[]{:S(2)}) collective-permute-start(f32[64,96]{1,0:T(8,128)S(1)} %shard_map.133), channel_id=1, source_target_pairs={{0,3},{1,0},{2,1},{3,2},{4,7},{5,4},{6,5},{7,6},{8,11},{9,8},{10,9... | collective-permute-start | bytes 73736 | tf_op jit(solution)/shard_map/ppermute | solution.py:648
  25.4 0.7 collective-permute-start.7
  26.1 0.1 collective-permute-start.6
  26.3 0.0 collective-permute-done.2
  26.3 0.0 copy-start.4
  26.3 2.7 %collective-permute-start.5 = (f32[4,48,128]{2,1,0:T(8,128)S(1)}, f32[4,48,128]{2,1,0:T(8,128)S(1)}, u32[]{:S(2)}, u32[]{:S(2)}) collective-permute-start(f32[4,48,128]{2,1,0:T(8,128)S(1)} %pad_maximum_fusion.1.refs_0_), channel_id=1, source_target_pairs={{0,96},{8,104},{16,112},{24,120},{32,0},{40,8},{48,16},{56,24},{64... | collective-permute-start | bytes 294920 | tf_op jit(solution)/shard_map/ppermute | solution.py:640
  29.0 0.2 collective-permute-start.4
  29.2 0.0 collective-permute-done.8
  29.2 0.4 collective-permute-start.3
  29.7 0.0 collective-permute-done.7
  29.7 0.4 collective-permute-done.6
  30.2 2.5 %collective-permute-start.9 = (f32[4,64,96]{2,1,0:T(8,128)S(1)}, f32[4,64,96]{2,1,0:T(8,128)S(1)}, u32[]{:S(2)}, u32[]{:S(2)}) collective-permute-start(f32[4,64,96]{2,1,0:T(8,128)S(1)} %pad_maximum_fusion.refs_10_), channel_id=1, source_target_pairs={{0,4},{1,5},{2,6},{3,7},{4,0},{5,1},{6,2},{7,3},{8,12},{9,13},{10,... | collective-permute-start | bytes 294920 | tf_op jit(solution)/shard_map/ppermute | solution.py:651
  32.6 0.0 copy-done
  32.6 5.7 %shard_map.132 = (f32[16,16,128]{2,1,0:T(8,128)}, f32[16,128]{1,0:T(8,128)}, f32[64,768]{1,0:T(8,128)}, f32[64,768]{1,0:T(8,128)}) custom-call(f32[64,128,128]{2,1,0:T(8,128)} %refs_0_.9, f32[16,128]{1,0:T(8,128)} %bitcast.15, f32[1,128]{1,0:T(1,128)} %bitcast.28, f32[8,96,128]{2,1,0:T(8,128)} %copy-done, f32[6,128]{1,0:T(8,128)} %bitcast.25, ...), custom_call_target="tpu_custom_call" | custom-call | flops 662700032 | bytes 9850368 | tf_op jit(solution)/shard_map/pallas_call | solution.py:83
  38.4 0.0 collective-permute-done.5.refs_3_
  38.4 0.0 collective-permute-done.4.refs_2_
  38.4 0.0 copy-start.7
  38.4 0.0 collective-permute-done.3.refs_1_
  38.4 0.0 collective-permute-done.9.refs_11_
  38.4 0.0 copy-start.5
  38.5 0.6 copy-done.6
  39.0 0.1 copy-done.7
  39.1 0.0 copy-done.8
  39.1 0.0 copy-done.5
  39.1 7.8 %shard_map.134 = (f32[8,64,128]{2,1,0:T(8,128)}, f32[64,16,128]{2,1,0:T(8,128)}, f32[64,16,128]{2,1,0:T(8,128)}, f32[64,128]{1,0:T(8,128)}) custom-call(f32[4,48,128]{2,1,0:T(8,128)} %copy-done.4, f32[4,48,128]{2,1,0:T(8,128)} %copy-done.8, f32[4,48,128]{2,1,0:T(8,128)} %copy-done.7, f32[4,48,128]{2,1,0:T(8,128)} %copy-done.6, f32[6,128]{1,0:T(8,128)} %bitcast.26, ...), custom_call_target="tpu_custom_call" | custom-call | flops 905969664 | bytes 7572480 | tf_op jit(solution)/shard_map/pallas_call | solution.py:83
  47.0 3.8 %all-to-all-start.1 = ((f32[8,64,128]{2,1,0:T(8,128)}), f32[8,64,128]{2,1,0:T(8,128)S(1)}, u32[]{:S(2)}, u32[]{:S(2)}) async-start(f32[8,64,128]{2,1,0:T(8,128)} %get-tuple-element.38), calls=%async_computation.1 | async-start | bytes 524288 | tf_op jit(solution)/shard_map/all_to_all | solution.py:584
  50.8 4.8 %shard_map.135.moment_ref = f32[64,32,128]{2,1,0:T(8,128)} custom-call(f32[64,128,128]{2,1,0:T(8,128)} %refs_0_.9, f32[64,16,128]{2,1,0:T(8,128)} %get-tuple-element.40.refs_1_, f32[64,16,128]{2,1,0:T(8,128)} %get-tuple-element.41.refs_2_, f32[48,128]{1,0:T(8,128)} %get-tuple-element.42.refs_3_.refs_4_, f32[16,128]{1,0:T(8,128)} %get-tuple-element.43.refs_4_), custom_call_target="tpu_custom_call" | custom-call | flops 201326592 | bytes 6324224 | tf_op jit(solution)/shard_map/pallas_call | solution.py:83
  55.6 2.9 %all-to-all-done.1.recv_ref = f32[8,64,128]{2,1,0:T(8,128)S(1)} async-done(((f32[8,64,128]{2,1,0:T(8,128)}), f32[8,64,128]{2,1,0:T(8,128)S(1)}, u32[]{:S(2)}, u32[]{:S(2)}) %all-to-all-start.1) | async-done | bytes 262176 | tf_op jit(solution)/shard_map/all_to_all | solution.py:584
  58.4 0.7 copy-done.2
  59.2 2.7 %shard_map.136 = (f32[8,64,128]{2,1,0:T(8,128)}, f32[64,128]{1,0:T(8,128)}) custom-call(f32[8,64,128]{2,1,0:T(8,128)} %copy-done.2, f32[64,128]{1,0:T(8,128)} %get-tuple-element.39.stat_ref, f32[64,32,128]{2,1,0:T(8,128)} %shard_map.135.moment_ref, f32[1,128]{1,0:T(1,128)} %bitcast.29), custom_call_target="tpu_custom_call" | custom-call | flops 1048576 | bytes 1638912 | tf_op jit(solution)/shard_map/pallas_call | solution.py:83
  61.9 3.8 %all-to-all-start.2 = ((f32[8,64,128]{2,1,0:T(8,128)}), f32[8,64,128]{2,1,0:T(8,128)S(1)}, u32[]{:S(2)}, u32[]{:S(2)}) async-start(f32[8,64,128]{2,1,0:T(8,128)} %get-tuple-element.44), calls=%async_computation.2 | async-start | bytes 524288 | tf_op jit(solution)/shard_map/all_to_all | solution.py:584
  65.7 5.5 %shard_map.137.refs_8_ = f32[64,128,128]{2,1,0:T(8,128)} custom-call(f32[64,128,128]{2,1,0:T(8,128)} %refs_0_.9, f32[64,16,128]{2,1,0:T(8,128)} %get-tuple-element.40.refs_1_, f32[64,16,128]{2,1,0:T(8,128)} %get-tuple-element.41.refs_2_, f32[48,16,128]{2,1,0:T(8,128)} %get-tuple-element.35.refs_8_.refs_3_, f32[48,128]{1,0:T(8,128)} %get-tuple-element.42.refs_3_.refs_4_, ...), custom_call_target="tpu_custom_call" | custom-call | flops 209715200 | bytes 9896448 | tf_op jit(solution)/shard_map/pallas_call | solution.py:83
  71.1 2.2 %all-to-all-done.2.recv_ref.refs_9_ = f32[8,64,128]{2,1,0:T(8,128)S(1)} async-done(((f32[8,64,128]{2,1,0:T(8,128)}), f32[8,64,128]{2,1,0:T(8,128)S(1)}, u32[]{:S(2)}, u32[]{:S(2)}) %all-to-all-start.2) | async-done | bytes 262176 | tf_op jit(solution)/shard_map/all_to_all | solution.py:584
  73.3 0.7 shard_map.138
  74.0 9.7 %all-to-all-start.3 = ((f32[16,16,128]{2,1,0:T(8,128)}), f32[16,16,128]{2,1,0:T(8,128)S(1)}, u32[]{:S(2)}, u32[]{:S(2)}) async-start(f32[16,16,128]{2,1,0:T(8,128)} %shard_map.138), calls=%async_computation.3 | async-start | bytes 262144 | tf_op jit(solution)/shard_map/all_to_all | solution.py:584
  83.7 4.0 %shard_map.139 = (f32[64,128,128]{2,1,0:T(8,128)}, f32[64,96]{1,0:T(8,128)}) custom-call(f32[64,128,128]{2,1,0:T(8,128)} %refs_0_.9, f32[64,16,128]{2,1,0:T(8,128)} %get-tuple-element.40.refs_1_, f32[64,16,128]{2,1,0:T(8,128)} %get-tuple-element.41.refs_2_, f32[16,16,128]{2,1,0:T(8,128)} %get-tuple-element.36.refs_9_.refs_3_, ...), custom_call_target="tpu_custom_call", output_to_operand_aliasing={{0}: (8, {})} | custom-call | flops 209715200 | bytes 14590464 | tf_op jit(solution)/shard_map/pallas_call | solution.py:83
  87.7 2.2 %all-to-all-done.3.recv_ref = f32[16,16,128]{2,1,0:T(8,128)S(1)} async-done(((f32[16,16,128]{2,1,0:T(8,128)}), f32[16,16,128]{2,1,0:T(8,128)S(1)}, u32[]{:S(2)}, u32[]{:S(2)}) %all-to-all-start.3) | async-done | bytes 131104 | tf_op jit(solution)/shard_map/all_to_all | solution.py:584
  89.9 0.6 shard_map.140
  (12 shorter events, 0.0 us)
Async XLA Ops:
  2.7 21.0 %all-to-all-start = ((f32[8,96,128]{2,1,0:T(8,128)}), f32[8,96,128]{2,1,0:T(8,128)S(1)}, u32[]{:S(2)}, u32[]{:S(2)}) async-start(f32[8,96,128]{2,1,0:T(8,128)} %get-tuple-element.28), calls=%async_computation | async-start | bytes 786432 | tf_op jit(solution)/shard_map/all_to_all | solution.py:584
  10.9 7.5 %collective-permute-start = (f32[48,128]{1,0:T(8,128)}, f32[48,128]{1,0:T(8,128)S(1)}, u32[]{:S(2)}, u32[]{:S(2)}) collective-permute-start(f32[48,128]{1,0:T(8,128)} %get-tuple-element.29), channel_id=1, source_target_pairs={{0,64},{1,32},{2,0},{3,96},{4,80},{5,48},{6,16},{7,112},{8,72},{9,... | collective-permute-start | bytes 73736 | tf_op jit(solution)/shard_map/ppermute | solution.py:617
  18.4 3.1 %collective-permute-start.1 = (f32[48,128]{1,0:T(8,128)S(1)}, f32[48,128]{1,0:T(8,128)S(1)}, u32[]{:S(2)}, u32[]{:S(2)}) collective-permute-start(f32[48,128]{1,0:T(8,128)S(1)} %collective-permute-done), channel_id=1, source_target_pairs={{0,8},{8,0},{16,24},{24,16},{32,40},{40,32},{48,56},{56,48},{64,72... | collective-permute-start | bytes 73736 | tf_op jit(solution)/shard_map/ppermute | solution.py:640
  21.5 4.8 %collective-permute-start.2 = (f32[2,48,128]{2,1,0:T(8,128)S(1)}, f32[2,48,128]{2,1,0:T(8,128)S(1)}, u32[]{:S(2)}, u32[]{:S(2)}) collective-permute-start(f32[2,48,128]{2,1,0:T(8,128)S(1)} %pad_maximum_fusion.2), channel_id=1, source_target_pairs={{0,16},{8,24},{16,0},{24,8},{32,48},{40,56},{48,32},{56,40},{64,80... | collective-permute-start | bytes 147464 | tf_op jit(solution)/shard_map/ppermute | solution.py:640
  23.8 8.9 %copy-start = (f32[8,96,128]{2,1,0:T(8,128)}, f32[8,96,128]{2,1,0:T(8,128)S(1)}, u32[]{:S(2)}) copy-start(f32[8,96,128]{2,1,0:T(8,128)S(1)} %all-to-all-done.refs_3_.recv_ref) | copy-start | bytes 1179652
  23.9 5.3 %collective-permute-start.8 = (f32[64,96]{1,0:T(8,128)S(1)}, f32[64,96]{1,0:T(8,128)S(1)}, u32[]{:S(2)}, u32[]{:S(2)}) collective-permute-start(f32[64,96]{1,0:T(8,128)S(1)} %shard_map.133), channel_id=1, source_target_pairs={{0,3},{1,0},{2,1},{3,2},{4,7},{5,4},{6,5},{7,6},{8,11},{9,8},{10,9... | collective-permute-start | bytes 73736 | tf_op jit(solution)/shard_map/ppermute | solution.py:648
  25.4 4.3 %collective-permute-start.7 = (f32[64,96]{1,0:T(8,128)S(1)}, f32[64,96]{1,0:T(8,128)S(1)}, u32[]{:S(2)}, u32[]{:S(2)}) collective-permute-start(f32[64,96]{1,0:T(8,128)S(1)} %shard_map.133), channel_id=1, source_target_pairs={{0,2},{1,3},{2,0},{3,1},{4,6},{5,7},{6,4},{7,5},{8,10},{9,11},{10,... | collective-permute-start | bytes 73736 | tf_op jit(solution)/shard_map/ppermute | solution.py:648
  26.1 4.0 %collective-permute-start.6 = (f32[64,96]{1,0:T(8,128)S(1)}, f32[64,96]{1,0:T(8,128)S(1)}, u32[]{:S(2)}, u32[]{:S(2)}) collective-permute-start(f32[64,96]{1,0:T(8,128)S(1)} %shard_map.133), channel_id=1, source_target_pairs={{0,1},{1,2},{2,3},{3,0},{4,5},{5,6},{6,7},{7,4},{8,9},{9,10},{10,1... | collective-permute-start | bytes 73736 | tf_op jit(solution)/shard_map/ppermute | solution.py:648
  26.3 12.1 %copy-start.4 = (f32[4,48,128]{2,1,0:T(8,128)}, f32[4,48,128]{2,1,0:T(8,128)S(1)}, u32[]{:S(2)}) copy-start(f32[4,48,128]{2,1,0:T(8,128)S(1)} %pad_maximum_fusion.1.refs_0_) | copy-start | bytes 294916
  26.3 12.1 %collective-permute-start.5 = (f32[4,48,128]{2,1,0:T(8,128)S(1)}, f32[4,48,128]{2,1,0:T(8,128)S(1)}, u32[]{:S(2)}, u32[]{:S(2)}) collective-permute-start(f32[4,48,128]{2,1,0:T(8,128)S(1)} %pad_maximum_fusion.1.refs_0_), channel_id=1, source_target_pairs={{0,96},{8,104},{16,112},{24,120},{32,0},{40,8},{48,16},{56,24},{64... | collective-permute-start | bytes 294920 | tf_op jit(solution)/shard_map/ppermute | solution.py:640
  29.0 9.4 %collective-permute-start.4 = (f32[4,48,128]{2,1,0:T(8,128)S(1)}, f32[4,48,128]{2,1,0:T(8,128)S(1)}, u32[]{:S(2)}, u32[]{:S(2)}) collective-permute-start(f32[4,48,128]{2,1,0:T(8,128)S(1)} %pad_maximum_fusion.1.refs_0_), channel_id=1, source_target_pairs={{0,64},{8,72},{16,80},{24,88},{32,96},{40,104},{48,112},{56,120},{... | collective-permute-start | bytes 294920 | tf_op jit(solution)/shard_map/ppermute | solution.py:640
  29.2 9.2 %collective-permute-start.3 = (f32[4,48,128]{2,1,0:T(8,128)S(1)}, f32[4,48,128]{2,1,0:T(8,128)S(1)}, u32[]{:S(2)}, u32[]{:S(2)}) collective-permute-start(f32[4,48,128]{2,1,0:T(8,128)S(1)} %pad_maximum_fusion.1.refs_0_), channel_id=1, source_target_pairs={{0,32},{8,40},{16,48},{24,56},{32,64},{40,72},{48,80},{56,88},{64,... | collective-permute-start | bytes 294920 | tf_op jit(solution)/shard_map/ppermute | solution.py:640
  30.1 8.2 %copy-start.3 = (f32[4,64,96]{2,1,0:T(8,128)}, f32[4,64,96]{2,1,0:T(8,128)S(1)}, u32[]{:S(2)}) copy-start(f32[4,64,96]{2,1,0:T(8,128)S(1)} %pad_maximum_fusion.refs_10_) | copy-start | bytes 294916
  30.2 8.3 %collective-permute-start.9 = (f32[4,64,96]{2,1,0:T(8,128)S(1)}, f32[4,64,96]{2,1,0:T(8,128)S(1)}, u32[]{:S(2)}, u32[]{:S(2)}) collective-permute-start(f32[4,64,96]{2,1,0:T(8,128)S(1)} %pad_maximum_fusion.refs_10_), channel_id=1, source_target_pairs={{0,4},{1,5},{2,6},{3,7},{4,0},{5,1},{6,2},{7,3},{8,12},{9,13},{10,... | collective-permute-start | bytes 294920 | tf_op jit(solution)/shard_map/ppermute | solution.py:651
  38.4 0.6 copy-start.6
  38.4 0.7 copy-start.7
  38.4 0.7 copy-start.8
  38.4 0.7 copy-start.5
  47.0 11.5 %all-to-all-start.1 = ((f32[8,64,128]{2,1,0:T(8,128)}), f32[8,64,128]{2,1,0:T(8,128)S(1)}, u32[]{:S(2)}, u32[]{:S(2)}) async-start(f32[8,64,128]{2,1,0:T(8,128)} %get-tuple-element.38), calls=%async_computation.1 | async-start | bytes 524288 | tf_op jit(solution)/shard_map/all_to_all | solution.py:584
  58.4 0.7 copy-start.2
  61.9 11.4 %all-to-all-start.2 = ((f32[8,64,128]{2,1,0:T(8,128)}), f32[8,64,128]{2,1,0:T(8,128)S(1)}, u32[]{:S(2)}, u32[]{:S(2)}) async-start(f32[8,64,128]{2,1,0:T(8,128)} %get-tuple-element.44), calls=%async_computation.2 | async-start | bytes 524288 | tf_op jit(solution)/shard_map/all_to_all | solution.py:584
  73.3 10.4 %copy-start.1 = (f32[8,64,128]{2,1,0:T(8,128)}, f32[8,64,128]{2,1,0:T(8,128)S(1)}, u32[]{:S(2)}) copy-start(f32[8,64,128]{2,1,0:T(8,128)S(1)} %all-to-all-done.2.recv_ref.refs_9_) | copy-start | bytes 786436
  74.0 15.9 %all-to-all-start.3 = ((f32[16,16,128]{2,1,0:T(8,128)}), f32[16,16,128]{2,1,0:T(8,128)S(1)}, u32[]{:S(2)}, u32[]{:S(2)}) async-start(f32[16,16,128]{2,1,0:T(8,128)} %shard_map.138), calls=%async_computation.3 | async-start | bytes 262144 | tf_op jit(solution)/shard_map/all_to_all | solution.py:584

commit v6 on v5

--- a/solution.py
+++ b/solution.py
@@ -213,14 +213,14 @@
 
 
 def back_kernel(recv_ref, back_ref):
-    rows, block = back_ref.shape
+    rows, block = back_ref.shape[0] * 4 // 3, back_ref.shape[1] * 3 // 4
     total = recv_ref[0]
     for k in range(1, recv_ref.shape[0]):
         total = total + recv_ref[k]
     rest = total.shape[1] - block
     right = jnp.concatenate([total[rows:, : block - rest], total[rows:, block - rest :]], axis=0)
     total = jnp.concatenate([total[:rows, block:], right], axis=1)
-    back_ref[...] = total
+    back_ref[...] = packed(total)
 
 
 def query_kernel(
@@ -318,10 +318,10 @@
         later.start()
     blocks = [piece.ready() for piece in (own, far_a, far_b, far_c)]
     n_sub = blocks[0].shape[0]
-    rows, block = back_four.dst.shape[1:]
     queries, heads, keys = expo_ref.shape
     width = normed.shape[1]
-    n_col = width // block
+    rows, n_col = queries, pay_ref.shape[0]
+    block = width // n_col
     me = lax.axis_index("row")
     col = lax.axis_index("col")
 
@@ -369,7 +369,8 @@
         part = slice(k * block, (k + 1) * block)
         spot = (col + n_x - k) % n_x
         near = col // n_x == k // n_x
-        dctx[:, part] = jnp.where(near, backs[0][spot], backs[1][spot]) * gate_ref[:, part]
+        one = jnp.where(near, backs[0][spot], backs[1][spot])
+        dctx[:, part] = unpacked(one, rows, block) * gate_ref[:, part]
     for (some, part), probs in zip(halves(heads, width), parts):
         high, low = vh[:, part], vl[:, part]
         eh, el = split(probs)
@@ -640,7 +641,7 @@
         return lax.ppermute(x, "row", [(r, target(r)) for r in range(n_row)])
 
     pair_of = jnp.stack([moved, along(moved, lambda r: r ^ 1)])
-    back_pay = call(back_kernel, sds(queries, block), queries * width, (recv1,), vmem=4 * MIB)
+    back_pay = call(back_kernel, sds(queries * block // LANES, LANES), queries * width, (recv1,), vmem=4 * MIB)
     four = jnp.concatenate([pair_of, along(pair_of, lambda r: r ^ 2)])
     n_x = 4
 

time: 91.1 us -> 91.1 us (level)
  no operation moved by 1% of the time
where the time goes in v6:
time: 91.1 us; the launch traced here: 90.5 us
  starting transfers between devices  41.1 us (45%)
  Pallas kernels  38.5 us (42%)
  waiting for transfers between devices  8.71 us (10%)
  local copies, waits for them, and re-layouts  1.4 us (2%)
    pallas_call x11, Pallas kernels, call(): pl.pallas_call(body, out_shape=out_shape, scratch_shapes=scratch, compile...  38.5 us
    all_to_all x4, starting transfers between devices, swap(): return lax.all_to_all(x, axis, 0, 0, tiled=True)  25.5 us
    ppermute x5, starting transfers between devices, along(): return lax.ppermute(x, 'row', [(r, target(r)) for r in range(n_row)])  7.87 us
    all_to_all x4, waiting for transfers between devices, swap(): return lax.all_to_all(x, axis, 0, 0, tiled=True)  7.24 us
    ppermute x1, starting transfers between devices, local(): moved = lax.ppermute(packed_single, ('row', 'col'), perm)  2.91 us
    ppermute x1, starting transfers between devices, local(): lax.ppermute(back_four, 'col', [(c, (c + n_x) % n_col) for c in range(n_c...  2.46 us
    ppermute x3, starting transfers between devices, around(): lax.ppermute(x, 'col', [(c, c - c % n_x + (c + k) % n_x) for c in range(n...  2.35 us
  transfers between devices with their start and end apart: 14, of which 6 were waited for; matrix products, arithmetic and copies ran while one was open for 0% of the time, Pallas kernels for 27%

profile of v6, /device:TPU:1, one launch (start us, length us, event | category | flops | bytes accessed | tf_op | source)
XLA Modules:
  0.0 90.5 jit_solution(1170618563187404652)
XLA Ops:
  0.6 2.1 %shard_map.130 = (f32[8,96,128]{2,1,0:T(8,128)}, f32[48,128]{1,0:T(8,128)}) custom-call(f32[64,96]{1,0:T(8,128)} %single_ref.1, f32[64,96]{1,0:T(8,128)} %cot_ref.1, f32[96,768]{1,0:T(8,128)} %bitcast.12), custom_call_target="tpu_custom_call" | custom-call | flops 28311552 | bytes 761856 | tf_op jit(solution)/shard_map/pallas_call | solution.py:83
  2.7 8.2 %all-to-all-start = ((f32[8,96,128]{2,1,0:T(8,128)}), f32[8,96,128]{2,1,0:T(8,128)S(1)}, u32[]{:S(2)}, u32[]{:S(2)}) async-start(f32[8,96,128]{2,1,0:T(8,128)} %get-tuple-element.28), calls=%async_computation | async-start | bytes 786432 | tf_op jit(solution)/shard_map/all_to_all | solution.py:585
  10.9 2.9 %collective-permute-start = (f32[48,128]{1,0:T(8,128)}, f32[48,128]{1,0:T(8,128)S(1)}, u32[]{:S(2)}, u32[]{:S(2)}) collective-permute-start(f32[48,128]{1,0:T(8,128)} %get-tuple-element.29), channel_id=1, source_target_pairs={{0,64},{1,32},{2,0},{3,96},{4,80},{5,48},{6,16},{7,112},{8,72},{9,... | collective-permute-start | bytes 73736 | tf_op jit(solution)/shard_map/ppermute | solution.py:618
  13.8 4.3 %shard_map.131 = (f32[48,16,128]{2,1,0:T(8,128)}, f32[48,128]{1,0:T(8,128)}) custom-call(f32[64,128,128]{2,1,0:T(8,128)} %refs_0_.9, f32[16,128]{1,0:T(8,128)} %bitcast.14, f32[1,128]{1,0:T(1,128)} %bitcast.27), custom_call_target="tpu_custom_call" | custom-call | flops 209715200 | bytes 4620800 | tf_op jit(solution)/shard_map/pallas_call | solution.py:83
  18.2 0.2 collective-permute-done
  18.4 2.2 %collective-permute-start.1 = (f32[48,128]{1,0:T(8,128)S(1)}, f32[48,128]{1,0:T(8,128)S(1)}, u32[]{:S(2)}, u32[]{:S(2)}) collective-permute-start(f32[48,128]{1,0:T(8,128)S(1)} %collective-permute-done), channel_id=1, source_target_pairs={{0,8},{8,0},{16,24},{24,16},{32,40},{40,32},{48,56},{56,48},{64,72... | collective-permute-start | bytes 73736 | tf_op jit(solution)/shard_map/ppermute | solution.py:641
  20.6 0.8 collective-permute-done.1
  21.5 2.3 %collective-permute-start.2 = (f32[2,48,128]{2,1,0:T(8,128)S(1)}, f32[2,48,128]{2,1,0:T(8,128)S(1)}, u32[]{:S(2)}, u32[]{:S(2)}) collective-permute-start(f32[2,48,128]{2,1,0:T(8,128)S(1)} %pad_maximum_fusion.2), channel_id=1, source_target_pairs={{0,16},{8,24},{16,0},{24,8},{32,48},{40,56},{48,32},{56,40},{64,80... | collective-permute-start | bytes 147464 | tf_op jit(solution)/shard_map/ppermute | solution.py:641
  23.8 0.0 all-to-all-done.refs_3_.recv_ref
  23.8 0.2 shard_map.133
  24.0 1.5 %collective-permute-start.8 = (f32[48,128]{1,0:T(8,128)S(1)}, f32[48,128]{1,0:T(8,128)S(1)}, u32[]{:S(2)}, u32[]{:S(2)}) collective-permute-start(f32[48,128]{1,0:T(8,128)S(1)} %shard_map.133), channel_id=1, source_target_pairs={{0,3},{1,0},{2,1},{3,2},{4,7},{5,4},{6,5},{7,6},{8,11},{9,8},{10,9... | collective-permute-start | bytes 73736 | tf_op jit(solution)/shard_map/ppermute | solution.py:649
  25.5 0.7 collective-permute-start.7
  26.2 0.1 collective-permute-start.6
  26.3 0.0 collective-permute-done.2
  26.3 0.0 copy-start.3
  26.3 2.7 %collective-permute-start.5 = (f32[4,48,128]{2,1,0:T(8,128)S(1)}, f32[4,48,128]{2,1,0:T(8,128)S(1)}, u32[]{:S(2)}, u32[]{:S(2)}) collective-permute-start(f32[4,48,128]{2,1,0:T(8,128)S(1)} %pad_maximum_fusion.refs_0_), channel_id=1, source_target_pairs={{0,96},{8,104},{16,112},{24,120},{32,0},{40,8},{48,16},{56,24},{64... | collective-permute-start | bytes 294920 | tf_op jit(solution)/shard_map/ppermute | solution.py:641
  29.0 0.3 collective-permute-start.4
  29.3 0.0 collective-permute-done.8
  29.3 0.4 collective-permute-start.3
  29.7 0.0 collective-permute-done.7
  29.7 0.4 collective-permute-done.6
  30.1 2.5 %collective-permute-start.9 = (f32[4,48,128]{2,1,0:T(8,128)S(1)}, f32[4,48,128]{2,1,0:T(8,128)S(1)}, u32[]{:S(2)}, u32[]{:S(2)}) collective-permute-start(f32[4,48,128]{2,1,0:T(8,128)S(1)} %pad_maximum_fusion.1.refs_10_), channel_id=1, source_target_pairs={{0,4},{1,5},{2,6},{3,7},{4,0},{5,1},{6,2},{7,3},{8,12},{9,13},{10,... | collective-permute-start | bytes 294920 | tf_op jit(solution)/shard_map/ppermute | solution.py:652
  32.6 0.0 copy-done
  32.6 5.7 %shard_map.132 = (f32[16,16,128]{2,1,0:T(8,128)}, f32[16,128]{1,0:T(8,128)}, f32[64,768]{1,0:T(8,128)}, f32[64,768]{1,0:T(8,128)}) custom-call(f32[64,128,128]{2,1,0:T(8,128)} %refs_0_.9, f32[16,128]{1,0:T(8,128)} %bitcast.15, f32[1,128]{1,0:T(1,128)} %bitcast.28, f32[8,96,128]{2,1,0:T(8,128)} %copy-done, f32[6,128]{1,0:T(8,128)} %bitcast.25, ...), custom_call_target="tpu_custom_call" | custom-call | flops 662700032 | bytes 9850368 | tf_op jit(solution)/shard_map/pallas_call | solution.py:83
  38.3 0.0 copy-done.3
  38.3 0.0 collective-permute-done.5.refs_3_
  38.4 0.0 collective-permute-done.4.refs_2_
  38.4 0.0 collective-permute-done.3.refs_1_
  38.4 0.0 copy-start.7
  38.4 0.0 collective-permute-done.9.refs_11_
  38.4 0.6 copy-done.5
  39.0 0.0 copy-done.6
  39.0 0.0 copy-done.7
  39.0 0.0 copy-done.8
  39.1 7.8 %shard_map.134 = (f32[8,64,128]{2,1,0:T(8,128)}, f32[64,16,128]{2,1,0:T(8,128)}, f32[64,16,128]{2,1,0:T(8,128)}, f32[64,128]{1,0:T(8,128)}) custom-call(f32[4,48,128]{2,1,0:T(8,128)} %copy-done.3, f32[4,48,128]{2,1,0:T(8,128)} %copy-done.7, f32[4,48,128]{2,1,0:T(8,128)} %copy-done.6, f32[4,48,128]{2,1,0:T(8,128)} %copy-done.5, f32[6,128]{1,0:T(8,128)} %bitcast.26, ...), custom_call_target="tpu_custom_call" | custom-call | flops 905969664 | bytes 7572480 | tf_op jit(solution)/shard_map/pallas_call | solution.py:83
  46.8 3.9 %all-to-all-start.1 = ((f32[8,64,128]{2,1,0:T(8,128)}), f32[8,64,128]{2,1,0:T(8,128)S(1)}, u32[]{:S(2)}, u32[]{:S(2)}) async-start(f32[8,64,128]{2,1,0:T(8,128)} %get-tuple-element.38), calls=%async_computation.1 | async-start | bytes 524288 | tf_op jit(solution)/shard_map/all_to_all | solution.py:585
  50.7 4.8 %shard_map.135.moment_ref = f32[64,32,128]{2,1,0:T(8,128)} custom-call(f32[64,128,128]{2,1,0:T(8,128)} %refs_0_.9, f32[64,16,128]{2,1,0:T(8,128)} %get-tuple-element.40.refs_1_, f32[64,16,128]{2,1,0:T(8,128)} %get-tuple-element.41.refs_2_, f32[48,128]{1,0:T(8,128)} %get-tuple-element.42.refs_3_.refs_4_, f32[16,128]{1,0:T(8,128)} %get-tuple-element.43.refs_4_), custom_call_target="tpu_custom_call" | custom-call | flops 201326592 | bytes 6324224 | tf_op jit(solution)/shard_map/pallas_call | solution.py:83
  55.5 2.9 %all-to-all-done.1.recv_ref = f32[8,64,128]{2,1,0:T(8,128)S(1)} async-done(((f32[8,64,128]{2,1,0:T(8,128)}), f32[8,64,128]{2,1,0:T(8,128)S(1)}, u32[]{:S(2)}, u32[]{:S(2)}) %all-to-all-start.1) | async-done | bytes 262176 | tf_op jit(solution)/shard_map/all_to_all | solution.py:585
  58.4 0.7 copy-done.2
  59.1 2.7 %shard_map.136 = (f32[8,64,128]{2,1,0:T(8,128)}, f32[64,128]{1,0:T(8,128)}) custom-call(f32[8,64,128]{2,1,0:T(8,128)} %copy-done.2, f32[64,128]{1,0:T(8,128)} %get-tuple-element.39.stat_ref, f32[64,32,128]{2,1,0:T(8,128)} %shard_map.135.moment_ref, f32[1,128]{1,0:T(1,128)} %bitcast.29), custom_call_target="tpu_custom_call" | custom-call | flops 1048576 | bytes 1638912 | tf_op jit(solution)/shard_map/pallas_call | solution.py:83
  61.9 3.8 %all-to-all-start.2 = ((f32[8,64,128]{2,1,0:T(8,128)}), f32[8,64,128]{2,1,0:T(8,128)S(1)}, u32[]{:S(2)}, u32[]{:S(2)}) async-start(f32[8,64,128]{2,1,0:T(8,128)} %get-tuple-element.44), calls=%async_computation.2 | async-start | bytes 524288 | tf_op jit(solution)/shard_map/all_to_all | solution.py:585
  65.6 5.5 %shard_map.137.refs_8_ = f32[64,128,128]{2,1,0:T(8,128)} custom-call(f32[64,128,128]{2,1,0:T(8,128)} %refs_0_.9, f32[64,16,128]{2,1,0:T(8,128)} %get-tuple-element.40.refs_1_, f32[64,16,128]{2,1,0:T(8,128)} %get-tuple-element.41.refs_2_, f32[48,16,128]{2,1,0:T(8,128)} %get-tuple-element.35.refs_8_.refs_3_, f32[48,128]{1,0:T(8,128)} %get-tuple-element.42.refs_3_.refs_4_, ...), custom_call_target="tpu_custom_call" | custom-call | flops 209715200 | bytes 9896448 | tf_op jit(solution)/shard_map/pallas_call | solution.py:83
  71.1 2.2 %all-to-all-done.2.recv_ref.refs_9_ = f32[8,64,128]{2,1,0:T(8,128)S(1)} async-done(((f32[8,64,128]{2,1,0:T(8,128)}), f32[8,64,128]{2,1,0:T(8,128)S(1)}, u32[]{:S(2)}, u32[]{:S(2)}) %all-to-all-start.2) | async-done | bytes 262176 | tf_op jit(solution)/shard_map/all_to_all | solution.py:585
  73.3 0.7 shard_map.138
  74.0 9.7 %all-to-all-start.3 = ((f32[16,16,128]{2,1,0:T(8,128)}), f32[16,16,128]{2,1,0:T(8,128)S(1)}, u32[]{:S(2)}, u32[]{:S(2)}) async-start(f32[16,16,128]{2,1,0:T(8,128)} %shard_map.138), calls=%async_computation.3 | async-start | bytes 262144 | tf_op jit(solution)/shard_map/all_to_all | solution.py:585
  83.7 4.0 %shard_map.139 = (f32[64,128,128]{2,1,0:T(8,128)}, f32[64,96]{1,0:T(8,128)}) custom-call(f32[64,128,128]{2,1,0:T(8,128)} %refs_0_.9, f32[64,16,128]{2,1,0:T(8,128)} %get-tuple-element.40.refs_1_, f32[64,16,128]{2,1,0:T(8,128)} %get-tuple-element.41.refs_2_, f32[16,16,128]{2,1,0:T(8,128)} %get-tuple-element.36.refs_9_.refs_3_, ...), custom_call_target="tpu_custom_call", output_to_operand_aliasing={{0}: (8, {})} | custom-call | flops 209715200 | bytes 14590464 | tf_op jit(solution)/shard_map/pallas_call | solution.py:83
  87.7 2.2 %all-to-all-done.3.recv_ref = f32[16,16,128]{2,1,0:T(8,128)S(1)} async-done(((f32[16,16,128]{2,1,0:T(8,128)}), f32[16,16,128]{2,1,0:T(8,128)S(1)}, u32[]{:S(2)}, u32[]{:S(2)}) %all-to-all-start.3) | async-done | bytes 131104 | tf_op jit(solution)/shard_map/all_to_all | solution.py:585
  89.9 0.6 shard_map.140
  (12 shorter events, 0.0 us)
Async XLA Ops:
  2.7 21.0 %all-to-all-start = ((f32[8,96,128]{2,1,0:T(8,128)}), f32[8,96,128]{2,1,0:T(8,128)S(1)}, u32[]{:S(2)}, u32[]{:S(2)}) async-start(f32[8,96,128]{2,1,0:T(8,128)} %get-tuple-element.28), calls=%async_computation | async-start | bytes 786432 | tf_op jit(solution)/shard_map/all_to_all | solution.py:585
  10.9 7.5 %collective-permute-start = (f32[48,128]{1,0:T(8,128)}, f32[48,128]{1,0:T(8,128)S(1)}, u32[]{:S(2)}, u32[]{:S(2)}) collective-permute-start(f32[48,128]{1,0:T(8,128)} %get-tuple-element.29), channel_id=1, source_target_pairs={{0,64},{1,32},{2,0},{3,96},{4,80},{5,48},{6,16},{7,112},{8,72},{9,... | collective-permute-start | bytes 73736 | tf_op jit(solution)/shard_map/ppermute | solution.py:618
  18.4 3.1 %collective-permute-start.1 = (f32[48,128]{1,0:T(8,128)S(1)}, f32[48,128]{1,0:T(8,128)S(1)}, u32[]{:S(2)}, u32[]{:S(2)}) collective-permute-start(f32[48,128]{1,0:T(8,128)S(1)} %collective-permute-done), channel_id=1, source_target_pairs={{0,8},{8,0},{16,24},{24,16},{32,40},{40,32},{48,56},{56,48},{64,72... | collective-permute-start | bytes 73736 | tf_op jit(solution)/shard_map/ppermute | solution.py:641
  21.5 4.9 %collective-permute-start.2 = (f32[2,48,128]{2,1,0:T(8,128)S(1)}, f32[2,48,128]{2,1,0:T(8,128)S(1)}, u32[]{:S(2)}, u32[]{:S(2)}) collective-permute-start(f32[2,48,128]{2,1,0:T(8,128)S(1)} %pad_maximum_fusion.2), channel_id=1, source_target_pairs={{0,16},{8,24},{16,0},{24,8},{32,48},{40,56},{48,32},{56,40},{64,80... | collective-permute-start | bytes 147464 | tf_op jit(solution)/shard_map/ppermute | solution.py:641
  23.8 8.8 %copy-start = (f32[8,96,128]{2,1,0:T(8,128)}, f32[8,96,128]{2,1,0:T(8,128)S(1)}, u32[]{:S(2)}) copy-start(f32[8,96,128]{2,1,0:T(8,128)S(1)} %all-to-all-done.refs_3_.recv_ref) | copy-start | bytes 1179652
  24.0 5.3 %collective-permute-start.8 = (f32[48,128]{1,0:T(8,128)S(1)}, f32[48,128]{1,0:T(8,128)S(1)}, u32[]{:S(2)}, u32[]{:S(2)}) collective-permute-start(f32[48,128]{1,0:T(8,128)S(1)} %shard_map.133), channel_id=1, source_target_pairs={{0,3},{1,0},{2,1},{3,2},{4,7},{5,4},{6,5},{7,6},{8,11},{9,8},{10,9... | collective-permute-start | bytes 73736 | tf_op jit(solution)/shard_map/ppermute | solution.py:649
  25.5 4.2 %collective-permute-start.7 = (f32[48,128]{1,0:T(8,128)S(1)}, f32[48,128]{1,0:T(8,128)S(1)}, u32[]{:S(2)}, u32[]{:S(2)}) collective-permute-start(f32[48,128]{1,0:T(8,128)S(1)} %shard_map.133), channel_id=1, source_target_pairs={{0,2},{1,3},{2,0},{3,1},{4,6},{5,7},{6,4},{7,5},{8,10},{9,11},{10,... | collective-permute-start | bytes 73736 | tf_op jit(solution)/shard_map/ppermute | solution.py:649
  26.2 3.9 %collective-permute-start.6 = (f32[48,128]{1,0:T(8,128)S(1)}, f32[48,128]{1,0:T(8,128)S(1)}, u32[]{:S(2)}, u32[]{:S(2)}) collective-permute-start(f32[48,128]{1,0:T(8,128)S(1)} %shard_map.133), channel_id=1, source_target_pairs={{0,1},{1,2},{2,3},{3,0},{4,5},{5,6},{6,7},{7,4},{8,9},{9,10},{10,1... | collective-permute-start | bytes 73736 | tf_op jit(solution)/shard_map/ppermute | solution.py:649
  26.3 12.0 %copy-start.3 = (f32[4,48,128]{2,1,0:T(8,128)}, f32[4,48,128]{2,1,0:T(8,128)S(1)}, u32[]{:S(2)}) copy-start(f32[4,48,128]{2,1,0:T(8,128)S(1)} %pad_maximum_fusion.refs_0_) | copy-start | bytes 294916
  26.3 12.0 %collective-permute-start.5 = (f32[4,48,128]{2,1,0:T(8,128)S(1)}, f32[4,48,128]{2,1,0:T(8,128)S(1)}, u32[]{:S(2)}, u32[]{:S(2)}) collective-permute-start(f32[4,48,128]{2,1,0:T(8,128)S(1)} %pad_maximum_fusion.refs_0_), channel_id=1, source_target_pairs={{0,96},{8,104},{16,112},{24,120},{32,0},{40,8},{48,16},{56,24},{64... | collective-permute-start | bytes 294920 | tf_op jit(solution)/shard_map/ppermute | solution.py:641
  29.0 9.3 %collective-permute-start.4 = (f32[4,48,128]{2,1,0:T(8,128)S(1)}, f32[4,48,128]{2,1,0:T(8,128)S(1)}, u32[]{:S(2)}, u32[]{:S(2)}) collective-permute-start(f32[4,48,128]{2,1,0:T(8,128)S(1)} %pad_maximum_fusion.refs_0_), channel_id=1, source_target_pairs={{0,64},{8,72},{16,80},{24,88},{32,96},{40,104},{48,112},{56,120},{... | collective-permute-start | bytes 294920 | tf_op jit(solution)/shard_map/ppermute | solution.py:641
  29.3 9.1 %collective-permute-start.3 = (f32[4,48,128]{2,1,0:T(8,128)S(1)}, f32[4,48,128]{2,1,0:T(8,128)S(1)}, u32[]{:S(2)}, u32[]{:S(2)}) collective-permute-start(f32[4,48,128]{2,1,0:T(8,128)S(1)} %pad_maximum_fusion.refs_0_), channel_id=1, source_target_pairs={{0,32},{8,40},{16,48},{24,56},{32,64},{40,72},{48,80},{56,88},{64,... | collective-permute-start | bytes 294920 | tf_op jit(solution)/shard_map/ppermute | solution.py:641
  30.1 8.2 %copy-start.4 = (f32[4,48,128]{2,1,0:T(8,128)}, f32[4,48,128]{2,1,0:T(8,128)S(1)}, u32[]{:S(2)}) copy-start(f32[4,48,128]{2,1,0:T(8,128)S(1)} %pad_maximum_fusion.1.refs_10_) | copy-start | bytes 294916
  30.1 8.3 %collective-permute-start.9 = (f32[4,48,128]{2,1,0:T(8,128)S(1)}, f32[4,48,128]{2,1,0:T(8,128)S(1)}, u32[]{:S(2)}, u32[]{:S(2)}) collective-permute-start(f32[4,48,128]{2,1,0:T(8,128)S(1)} %pad_maximum_fusion.1.refs_10_), channel_id=1, source_target_pairs={{0,4},{1,5},{2,6},{3,7},{4,0},{5,1},{6,2},{7,3},{8,12},{9,13},{10,... | collective-permute-start | bytes 294920 | tf_op jit(solution)/shard_map/ppermute | solution.py:652
  38.3 0.6 copy-start.5
  38.4 0.7 copy-start.6
  38.4 0.7 copy-start.7
  38.4 0.7 copy-start.8
  46.8 11.6 %all-to-all-start.1 = ((f32[8,64,128]{2,1,0:T(8,128)}), f32[8,64,128]{2,1,0:T(8,128)S(1)}, u32[]{:S(2)}, u32[]{:S(2)}) async-start(f32[8,64,128]{2,1,0:T(8,128)} %get-tuple-element.38), calls=%async_computation.1 | async-start | bytes 524288 | tf_op jit(solution)/shard_map/all_to_all | solution.py:585
  58.4 0.7 copy-start.2
  61.9 11.4 %all-to-all-start.2 = ((f32[8,64,128]{2,1,0:T(8,128)}), f32[8,64,128]{2,1,0:T(8,128)S(1)}, u32[]{:S(2)}, u32[]{:S(2)}) async-start(f32[8,64,128]{2,1,0:T(8,128)} %get-tuple-element.44), calls=%async_computation.2 | async-start | bytes 524288 | tf_op jit(solution)/shard_map/all_to_all | solution.py:585
  73.3 10.4 %copy-start.1 = (f32[8,64,128]{2,1,0:T(8,128)}, f32[8,64,128]{2,1,0:T(8,128)S(1)}, u32[]{:S(2)}) copy-start(f32[8,64,128]{2,1,0:T(8,128)S(1)} %all-to-all-done.2.recv_ref.refs_9_) | copy-start | bytes 786436
  74.0 15.9 %all-to-all-start.3 = ((f32[16,16,128]{2,1,0:T(8,128)}), f32[16,16,128]{2,1,0:T(8,128)S(1)}, u32[]{:S(2)}, u32[]{:S(2)}) async-start(f32[16,16,128]{2,1,0:T(8,128)} %shard_map.138), calls=%async_computation.3 | async-start | bytes 262144 | tf_op jit(solution)/shard_map/all_to_all | solution.py:585
